TPU v7x, 32 devices: a whole 2x2x4 slice. The times are simulated.
32 devices in a mesh: dp: 2 (over core), fsdp: 16 (over z, y, x).
Axes of the slice: x: 2, y: 2, z: 4, core: 2. Of those that a mesh axis runs over, the one named last changes fastest.
Arguments:
- tokens: bfloat16 [2, 8192, 768], P(None, ('dp', 'fsdp')), may hold values from -6 to 6
- cotangent: bfloat16 [2, 8192, 768], P(None, ('dp', 'fsdp')), may hold values from -6 to 6
- routes: int32 [2, 8192, 1], P(None, ('dp', 'fsdp')), may hold values from 0 to 15
- lengths: int32 [2, 32, 2], P(None, ('dp', 'fsdp')), may hold values from 32 to 224, as said below
- norm1_gain: bfloat16 [768], P(('dp', 'fsdp')), may hold values from 0.5 to 1.5
- input_weight: bfloat16 [768, 3072], P(('dp', 'fsdp')), may hold values from -0.21875 to 0.21875
- conv_weight: bfloat16 [1536, 4], P(('dp', 'fsdp')), may hold values from -3 to 3
- conv_bias: bfloat16 [1536], P(('dp', 'fsdp')), may hold values from -1.5 to 1.5
- scan_weight: bfloat16 [1536, 80], P(('dp', 'fsdp')), may hold values from -0.15625 to 0.15625
- step_weight: bfloat16 [1536, 48], P(('dp', 'fsdp')), may hold values from -0.875 to 0.875
- step_bias: bfloat16 [1536], P(('dp', 'fsdp')), may hold values from -4.59375 to -2.296875
- decay_log: bfloat16 [1536, 16], P(('dp', 'fsdp')), may hold values from 0 to 2.765625
- skip_gain: bfloat16 [1536], P(('dp', 'fsdp')), may hold values from 0.5 to 1.5
- out_weight: bfloat16 [1536, 768], P(('dp', 'fsdp')), may hold values from -0.15625 to 0.15625
- norm2_gain: bfloat16 [768], P(('dp', 'fsdp')), may hold values from 0.5 to 1.5
- router_weight: bfloat16 [768, 16], P(('dp', 'fsdp')), may hold values from -0.15625 to 0.15625
- expert_up: bfloat16 [16, 768, 3072], P('fsdp', None, 'dp'), may hold values from -0.21875 to 0.21875
- expert_down: bfloat16 [16, 3072, 768], P('fsdp', 'dp'), may hold values from -1.75 to 1.75
Outputs:
- block_output: bfloat16 [2, 8192, 768], P(None, ('dp', 'fsdp'))
- tokens_grad: float32 [2, 8192, 768], P(None, ('dp', 'fsdp'))
- norm1_gain_grad: float32 [768], P(('dp', 'fsdp'))
- input_weight_grad: float32 [768, 3072], P(('dp', 'fsdp'))
- conv_weight_grad: float32 [1536, 4], P(('dp', 'fsdp'))
- conv_bias_grad: float32 [1536], P(('dp', 'fsdp'))
- scan_weight_grad: float32 [1536, 80], P(('dp', 'fsdp'))
- step_weight_grad: float32 [1536, 48], P(('dp', 'fsdp'))
- step_bias_grad: float32 [1536], P(('dp', 'fsdp'))
- decay_log_grad: float32 [1536, 16], P(('dp', 'fsdp'))
- skip_gain_grad: float32 [1536], P(('dp', 'fsdp'))
- out_weight_grad: float32 [1536, 768], P(('dp', 'fsdp'))
- norm2_gain_grad: float32 [768], P(('dp', 'fsdp'))
- router_weight_grad: float32 [768, 16], P(('dp', 'fsdp'))
- expert_up_grad: float32 [16, 768, 3072], P('fsdp', None, 'dp')
- expert_down_grad: float32 [16, 3072, 768], P('fsdp', 'dp')
Inputs may be any that keep to these rules, and one draw needn't show every extreme that they name: `routes`: routes of padding rows are ignored. `lengths`: A pack's two entries sum to 256: first its sample's length, from 128 to 224, then its padding. In every micro-batch some pack has the longest sample and another the shortest.
All inputs are finite; a program needn't handle non-finite values.
Results may differ from a plain program's by a relative error of at most 0.013.
Values may be sent and summed in bfloat16 or wider, within the bound.
No kernel may reach another device: no remote copies, remote signals or barrier semaphores. Data moves between devices by JAX's collectives and lax.ppermute only.
A program may use at most 256 MiB of HBM per device.

v0:
```python
import functools

import jax
import jax.numpy as jnp
from jax import lax
from jax.experimental import pallas as pl
from jax.experimental.pallas import tpu as pltpu
from jax.sharding import PartitionSpec as P

EPSILON = 1e-05
LOG2E = 1.4426950408889634
LN2 = 0.6931471805599453
LANES = 128
ROWS = 8
F32 = jnp.float32
BF16 = jnp.bfloat16


def dot(left, right, dims=((1,), (0,))):
    return lax.dot_general(left, right, (dims, ((), ())), preferred_element_type=F32)


def fold_rows(parts):
    place = lax.broadcasted_iota(jnp.int32, parts[0].shape, 0)
    half = 1
    while half < ROWS:
        lower = (place & half) == 0
        merged = []
        for i in range(0, len(parts), 2):
            a, b = parts[i], parts[i + 1]
            merged.append(jnp.where(lower, a, b) + pltpu.roll(jnp.where(lower, b, a), half, 0))
        parts = merged
        half *= 2
    return parts[0]


def sum_states(parts):
    halves = []
    for p in parts:
        total = p[:ROWS]
        for i in range(1, p.shape[0] // ROWS):
            total = total + p[i * ROWS : (i + 1) * ROWS]
        halves.append(total)
    return fold_rows(halves)


def lane_chunk(k, count=1):
    return pl.ds(pl.multiple_of(k * LANES * count, LANES), LANES * count)


def split_low(values):
    high = values.astype(BF16)
    return high, (values - high.astype(F32)).astype(BF16)


def own_lanes(first, states, size):
    lane = lax.broadcasted_iota(jnp.int32, (size, states, LANES), 2)
    row = lax.broadcasted_iota(jnp.int32, (size, states, LANES), 1)
    return (lane == row + first) | (lane == row + first + states)


def widen(selected, first, states, bw, cw):
    steps = selected.shape[0]
    lane = lax.broadcasted_iota(jnp.int32, (2 * LANES, 2 * LANES), 0) % LANES
    to_c = lax.broadcasted_iota(jnp.int32, (2 * LANES, 2 * LANES), 1) >= LANES
    spread = (to_c == (lane >= first + states)).astype(BF16)
    size = 64
    own = own_lanes(first, states, size)
    for at in range(0, steps, size):
        rows = jnp.where(own, selected[at : at + size][:, None, :], 0.0).reshape(size * states, LANES)
        wide = dot(jnp.concatenate(split_low(rows), axis=1), spread)
        bw[at * states : (at + size) * states, :] = wide[:, :LANES]
        cw[at * states : (at + size) * states, :] = wide[:, LANES:]


def narrow(gb, gc, first, states, steps):
    lane = lax.broadcasted_iota(jnp.int32, (2 * LANES, LANES), 1)
    from_c = lax.broadcasted_iota(jnp.int32, (2 * LANES, LANES), 0) >= LANES
    gather = (from_c == (lane >= first + states)).astype(BF16)
    size = 64
    own = own_lanes(first, states, size)
    out = []
    for at in range(0, steps, size):
        here = slice(at * states, (at + size) * states)
        rows = jnp.concatenate([gb[here, :].astype(BF16), gc[here, :].astype(BF16)], axis=1)
        sums = dot(rows, gather).reshape(size, states, LANES)
        out.append(jnp.sum(jnp.where(own, sums, 0.0), axis=1))
    return jnp.concatenate(out, axis=0)


def conv_of(x_ref, vec_ref, lanes, taps, steps):
    total = vec_ref[taps : taps + 1, lanes]
    for shift in range(taps):
        total = total + vec_ref[taps - 1 - shift : taps - shift, lanes] * x_ref[ROWS - shift : ROWS - shift + steps, lanes]
    return total


def forward_kernel(len_ref, u_ref, wx_ref, sela_ref, stepb_ref, vec_ref, a_ref,
                   bx_ref, xs_ref, delta_ref, sel_ref, mix_ref, h_ref,
                   state, bw, cw, low, *, group, rank, taps):
    states, width = a_ref.shape
    steps = u_ref.shape[0]
    chunks = width // LANES
    bias_step, skip = taps + 1, taps + 2
    state[...] = jnp.zeros_like(state)
    bx_ref[:ROWS, :] = jnp.zeros((ROWS, width), F32)

    def project(k, _):
        lanes = lane_chunk(k, 2)
        bx_ref[ROWS:, lanes] = dot(u_ref[...], wx_ref[:, lanes])
        return 0

    lax.fori_loop(0, chunks // 2, project, 0, unroll=True)

    def convolve(k, _):
        lanes = lane_chunk(k)
        conv = conv_of(bx_ref, vec_ref, lanes, taps, steps)
        xs = conv * jax.nn.sigmoid(conv)
        xs_ref[:, lanes] = xs
        low[:, lanes] = xs.astype(BF16)
        return 0

    lax.fori_loop(0, chunks, convolve, 0, unroll=2)
    selected = dot(low[...], sela_ref[...])
    sel_ref[...] = selected
    lane = lax.broadcasted_iota(jnp.int32, selected.shape, 1)
    rank_low = jnp.where(lane < rank, selected, 0.0).astype(BF16)
    widen(selected, rank, states, bw, cw)

    def sizes(k, _):
        lanes = lane_chunk(k, 2)
        pre = dot(rank_low, stepb_ref[lanes, :], ((1,), (1,))) + vec_ref[bias_step : bias_step + 1, lanes]
        delta_ref[:, lanes] = jnp.maximum(pre, 0.0) + jnp.log1p(jnp.exp(-jnp.abs(pre)))
        return 0

    lax.fori_loop(0, chunks // 2, sizes, 0, unroll=2)

    def rows(s, _):
        at = pl.multiple_of(s * ROWS, ROWS)

        def chunk(g, _):
            for u in range(group):
                lanes = lane_chunk(g * group + u)
                d = delta_ref[pl.ds(at, ROWS), lanes]
                x = xs_ref[pl.ds(at, ROWS), lanes]
                dx = d * x
                a = a_ref[:, lanes]
                h = state[:, lanes]
                h_ref[s, :, lanes] = h
                parts = []
                for t in range(ROWS):
                    here = pl.ds(pl.multiple_of((at + t) * states, states), states)
                    h = jnp.exp2(d[t : t + 1] * a) * h + bw[here, :] * dx[t : t + 1]
                    parts.append(cw[here, :] * h)
                state[:, lanes] = h
                mix_ref[pl.ds(at, ROWS), lanes] = sum_states(parts) + vec_ref[skip : skip + 1, lanes] * x
            return 0

        lax.fori_loop(0, chunks // group, chunk, 0)
        return 0

    used = (len_ref[pl.program_id(0)] + ROWS - 1) // ROWS
    lax.fori_loop(0, used, rows, 0)

    def clear(s, _):
        mix_ref[pl.ds(pl.multiple_of(s * ROWS, ROWS), ROWS), :] = jnp.zeros((ROWS, width), F32)
        return 0

    lax.fori_loop(used, steps // ROWS, clear, 0)


def mixer_forward(sample, u, wx, sela, stepb, vec, a2, packs, rank, taps, group=12):
    rows, model = u.shape
    steps = rows // packs
    states, width = a2.shape
    per_pack = lambda p, lens: (p, 0)
    whole = lambda v: pl.BlockSpec(v.shape, lambda p, lens: (0, 0))
    mats = pl.BlockSpec((steps, width), per_pack)
    return pl.pallas_call(
        functools.partial(forward_kernel, group=group, rank=rank, taps=taps),
        grid_spec=pltpu.PrefetchScalarGridSpec(
            num_scalar_prefetch=1,
            grid=(packs,),
            in_specs=[pl.BlockSpec((steps, model), per_pack), whole(wx), whole(sela), whole(stepb), whole(vec), whole(a2)],
            out_specs=[
                pl.BlockSpec((steps + ROWS, width), per_pack),
                mats,
                mats,
                pl.BlockSpec((steps, LANES), per_pack),
                mats,
                pl.BlockSpec((steps // ROWS, states, width), lambda p, lens: (p, 0, 0)),
            ],
            scratch_shapes=[
                pltpu.VMEM((states, width), F32),
                pltpu.VMEM((steps * states, LANES), F32),
                pltpu.VMEM((steps * states, LANES), F32),
                pltpu.VMEM((steps, width), BF16),
            ],
        ),
        out_shape=[
            jax.ShapeDtypeStruct((rows + packs * ROWS, width), F32),
            jax.ShapeDtypeStruct((rows, width), F32),
            jax.ShapeDtypeStruct((rows, width), F32),
            jax.ShapeDtypeStruct((rows, LANES), F32),
            jax.ShapeDtypeStruct((rows, width), F32),
            jax.ShapeDtypeStruct((rows // ROWS, states, width), F32),
        ],
        compiler_params=pltpu.CompilerParams(vmem_limit_bytes=56 << 20),
        cost_estimate=pl.CostEstimate(flops=0, bytes_accessed=120_000_000, transcendentals=0),
        name="mixer_forward",
    )(sample, u, wx, sela, stepb, vec, a2)


def backward_kernel(len_ref, delta_ref, xs_ref, bx_ref, gm_ref, sel_ref, sela_ref, stepb_ref, vec_ref, a_ref, h_ref,
                    wx_ref, x_ref, gain_ref, gu_ref, gh_ref,
                    gx_ref, gsel_ref, gstep_ref, ggain_ref, gtok_ref,
                    mu_s, bw, cw, gb, gc, gd, gxs, low, gvec_ref, ga_ref, *, group, rank, taps):
    pack = pl.program_id(0)
    states, width = a_ref.shape
    steps = sel_ref.shape[0]
    chunks = width // LANES
    bias_conv, bias_step, skip = taps, taps + 1, taps + 2

    @pl.when(pack == 0)
    def _():
        ga_ref[...] = jnp.zeros_like(ga_ref)
        gsel_ref[...] = jnp.zeros_like(gsel_ref)
        gstep_ref[...] = jnp.zeros_like(gstep_ref)
        gvec_ref[...] = jnp.zeros_like(gvec_ref)
        ggain_ref[...] = jnp.zeros_like(ggain_ref)

    mu_s[...] = jnp.zeros_like(mu_s)
    gb[...] = jnp.zeros_like(gb)
    gc[...] = jnp.zeros_like(gc)
    selected = sel_ref[...]
    widen(selected, rank, states, bw, cw)
    used = (len_ref[pack] + ROWS - 1) // ROWS

    def clear(s, _):
        here = pl.ds(pl.multiple_of(s * ROWS, ROWS), ROWS)
        gd[here, :] = jnp.zeros((ROWS, width), F32)
        gxs[here, :] = jnp.zeros((ROWS, width), F32)
        return 0

    lax.fori_loop(used, steps // ROWS, clear, 0)

    def rows(back, _):
        s = used - 1 - back
        at = pl.multiple_of(s * ROWS, ROWS)
        place = [pl.ds(pl.multiple_of((at + t) * states, states), states) for t in range(ROWS)]

        def chunk(g, _):
            each = []
            for u in range(group):
                lanes = lane_chunk(g * group + u)
                d = delta_ref[pl.ds(at, ROWS), lanes]
                x = xs_ref[pl.ds(at, ROWS), lanes]
                a = a_ref[:, lanes]
                dx = d * x
                h, decay = [h_ref[s, :, lanes]], []
                for t in range(ROWS):
                    decay.append(jnp.exp2(d[t : t + 1] * a))
                    h.append(decay[t] * h[t] + bw[place[t], :] * dx[t : t + 1])
                each.append(dict(lanes=lanes, d=d, x=x, gy=gm_ref[pl.ds(at, ROWS), lanes], dx=dx, a=a, mu=mu_s[:, lanes],
                                 h=h, decay=decay, ga=ga_ref[:, lanes], sp=[None] * ROWS, gp=[None] * ROWS))
            for t in range(ROWS - 1, -1, -1):
                b, c = bw[place[t], :], cw[place[t], :]
                one_b = one_c = None
                for v in each:
                    gyt = v["gy"][t : t + 1]
                    lam = c * gyt + v["mu"]
                    v["sp"][t] = b * lam
                    to_b = lam * v["dx"][t : t + 1]
                    to_c = v["h"][t + 1] * gyt
                    one_b = to_b if one_b is None else one_b + to_b
                    one_c = to_c if one_c is None else one_c + to_c
                    v["mu"] = v["decay"][t] * lam
                    q = v["mu"] * v["h"][t]
                    v["gp"][t] = q * v["a"]
                    v["ga"] = v["ga"] + q * v["d"][t : t + 1]
                gb[place[t], :] += one_b
                gc[place[t], :] += one_c
            for v in each:
                lanes = v["lanes"]
                mu_s[:, lanes], ga_ref[:, lanes] = v["mu"], v["ga"]
                total = sum_states(v["sp"])
                gd[pl.ds(at, ROWS), lanes] = sum_states(v["gp"]) * LN2 + v["x"] * total
                gxs[pl.ds(at, ROWS), lanes] = v["d"] * total
            return 0

        lax.fori_loop(0, chunks // group, chunk, 0)
        return 0

    lax.fori_loop(0, used, rows, 0)

    def add_row(row, lanes, values):
        gvec_ref[row : row + 1, lanes] += jnp.sum(values, axis=0, keepdims=True)

    def sizes(k, _):
        lanes = lane_chunk(k)
        d = delta_ref[:, lanes]
        rise = jnp.where(d < 0.01, d * (1.0 - d * (0.5 - d * (1.0 / 6.0))), 1.0 - jnp.exp(-d))
        grad = gd[:steps, lanes] * rise
        add_row(bias_step, lanes, grad)
        low[:, lanes] = grad.astype(BF16)
        add_row(skip, lanes, gm_ref[:, lanes] * xs_ref[:, lanes])
        return 0

    lax.fori_loop(0, chunks, sizes, 0, unroll=2)
    gd[steps:, :] = jnp.zeros((ROWS, width), F32)
    lane = lax.broadcasted_iota(jnp.int32, selected.shape, 1)
    rank_low = jnp.where(lane < rank, selected, 0.0).astype(BF16)
    grad_rank = dot(low[...], stepb_ref[...])
    gstep_ref[...] += dot(low[...], rank_low, ((0,), (0,)))
    grad_sel = jnp.where(lane < rank, grad_rank, narrow(gb, gc, rank, states, steps)).astype(BF16)

    def values(k, _):
        lanes = lane_chunk(k)
        conv = conv_of(bx_ref, vec_ref, lanes, taps, steps)
        sig = jax.nn.sigmoid(conv)
        low[:, lanes] = (conv * sig).astype(BF16)
        grad = dot(grad_sel, sela_ref[lanes, :], ((1,), (1,)))
        grad = grad + gxs[:, lanes] + gm_ref[:, lanes] * vec_ref[skip : skip + 1, lanes]
        grad = grad * (sig * (1.0 + conv * (1.0 - sig)))
        gd[:steps, lanes] = grad
        add_row(bias_conv, lanes, grad)
        back_x = None
        for j in range(taps):
            shift = taps - 1 - j
            add_row(j, lanes, grad * bx_ref[ROWS - shift : ROWS - shift + steps, lanes])
            term = vec_ref[j : j + 1, lanes] * gd[shift : shift + steps, lanes]
            back_x = term if back_x is None else back_x + term
        gx_ref[:, lanes] = back_x.astype(BF16)
        return 0

    lax.fori_loop(0, chunks, values, 0, unroll=2)
    gsel_ref[...] += dot(low[...], grad_sel, ((0,), (0,)))

    hidden = x_ref[...].astype(F32)
    inv = lax.rsqrt(jnp.mean(hidden * hidden, axis=1, keepdims=True) + EPSILON)
    normed = hidden * inv
    grad_u = dot(gx_ref[...], wx_ref[...], ((1,), (1,))) + gu_ref[...]
    scaled = grad_u * gain_ref[...]
    ggain_ref[...] += jnp.sum(grad_u * normed, axis=0, keepdims=True)
    gtok_ref[...] = gh_ref[...] + inv * (scaled - normed * jnp.mean(scaled * normed, axis=1, keepdims=True))

    @pl.when(pack == pl.num_programs(0) - 1)
    def _():
        rows_of_vectors = jnp.concatenate([gvec_ref[...], ga_ref[...] * a_ref[...] * LN2], axis=0)
        before = jnp.zeros((rank, width), F32)
        after = jnp.zeros((LANES - rank - rows_of_vectors.shape[0], width), F32)
        gstep_ref[...] += jnp.concatenate([before, rows_of_vectors, after], axis=0).T


def mixer_backward(sample, delta, xs, bx, gm, sel, sela, stepb, vec, a2, hall, wx, tokens, gain, grad_u, grad_h,
                   packs, rank, taps, group=2):
    rows, width = delta.shape
    steps = rows // packs
    states, model = a2.shape[0], tokens.shape[1]
    per_pack = lambda p, lens: (p, 0)
    fixed = lambda p, lens: (0, 0)
    whole = lambda v: pl.BlockSpec(v.shape, fixed)
    mats = pl.BlockSpec((steps, width), per_pack)
    toks = pl.BlockSpec((steps, model), per_pack)
    return pl.pallas_call(
        functools.partial(backward_kernel, group=group, rank=rank, taps=taps),
        grid_spec=pltpu.PrefetchScalarGridSpec(
            num_scalar_prefetch=1,
            grid=(packs,),
            in_specs=[
                mats, mats,
                pl.BlockSpec((steps + ROWS, width), per_pack),
                mats,
                pl.BlockSpec((steps, LANES), per_pack),
                whole(sela), whole(stepb), whole(vec), whole(a2),
                pl.BlockSpec((steps // ROWS, states, width), lambda p, lens: (p, 0, 0)),
                whole(wx), toks, whole(gain), toks, toks,
            ],
            out_specs=[
                mats,
                pl.BlockSpec((width, LANES), fixed),
                pl.BlockSpec((width, LANES), fixed),
                pl.BlockSpec((1, model), fixed),
                toks,
            ],
            scratch_shapes=[
                pltpu.VMEM((states, width), F32),
                pltpu.VMEM((steps * states, LANES), F32),
                pltpu.VMEM((steps * states, LANES), F32),
                pltpu.VMEM((steps * states, LANES), F32),
                pltpu.VMEM((steps * states, LANES), F32),
                pltpu.VMEM((steps + ROWS, width), F32),
                pltpu.VMEM((steps, width), F32),
                pltpu.VMEM((steps, width), BF16),
                pltpu.VMEM((ROWS, width), F32),
                pltpu.VMEM((states, width), F32),
            ],
        ),
        out_shape=[
            jax.ShapeDtypeStruct((rows, width), BF16),
            jax.ShapeDtypeStruct((width, LANES), F32),
            jax.ShapeDtypeStruct((width, LANES), F32),
            jax.ShapeDtypeStruct((1, model), F32),
            jax.ShapeDtypeStruct((rows, model), F32),
        ],
        compiler_params=pltpu.CompilerParams(vmem_limit_bytes=60 << 20),
        cost_estimate=pl.CostEstimate(flops=0, bytes_accessed=190_000_000, transcendentals=0),
        name="mixer_backward",
    )(sample, delta, xs, bx, gm, sel, sela, stepb, vec, a2, hall, wx, tokens, gain, grad_u, grad_h)


def expert_kernel(*refs, parts):
    q_ref, gy_ref, router_ref, mine_ref = refs[:4]
    ups, downs = refs[4 : 4 + parts], refs[4 + parts : 4 + 2 * parts]
    outs = refs[4 + 2 * parts :]
    result_ref, gq_ref, gr_ref, grouter_ref = outs[:4]
    acts, grads = outs[4 : 4 + parts], outs[4 + parts : 4 + 2 * parts]
    total, back, gates = outs[4 + 2 * parts :]
    step = pl.program_id(0)

    @pl.when(step == 0)
    def _():
        logits = dot(q_ref[...], router_ref[...], ((1,), (1,)))
        odds = jnp.exp(logits - jnp.max(logits, axis=1, keepdims=True))
        probs = odds / jnp.sum(odds, axis=1, keepdims=True)
        gate = jnp.sum(probs * mine_ref[...], axis=1, keepdims=True)
        gates[...] = gate * (mine_ref[...] - probs)
        gr_ref[...] = (gate * gy_ref[...].astype(F32)).astype(BF16)
        total[...] = jnp.zeros_like(total)
        back[...] = jnp.zeros_like(back)

    q, gr = q_ref[...], gr_ref[...]
    root = 0.7978845608028654
    for k in range(parts):
        pre = dot(q, ups[k][...])
        grad_act = dot(gr, downs[k][...], ((1,), (1,)))
        square = pre * pre
        t = jnp.tanh(root * pre * (1.0 + 0.044715 * square))
        half = 0.5 * (1.0 + t)
        act = (pre * half).astype(BF16)
        slope = half + (0.5 * root) * pre * (1.0 - t * t) * (1.0 + 0.134145 * square)
        grad = (grad_act * slope).astype(BF16)
        acts[k][...] = act
        grads[k][...] = grad
        total[...] += dot(act, downs[k][...])
        back[...] += dot(grad, ups[k][...], ((1,), (1,)))

    @pl.when(step == pl.num_programs(0) - 1)
    def _():
        result = total[...].astype(BF16)
        result_ref[...] = result
        grad_gate = jnp.sum(gy_ref[...].astype(F32) * result.astype(F32), axis=1, keepdims=True)
        grad_logits = (grad_gate * gates[...]).astype(BF16)
        grouter_ref[...] = dot(grad_logits, q_ref[...], ((0,), (0,)))
        gq_ref[...] = (dot(grad_logits, router_ref[...]) + back[...]).astype(BF16)


def expert_pass(q, gy, router, mine, ups, downs):
    rows, model = q.shape
    experts = router.shape[0]
    parts = len(ups)
    hidden = ups[0].shape[1]
    block = 256 if hidden % 256 == 0 else 128
    fixed = lambda i: (0, 0)
    whole = lambda shape: pl.BlockSpec(shape, fixed)
    across = lambda n: pl.BlockSpec((n, block), lambda i: (0, i))
    down = pl.BlockSpec((block, model), lambda i: (i, 0))
    outs = pl.pallas_call(
        functools.partial(expert_kernel, parts=parts),
        grid=(hidden // block,),
        in_specs=[whole(q.shape), whole(gy.shape), whole(router.shape), whole(mine.shape)]
        + [across(model)] * parts
        + [down] * parts,
        out_specs=[whole((rows, model))] * 3 + [whole((experts, model))] + [across(rows)] * (2 * parts),
        out_shape=[jax.ShapeDtypeStruct((rows, model), BF16)] * 3
        + [jax.ShapeDtypeStruct((experts, model), F32)]
        + [jax.ShapeDtypeStruct((rows, hidden), BF16)] * (2 * parts),
        scratch_shapes=[pltpu.VMEM((rows, model), F32), pltpu.VMEM((rows, model), F32), pltpu.VMEM((rows, experts), F32)],
        compiler_params=pltpu.CompilerParams(vmem_limit_bytes=56 << 20),
        cost_estimate=pl.CostEstimate(flops=0, bytes_accessed=70_000_000, transcendentals=0),
        name="expert_pass",
    )(q, gy, router, mine, *ups, *downs)
    return (*outs[:4], outs[4 : 4 + parts], outs[4 + parts :])
def live_rows(length, steps):
    return (lax.broadcasted_iota(jnp.int32, (steps, 1), 0) < length).astype(F32)


def norm_of(values):
    inv = lax.rsqrt(jnp.mean(values * values, axis=1, keepdims=True) + EPSILON)
    return values * inv, inv


def home_forward_kernel(len_ref, u_ref, wl_ref, wr_ref, wout_ref, mix_ref, x_ref, gain_ref, router_ref, hot_ref, choose_ref,
                        z_ref, gated_ref, h1_ref, weight_ref, sent_ref, total):
    pack = pl.program_id(0)
    steps, model = u_ref.shape
    mixed = jnp.zeros((steps, model), F32)
    for half, w_ref in enumerate((wl_ref, wr_ref)):
        here = slice(half * model, (half + 1) * model)
        z = dot(u_ref[...], w_ref[...])
        z_ref[:, here] = z
        gated = (mix_ref[:, here] * (z * jax.nn.sigmoid(z))).astype(BF16)
        gated_ref[:, here] = gated
        mixed = mixed + dot(gated, wout_ref[here, :])
    h1 = x_ref[...].astype(F32) + live_rows(len_ref[pack], steps) * mixed
    h1_ref[...] = h1
    routed = (norm_of(h1)[0] * gain_ref[...]).astype(BF16)
    logits = dot(routed, router_ref[...], ((1,), (1,)))
    odds = jnp.exp(logits - jnp.max(logits, axis=1, keepdims=True))
    probs = odds / jnp.sum(odds, axis=1, keepdims=True)
    weight_ref[...] = jnp.sum(probs * hot_ref[...], axis=1, keepdims=True)
    sent = dot(choose_ref[...], routed)

    @pl.when(pack == 0)
    def _():
        total[...] = sent

    @pl.when(pack > 0)
    def _():
        total[...] += sent

    @pl.when(pack == pl.num_programs(0) - 1)
    def _():
        sent_ref[...] = total[...].astype(BF16)


def home_forward(sample, u, wz, wout, mix, tokens, gain, router, hot, chooser):
    packs = sample.shape[0]
    rows, model = u.shape
    steps, inner, slots = rows // packs, mix.shape[1], chooser.shape[0]
    whole = lambda v: pl.BlockSpec(v.shape, lambda p, lens: (0, 0))
    part = lambda n: pl.BlockSpec((steps, n), lambda p, lens: (p, 0))
    return pl.pallas_call(
        home_forward_kernel,
        grid_spec=pltpu.PrefetchScalarGridSpec(
            num_scalar_prefetch=1,
            grid=(packs,),
            in_specs=[
                part(model), whole(wz[0]), whole(wz[1]), whole(wout), part(inner), part(model), whole(gain), whole(router),
                part(hot.shape[1]), pl.BlockSpec((slots, steps), lambda p, lens: (0, p)),
            ],
            out_specs=[
                part(inner), part(inner), part(model), part(1), pl.BlockSpec((slots, model), lambda p, lens: (0, 0)),
            ],
            scratch_shapes=[pltpu.VMEM((slots, model), F32)],
        ),
        out_shape=[
            jax.ShapeDtypeStruct((rows, inner), F32),
            jax.ShapeDtypeStruct((rows, inner), BF16),
            jax.ShapeDtypeStruct((rows, model), F32),
            jax.ShapeDtypeStruct((rows, 1), F32),
            jax.ShapeDtypeStruct((slots, model), BF16),
        ],
        compiler_params=pltpu.CompilerParams(vmem_limit_bytes=56 << 20),
        name="home_forward",
    )(sample, u, wz[0], wz[1], wout, mix, tokens, gain, router, hot, chooser)


def home_backward_kernel(len_ref, choose_ref, back_ref, h1_ref, gy_ref, gain_ref, wout_ref, z_ref, mix_ref, u_ref, gated_ref,
                         wl_ref, wr_ref,
                         gh_ref, gm_ref, gu_ref, ggain_ref, gwz_ref, gwout_ref, sum_z, sum_out):
    pack = pl.program_id(0)
    steps, model = u_ref.shape

    @pl.when(pack == 0)
    def _():
        ggain_ref[...] = jnp.zeros_like(ggain_ref)
        sum_z[...] = jnp.zeros_like(sum_z)
        sum_out[...] = jnp.zeros_like(sum_out)

    grad = dot(choose_ref[...], back_ref[...], ((0,), (0,)))
    normed, inv = norm_of(h1_ref[...])
    scaled = grad * gain_ref[...]
    ggain_ref[...] += jnp.sum(grad * normed, axis=0, keepdims=True)
    gh = gy_ref[...].astype(F32) + inv * (scaled - normed * jnp.mean(scaled * normed, axis=1, keepdims=True))
    gh_ref[...] = gh
    grad_mixed = (live_rows(len_ref[pack], steps) * gh).astype(BF16)
    grad_u = jnp.zeros((steps, model), F32)
    for half, w_ref in enumerate((wl_ref, wr_ref)):
        here = slice(half * model, (half + 1) * model)
        grad_gated = dot(grad_mixed, wout_ref[here, :], ((1,), (1,)))
        z = z_ref[:, here]
        sig = jax.nn.sigmoid(z)
        gm_ref[:, here] = grad_gated * (z * sig)
        grad_z = (grad_gated * mix_ref[:, here] * sig * (1.0 + z * (1.0 - sig))).astype(BF16)
        grad_u = grad_u + dot(grad_z, w_ref[...], ((1,), (1,)))
        sum_z[:, here] += dot(u_ref[...], grad_z, ((0,), (0,)))
        sum_out[here, :] += dot(gated_ref[:, here], grad_mixed, ((0,), (0,)))
    gu_ref[...] = grad_u

    @pl.when(pack == pl.num_programs(0) - 1)
    def _():
        gwz_ref[...] = sum_z[...].astype(BF16)
        gwout_ref[...] = sum_out[...].astype(BF16)


def home_backward(sample, chooser, back, h1, gy, gain, wout, z, mix, u, gated, wz):
    packs = sample.shape[0]
    rows, model = u.shape
    steps, inner, slots = rows // packs, mix.shape[1], chooser.shape[0]
    fixed = lambda p, lens: (0, 0)
    whole = lambda v: pl.BlockSpec(v.shape, fixed)
    part = lambda n: pl.BlockSpec((steps, n), lambda p, lens: (p, 0))
    return pl.pallas_call(
        home_backward_kernel,
        grid_spec=pltpu.PrefetchScalarGridSpec(
            num_scalar_prefetch=1,
            grid=(packs,),
            in_specs=[
                pl.BlockSpec((slots, steps), lambda p, lens: (0, p)), whole(back), part(model), part(model), whole(gain),
                whole(wout), part(inner), part(inner), part(model), part(inner), whole(wz[0]), whole(wz[1]),
            ],
            out_specs=[
                part(model), part(inner), part(model), whole(gain),
                pl.BlockSpec((model, inner), fixed), pl.BlockSpec((inner, model), fixed),
            ],
            scratch_shapes=[pltpu.VMEM((model, inner), F32), pltpu.VMEM((inner, model), F32)],
        ),
        out_shape=[
            jax.ShapeDtypeStruct((rows, model), F32),
            jax.ShapeDtypeStruct((rows, inner), F32),
            jax.ShapeDtypeStruct((rows, model), F32),
            jax.ShapeDtypeStruct((1, model), F32),
            jax.ShapeDtypeStruct((model, inner), BF16),
            jax.ShapeDtypeStruct((inner, model), BF16),
        ],
        compiler_params=pltpu.CompilerParams(vmem_limit_bytes=60 << 20),
        cost_estimate=pl.CostEstimate(flops=0, bytes_accessed=100_000, transcendentals=0),
        name="home_backward",
    )(sample, chooser, back, h1, gy, gain, wout, z, mix, u, gated, wz[0], wz[1])


def expert_grads_kernel(q_ref, gr_ref, *refs, parts):
    gps, acts, outs = refs[:parts], refs[parts : 2 * parts], refs[2 * parts :]
    for k in range(parts):
        outs[2 * k][...] = dot(q_ref[...], gps[k][...], ((0,), (0,))).astype(BF16)
        outs[2 * k + 1][...] = dot(acts[k][...], gr_ref[...], ((0,), (0,))).astype(BF16)


def expert_grads(q, gr, gps, acts):
    rows, model = q.shape
    hidden, parts = gps[0].shape[1], len(gps)
    block = 256 if hidden % 256 == 0 else 128
    whole = pl.BlockSpec((rows, model), lambda i: (0, 0))
    across = lambda n: pl.BlockSpec((n, block), lambda i: (0, i))
    down = pl.BlockSpec((block, model), lambda i: (i, 0))
    return pl.pallas_call(
        functools.partial(expert_grads_kernel, parts=parts),
        grid=(hidden // block,),
        in_specs=[whole, whole] + [across(rows)] * (2 * parts),
        out_specs=[across(model), down] * parts,
        out_shape=[jax.ShapeDtypeStruct((model, hidden), BF16), jax.ShapeDtypeStruct((hidden, model), BF16)] * parts,
        compiler_params=pltpu.CompilerParams(vmem_limit_bytes=60 << 20),
        cost_estimate=pl.CostEstimate(flops=0, bytes_accessed=100_000, transcendentals=0),
        name="expert_grads",
    )(q, gr, *gps, *acts)


def swap(values, axis, mask):
    count = lax.axis_size(axis)
    return lax.ppermute(values, axis, [(i, i ^ mask) for i in range(count)])


def grow(values, axis, mask, dim):
    got = swap(values, axis, mask)
    upper = (lax.axis_index(axis) & mask) != 0
    return jnp.concatenate([jnp.where(upper, got, values), jnp.where(upper, values, got)], axis=dim)


def gather_stages(width):
    bits = lax.axis_size("fsdp").bit_length() - 1
    place = lambda bit: bits - 1 - bit
    half = width // 2

    def single(bit):
        return lambda values: grow(values, "fsdp", 1 << bit, place(bit))

    def split(values):
        return grow(values[..., :half], "fsdp", 2, place(1)), grow(values[..., half:], "fsdp", 1, place(0))

    def join(pair):
        left, right = grow(pair[0], "fsdp", 1, place(0)), grow(pair[1], "fsdp", 2, place(1))
        return jnp.concatenate([left, right], axis=-1)

    def across(mask):
        return lambda values: grow(values.reshape(1, -1, width), "dp", mask, 0)

    masks = [1 << i for i in range(lax.axis_size("dp").bit_length() - 1)]
    return [single(bit) for bit in range(2, bits)] + [split, join] + [across(mask) for mask in masks]


def gather_both(early, late, lag, beside):
    bits = lax.axis_size("fsdp").bit_length() - 1
    shapes = [(-1, v.shape[1]) for v in (early, late)]
    values = [v.reshape((1,) * bits + v.shape) for v in (early, late)]
    stages = [gather_stages(v.shape[1]) for v in (early, late)]
    count = len(stages[0])
    for at in range(count + lag):
        if lag <= at:
            *values, beside = lax.optimization_barrier((*values, beside))
        if at < count:
            values[0] = stages[0][at](values[0])
        if at >= lag:
            values[1] = stages[1][at - lag](values[1])
    return [v.reshape(shape) for v, shape in zip(values, shapes)] + [beside]


def fold(values, count):
    rows = values.shape[-2] // count
    return jnp.concatenate([values[..., j * rows : (j + 1) * rows, :] for j in range(count)], axis=-1)


def unfold(values, count):
    width = values.shape[-1] // count
    return jnp.concatenate([values[..., j * width : (j + 1) * width] for j in range(count)], axis=-2)


def own_block(values, index, count, axis):
    size = values.shape[axis] // count
    return lax.dynamic_slice_in_dim(values, index * size, size, axis)


def scatter_begin(piece):
    me, groups = lax.axis_index("dp"), lax.axis_size("dp")
    sent = [swap(piece(me ^ k).astype(BF16), "dp", k) for k in range(1, groups)]
    total = piece(me).astype(F32)
    for got in sent:
        total = total + got.astype(F32)
    return total.astype(BF16)


def scatter_end(parts):
    return jnp.sum(lax.all_to_all(parts, "fsdp", 0, 0, tiled=True).astype(F32), axis=0)


def rows_of(left, right, i):
    product = dot(own_block(left, i, lax.axis_size("dp"), 1), right, ((0,), (0,)))
    return product.reshape(lax.axis_size("fsdp"), -1, product.shape[1])


def body(
    tokens,
    cotangent,
    routes,
    lengths,
    norm1_gain,
    input_weight,
    conv_weight,
    conv_bias,
    scan_weight,
    step_weight,
    step_bias,
    decay_log,
    skip_gain,
    out_weight,
    norm2_gain,
    router_weight,
    expert_up,
    expert_down,
):
    micro, steps, model = tokens.shape
    rows = micro * steps
    experts = lax.axis_size("fsdp")
    groups = lax.axis_size("dp")
    devices = experts * groups
    capacity = (5 * steps + 4 * experts - 1) // (4 * experts)
    slots = micro * capacity
    inner = input_weight.shape[1] // 2
    states = decay_log.shape[1]
    rank = step_weight.shape[1]
    taps = conv_weight.shape[1]
    own_model, own_inner = norm1_gain.shape[0], conv_bias.shape[0]

    half = experts // 2
    vectors = jnp.concatenate(
        [
            conv_weight,
            jnp.stack([conv_bias, step_bias, skip_gain, jnp.concatenate([norm1_gain, norm2_gain])]).T,
            decay_log,
            jnp.concatenate([router_weight[:, :half], router_weight[:, half:]], axis=0),
        ],
        axis=1,
    )
    padding = lambda n: jnp.zeros((own_inner, n), BF16)
    small = jnp.concatenate(
        [
            scan_weight,
            padding(LANES - rank - 2 * states),
            step_weight,
            vectors,
            padding(LANES - rank - vectors.shape[1]),
        ],
        axis=1,
    )
    folds = inner // (2 * LANES)
    late = jnp.concatenate([input_weight[:, inner : inner + model], input_weight[:, inner + model :], out_weight], axis=0)
    late = lax.all_gather(late, ("dp", "fsdp"), axis=0, tiled=False)
    input_z = [late[:, i * own_model : (i + 1) * own_model].reshape(model, model) for i in range(2)]
    output_full = late[:, 2 * own_model :].reshape(inner, model)
    ups = [expert_up[0]] + [swap(expert_up[0], "dp", k) for k in range(1, groups)]
    downs = [expert_down[0]] + [swap(expert_down[0], "dp", k) for k in range(1, groups)]

    place = jnp.arange(steps, dtype=jnp.int32)
    sample = lengths[:, 0, 0]
    live = (place[None, :] < sample[:, None]).astype(jnp.int32)
    route = routes[:, :, 0]
    expert_ids = jnp.arange(experts, dtype=jnp.int32)
    route_hot = (route[:, :, None] == expert_ids).astype(BF16)
    live_hot = route_hot * live[:, :, None].astype(BF16)
    earlier = (place[:, None] > place[None, :]).astype(BF16)
    before = lax.dot_general(
        jnp.broadcast_to(earlier, (micro, steps, steps)), live_hot, (((2,), (1,)), ((0,), (0,))),
        preferred_element_type=F32,
    )
    slot = jnp.sum(before * live_hot.astype(F32), axis=2).astype(jnp.int32)
    kept = (live * (slot < capacity).astype(jnp.int32)).reshape(rows)
    target = (route * slots + jnp.arange(micro, dtype=jnp.int32)[:, None] * capacity + slot).reshape(rows)
    chooser = (
        (jnp.arange(experts * slots, dtype=jnp.int32)[:, None] == target[None, :]) & (kept[None, :] == 1)
    ).astype(BF16)
    kept = kept.astype(F32)

    def to_experts(values):
        return lax.all_to_all(values.reshape(experts, slots, -1), "fsdp", 0, 0, tiled=True).reshape(experts * slots, -1)

    def from_experts(values):
        return dot(chooser, values.reshape(experts * slots, -1), ((0,), (0,)))

    def back_home(values):
        return lax.all_to_all(values.reshape(experts, slots, -1), "fsdp", 0, 0, tiled=True)

    cotangent = cotangent.reshape(rows, model)

    hidden = tokens.reshape(rows, model).astype(F32)
    inv_first = lax.rsqrt(jnp.mean(hidden * hidden, axis=-1, keepdims=True) + EPSILON)
    normed_first = hidden * inv_first
    input_x, small_full, upstream_rows = gather_both(
        input_weight[:, :inner], small, 1, dot(chooser, cotangent).astype(BF16)
    )
    upstream_sent = to_experts(upstream_rows)
    select_full, step_full = small_full[:, :LANES], small_full[:, LANES:]
    vectors_full = step_full[:, rank:].T
    vectors_first = vectors_full[:ROWS].astype(F32)
    decay_full = vectors_full[taps + 4 : taps + 4 + states].astype(F32)
    gains = vectors_full[taps + 3].reshape(devices, 2, own_model)
    gain_one = gains[:, 0].reshape(model).astype(F32)
    gain_two = gains[:, 1].reshape(model).astype(F32)
    router_full = vectors_full[taps + 4 + states : taps + 4 + states + half].reshape(half, devices, 2, own_model)
    router_full = router_full.transpose(2, 0, 1, 3).reshape(experts, model)

    normed_low = (normed_first * gain_one).astype(BF16)
    decay_mat = -jnp.exp(decay_full)
    decay_two = decay_mat * LOG2E
    branch_x, scan_in, step_size, selected, mixer_out, states_kept = mixer_forward(
        sample, normed_low, input_x, select_full, step_full, vectors_first, decay_two, micro, rank, taps
    )
    mixer_out, upstream_sent = lax.optimization_barrier((mixer_out, upstream_sent))
    kept_hot = route_hot.reshape(rows, experts).astype(F32) * kept[:, None]
    branch_z, gated_low, residual, weight_row, sent = home_forward(
        sample, normed_low, input_z, output_full, mixer_out, tokens.reshape(rows, model), gain_two[None, :], router_full,
        kept_hot, chooser,
    )
    received = to_experts(sent)

    mine = (expert_ids == lax.axis_index("fsdp")).astype(F32)[None, :]
    result, grad_rows, flat_grad, router_grad, acts, grad_pres = expert_pass(
        received, upstream_sent, router_full, mine, ups, downs
    )
    grad_rows, result, received, flat_grad = lax.optimization_barrier((grad_rows, result, received, flat_grad))
    grad_back = back_home(grad_rows)
    matrix_grads = expert_grads(received, flat_grad, grad_pres, acts)
    grad_back, matrix_grads = lax.optimization_barrier((grad_back, matrix_grads))
    up_own, down_own, *others = matrix_grads
    others = [swap(other, "dp", k // 2 + 1) for k, other in enumerate(others)]

    grad_residual, grad_mixer, grad_normed_z, gain_two_grad, input_z_grad, output_grad = home_backward(
        sample, chooser, grad_back.reshape(experts * slots, model), residual, cotangent, gain_two[None, :], output_full,
        branch_z, mixer_out, normed_low, gated_low, input_z,
    )
    late_terms = jnp.concatenate(
        [
            input_z_grad.reshape(devices, own_model, inner),
            fold(output_grad.reshape(devices, own_inner, model), 2),
        ],
        axis=1,
    ).reshape(-1, inner)
    late_grads = lax.psum_scatter(late_terms, ("dp", "fsdp"), scatter_dimension=0, tiled=True)
    grad_mixer, result, others = lax.optimization_barrier((grad_mixer, result, others))
    result = back_home(result)
    grad_x, select_grad, step_grad, gain_one_grad, tokens_grad = mixer_backward(
        sample, step_size, scan_in, branch_x, grad_mixer, selected, select_full, step_full, vectors_first, decay_two,
        states_kept, input_x, tokens.reshape(rows, model), gain_one[None, :], grad_normed_z, grad_residual,
        micro, rank, taps,
    )
    grad_x, result = lax.optimization_barrier((grad_x, result))

    gain_grads = jnp.concatenate(
        [gain_one_grad.reshape(devices, 1, own_model), gain_two_grad.reshape(devices, 1, own_model)], axis=1
    ).reshape(inner, 1)
    router_grads = (
        router_grad.reshape(2, half, devices, own_model).transpose(2, 0, 3, 1).reshape(inner, half)
    )
    at_gain, at_decay, at_router = rank + taps + 3, rank + taps + 4, rank + taps + 4 + states
    lane = jnp.arange(LANES)
    step_grad = jnp.where(lane == at_gain, gain_grads, step_grad) + jnp.pad(
        router_grads, ((0, 0), (at_router, LANES - at_router - half))
    )

    def early_terms(i):
        blocks = [own_block(v, i, groups, 0).reshape(experts, own_inner, LANES) for v in (select_grad, step_grad)]
        return jnp.concatenate([rows_of(normed_low, grad_x, i), fold(jnp.concatenate(blocks, axis=2), folds)], axis=1)

    early_parts, others, result = lax.optimization_barrier((scatter_begin(early_terms), others, result))
    early_grads = scatter_end(early_parts)
    up_grad, down_grad = up_own.astype(F32), down_own.astype(F32)
    for k in range(groups - 1):
        up_grad = up_grad + others[2 * k].astype(F32)
        down_grad = down_grad + others[2 * k + 1].astype(F32)
    late_grads = late_grads.astype(F32)
    block_output = (residual + weight_row * from_experts(result)).astype(BF16)
    small_grads = unfold(early_grads[own_model:], folds)
    vector_grads = small_grads[:, LANES:]
    routers = vector_grads[:, at_router : at_router + half]
    return (
        block_output.reshape(micro, steps, model),
        tokens_grad.reshape(micro, steps, model),
        vector_grads[:own_model, at_gain],
        jnp.concatenate([early_grads[:own_model], late_grads[:own_model]], axis=1),
        vector_grads[:, rank : rank + taps],
        vector_grads[:, rank + taps],
        small_grads[:, : rank + 2 * states],
        vector_grads[:, :rank],
        vector_grads[:, rank + taps + 1],
        vector_grads[:, at_decay : at_decay + states],
        vector_grads[:, rank + taps + 2],
        unfold(late_grads[own_model:], 2),
        vector_grads[own_model:, at_gain],
        jnp.concatenate([routers[:own_model], routers[own_model:]], axis=1),
        up_grad[None],
        down_grad[None],
    )


def solution(mesh):
    rows3 = P(None, ("dp", "fsdp"), None)
    vector = P(("dp", "fsdp"))
    matrix = P(("dp", "fsdp"), None)
    weights = (
        vector, matrix, matrix, vector, matrix, matrix, vector, matrix, vector, matrix, vector, matrix,
        P("fsdp", None, "dp"), P("fsdp", "dp", None),
    )
    return jax.shard_map(
        body,
        mesh=mesh,
        in_specs=(rows3, rows3, rows3, rows3) + weights,
        out_specs=(rows3, rows3) + weights,
        check_vma=False,
    )
```

profile of v0, /device:TPU:8, one launch (start us, length us, event | category | flops | bytes accessed | tf_op | source)
XLA Modules:
  0.0 375.8 jit_solution(5070011363729277034)
XLA Ops:
  14.9 2.8 convolution_convert_fusion.1
  18.3 2.1 collective-permute-start.2
  20.4 2.6 collective-permute-start.1
  23.0 8.7 %collective-permute-done.1 = bf16[1,2,1,1,24,1536]{5,4,3,2,1,0:T(8,128)(2,1)S(1)} collective-permute-done((bf16[1,2,1,1,24,1536]{5,4,3,2,1,0:T(8,128)(2,1)S(1)}, bf16[1,2,1,1,24,1536]{5,4,3,2,1,0:T(8,128)(2,1)S(1)}, u32[]{:S(2)}, u32[]{:S(2)}) %collective-permute-start.1) | collective-permute-done | bytes 147488 | tf_op jit(solution)/shard_map/ppermute | solution.py:661
  31.7 3.5 collective-permute-start.5
  38.5 2.2 collective-permute-done.3
  48.4 6.7 %collective-permute-done.6 = bf16[2,2,2,1,24,768]{5,4,3,2,1,0:T(8,128)(2,1)S(1)} collective-permute-done((bf16[2,2,2,1,24,768]{5,4,3,2,1,0:T(8,128)(2,1)S(1)}, bf16[2,2,2,1,24,768]{5,4,3,2,1,0:T(8,128)(2,1)S(1)}, u32[]{:S(2)}, u32[]{:S(2)}) %collective-permute-start.6) | collective-permute-done | bytes 294944 | tf_op jit(solution)/shard_map/ppermute | solution.py:661
  58.6 2.8 collective-permute-done.11
  65.7 6.2 %all-to-all-start = ((bf16[16,40,768]{2,1,0:T(8,128)(2,1)}), bf16[16,40,768]{2,1,0:T(8,128)(2,1)S(1)}, u32[]{:S(2)}, u32[]{:S(2)}) async-start(bf16[16,40,768]{2,1,0:T(8,128)(2,1)} %bitcast.19), calls=%async_computation | async-start | bytes 1966080 | tf_op jit(solution)/shard_map/all_to_all | solution.py:824
  77.8 23.9 %mixer_forward.1 = (f32[528,1536]{1,0:T(8,128)}, f32[512,1536]{1,0:T(8,128)}, f32[512,1536]{1,0:T(8,128)}, f32[512,128]{1,0:T(8,128)}, f32[512,1536]{1,0:T(8,128)}, /*index=5*/f32[64,16,1536]{2,1,0:T(8,128)}) custom-call(s32[2]{0:T(128)} %copy-done.17, bf16[512,768]{1,0:T(8,128)(2,1)} %multiply_convert_fusion.u_ref, bf16[768,1536]{1,0:T(8,128)(2,1)} %bitcast.77, ...), custom_call_target="tpu_custom_call" | custom-call | bytes 120000000 | tf_op jit(solution)/shard_map/mixer_forward/pallas_call | solution.py:179
  101.8 3.6 slice.267
  107.4 11.5 %home_forward.1 = (f32[512,1536]{1,0:T(8,128)}, bf16[512,1536]{1,0:T(8,128)(2,1)}, f32[512,768]{1,0:T(8,128)}, f32[512,1]{1,0:T(8,128)}, bf16[640,768]{1,0:T(8,128)(2,1)}) custom-call(s32[2]{0:T(128)} %copy-done.17, bf16[512,768]{1,0:T(8,128)(2,1)} %multiply_convert_fusion.u_ref, bf16[768,768]{1,0:T(8,128)(2,1)} %bitcast.99, bf16[768,768]{1,0:T(8,128)(2,1)} %bitcast.97, ...), custom_call_target="tpu_custom_call" | custom-call | tf_op jit(solution)/shard_map/home_forward/pallas_call | solution.py:533
  118.9 11.2 %all-to-all-start.1 = ((bf16[16,40,768]{2,1,0:T(8,128)(2,1)}), bf16[16,40,768]{2,1,0:T(8,128)(2,1)S(1)}, u32[]{:S(2)}, u32[]{:S(2)}) async-start(bf16[16,40,768]{2,1,0:T(8,128)(2,1)} %bitcast.120), calls=%async_computation.1 | async-start | bytes 1966080 | tf_op jit(solution)/shard_map/all_to_all | solution.py:824
  130.6 21.8 %all-to-all-done.1 = bf16[16,40,768]{2,1,0:T(8,128)(2,1)S(1)} async-done(((bf16[16,40,768]{2,1,0:T(8,128)(2,1)}), bf16[16,40,768]{2,1,0:T(8,128)(2,1)S(1)}, u32[]{:S(2)}, u32[]{:S(2)}) %all-to-all-start.1) | async-done | bytes 983072 | tf_op jit(solution)/shard_map/all_to_all | solution.py:824
  153.3 22.8 %expert_pass.1 = (bf16[640,768]{1,0:T(8,128)(2,1)}, bf16[640,768]{1,0:T(8,128)(2,1)}, bf16[640,768]{1,0:T(8,128)(2,1)}, f32[16,768]{1,0:T(8,128)}, bf16[640,1536...) custom-call(bf16[640,768]{1,0:T(8,128)(2,1)} %bitcast.101, ...), custom_call_target="tpu_custom_call" | custom-call | bytes 70000000 | tf_op jit(solution)/shard_map/expert_pass/pallas_call | solution.py:468
  176.1 5.0 %all-to-all-start.2 = ((bf16[16,40,768]{2,1,0:T(8,128)(2,1)}), bf16[16,40,768]{2,1,0:T(8,128)(2,1)S(1)}, u32[]{:S(2)}, u32[]{:S(2)}) async-start(bf16[16,40,768]{2,1,0:T(8,128)(2,1)} %bitcast.119), calls=%async_computation.2 | async-start | bytes 1966080 | tf_op jit(solution)/shard_map/all_to_all | solution.py:830
  181.1 12.1 %expert_grads.1 = (bf16[768,1536]{1,0:T(8,128)(2,1)}, bf16[1536,768]{1,0:T(8,128)(2,1)}, bf16[768,1536]{1,0:T(8,128)(2,1)}, bf16[1536,768]{1,0:T(8,128)(2,1)}) custom-call(bf16[640,768]{1,0:T(8,128)(2,1)} %bitcast.102, bf16[640,768]{1,0:T(8,128)(2,1)} %get-tuple-element.119.gr_ref, bf16[640,1536]{1,0:T(8,128)(2,1)} %get-tuple-element.120.refs_0_, ...), custom_call_target="tpu_custom_call" | custom-call | bytes 100000 | tf_op jit(solution)/shard_map/expert_grads/pallas_call | solution.py:647
  193.1 10.5 %all-to-all-done.2 = bf16[16,40,768]{2,1,0:T(8,128)(2,1)S(1)} async-done(((bf16[16,40,768]{2,1,0:T(8,128)(2,1)}), bf16[16,40,768]{2,1,0:T(8,128)(2,1)S(1)}, u32[]{:S(2)}, u32[]{:S(2)}) %all-to-all-start.2) | async-done | bytes 983072 | tf_op jit(solution)/shard_map/all_to_all | solution.py:830
  205.4 17.6 %home_backward.1 = (f32[512,768]{1,0:T(8,128)}, f32[512,1536]{1,0:T(8,128)}, f32[512,768]{1,0:T(8,128)}, f32[1,768]{1,0:T(1,128)}, bf16[768,1536]{1,0:T(8,128)(2,1)}, /*index=5*/bf16[1536,768]{1,0:T(8,128)(2,1)}) custom-call(s32[2]{0:T(128)} %copy-done.17, bf16[640,512]{1,0:T(8,128)(2,1)} %fusion.3.choose_ref, bf16[640,768]{1,0:T(8,128)(2,1)} %bitcast.110, ...), custom_call_target="tpu_custom_call" | custom-call | bytes 100000 | tf_op jit(solution)/shard_map/home_backward/pallas_call | solution.py:604
  223.8 1.9 fusion.41
  226.2 2.4 maximum_maximum_fusion
  228.6 5.0 %all-to-all-start.3 = ((bf16[16,40,768]{2,1,0:T(8,128)(2,1)}), bf16[16,40,768]{2,1,0:T(8,128)(2,1)S(1)}, u32[]{:S(2)}, u32[]{:S(2)}) async-start(bf16[16,40,768]{2,1,0:T(8,128)(2,1)} %bitcast.28), calls=%async_computation.3 | async-start | bytes 1966080 | tf_op jit(solution)/shard_map/all_to_all | solution.py:830
  233.5 55.5 %mixer_backward.1 = (bf16[512,1536]{1,0:T(8,128)(2,1)}, f32[1536,128]{1,0:T(8,128)}, f32[1536,128]{1,0:T(8,128)}, f32[1,768]{1,0:T(1,128)}, f32[512,768]{1,0:T(8,128)}) custom-call(s32[2]{0:T(128)} %copy-done.17, f32[512,1536]{1,0:T(8,128)} %get-tuple-element.109.delta_ref, f32[512,1536]{1,0:T(8,128)} %get-tuple-element.110.xs_ref, ...), custom_call_target="tpu_custom_call" | custom-call | bytes 190000000 | tf_op jit(solution)/shard_map/mixer_backward/pallas_call | solution.py:365
  292.9 2.6 convolution_convert_fusion
  296.8 5.7 %collective-permute-start.18 = (bf16[16,32,1536]{2,1,0:T(8,128)(2,1)}, bf16[16,32,1536]{2,1,0:T(8,128)(2,1)}, u32[]{:S(2)}, u32[]{:S(2)}) collective-permute-start(bf16[16,32,1536]{2,1,0:T(8,128)(2,1)} %pad_maximum_fusion.1), channel_id=1, source_target_pairs={{0,16},{16,0},{1,17},{17,1},{2,18},{18,2},{3,19},{19,3},{4,20},{20... | collective-permute-start | bytes 4718600 | tf_op jit(solution)/shard_map/ppermute | solution.py:661
  305.9 3.2 fusion
  309.1 14.3 %all-to-all-start.4 = ((bf16[16,32,1536]{2,1,0:T(8,128)(2,1)}), bf16[16,32,1536]{2,1,0:T(8,128)(2,1)S(1)}, u32[]{:S(2)}, u32[]{:S(2)}) async-start(bf16[16,32,1536]{2,1,0:T(8,128)(2,1)} %fusion), calls=%async_computation.4 | async-start | bytes 3145728 | tf_op jit(solution)/shard_map/all_to_all | solution.py:733
  323.6 3.1 add_convert_fusion
  326.7 4.5 %add_bitcast_fusion = f32[1,1536,768]{2,1,0:T(8,128)} fusion(bf16[1536,768]{1,0:T(8,128)(2,1)} %collective-permute-done.17, bf16[1536,768]{1,0:T(8,128)(2,1)S(1)} %copy-done.7), kind=kLoop, calls=%fused_computation.1 | loop fusion | flops 3538944 | bytes 9437184 | tf_op jit(solution)/shard_map/broadcast_in_dim | solution.py:940
  331.3 4.5 %add_bitcast_fusion.1 = f32[1,768,1536]{2,1,0:T(8,128)} fusion(bf16[768,1536]{1,0:T(8,128)(2,1)} %collective-permute-done.16, bf16[768,1536]{1,0:T(8,128)(2,1)S(1)} %copy-done.6), kind=kLoop, calls=%fused_computation.2 | loop fusion | flops 3538944 | bytes 9437184 | tf_op jit(solution)/shard_map/broadcast_in_dim | solution.py:939
  335.8 5.1 %reduce-scatter.2.cloned.1.call-done = bf16[48,1536]{1,0:T(8,128)(2,1)} async-done(((bf16[1536,1536]{1,0:T(8,128)(2,1)}), bf16[48,1536]{1,0:T(8,128)(2,1)}) %reduce-scatter.2.cloned.1.call-update) | async-done | bytes 147472 | tf_op jit(solution)/shard_map/reduce_scatter | solution.py:887
  343.3 18.9 %all-to-all-done.4 = bf16[16,32,1536]{2,1,0:T(8,128)(2,1)S(1)} async-done(((bf16[16,32,1536]{2,1,0:T(8,128)(2,1)}), bf16[16,32,1536]{2,1,0:T(8,128)(2,1)S(1)}, u32[]{:S(2)}, u32[]{:S(2)}) %all-to-all-start.4) | async-done | bytes 1572896 | tf_op jit(solution)/shard_map/all_to_all | solution.py:733
  (218 shorter events, 56.6 us)
Async XLA Ops:
  7.2 10.5 %copy-start.24 = (bf16[48]{0:T(256)(128)(2,1)S(1)}, bf16[48]{0:T(256)(128)(2,1)}, u32[]{:S(2)}) copy-start(bf16[48]{0:T(256)(128)(2,1)} %param.25) | copy-start | bytes 292
  7.2 10.7 %copy-start.21 = (bf16[48,4]{0,1:T(4,128)(2,1)S(1)}, bf16[48,4]{0,1:T(4,128)(2,1)}, u32[]{:S(2)}) copy-start(bf16[48,4]{0,1:T(4,128)(2,1)} %param.24) | copy-start | bytes 1156
  7.2 94.6 %all-gather.3.cloned.1.call-start = ((), (), s32[]{:S(2)}) async-start(), calls=%async_computation.7 | async-start | bytes 4866048 | tf_op jit(solution)/shard_map/all_gather | solution.py:797
  8.2 10.0 %collective-permute-start = (bf16[1,1,1,1,24,1536]{5,4,3,2,1,0:T(8,128)(2,1)S(1)}, bf16[1,1,1,1,24,1536]{5,4,3,2,1,0:T(8,128)(2,1)S(1)}, u32[]{:S(2)}, u32[]{:S(2)}) collective-permute-start(bf16[1,1,1,1,24,1536]{5,4,3,2,1,0:T(8,128)(2,1)S(1)} %slice_bitcast_fusion), channel_id=1, source_target_pairs={{0,4},{1,5},{2,6},{3,7},{4,0},{5,1},{6,2},{7,3},{8,12},{9,13},{10,... | collective-permute-start | bytes 221192 | tf_op jit(solution)/shard_map/ppermute | solution.py:661
  11.5 11.4 %copy-start.17 = (s32[2]{0:T(128)}, s32[2]{0:T(128)S(1)}, u32[]{:S(2)}) copy-start(s32[2]{0:T(128)S(1)} %slice_reduce_fusion.6.len_ref) | copy-start | bytes 28
  18.3 4.7 %collective-permute-start.2 = (bf16[1,1,1,1,48,256]{5,4,3,2,1,0:T(8,128)(2,1)S(1)}, bf16[1,1,1,1,48,256]{5,4,3,2,1,0:T(8,128)(2,1)S(1)}, u32[]{:S(2)}, u32[]{:S(2)}) collective-permute-start(bf16[1,1,1,1,48,256]{5,4,3,2,1,0:T(8,128)(2,1)S(1)} %bitcast.129), channel_id=1, source_target_pairs={{0,4},{1,5},{2,6},{3,7},{4,0},{5,1},{6,2},{7,3},{8,12},{9,13},{10,... | collective-permute-start | bytes 73736 | tf_op jit(solution)/shard_map/ppermute | solution.py:661
  20.4 11.3 %collective-permute-start.1 = (bf16[1,2,1,1,24,1536]{5,4,3,2,1,0:T(8,128)(2,1)S(1)}, bf16[1,2,1,1,24,1536]{5,4,3,2,1,0:T(8,128)(2,1)S(1)}, u32[]{:S(2)}, u32[]{:S(2)}) collective-permute-start(bf16[1,2,1,1,24,1536]{5,4,3,2,1,0:T(8,128)(2,1)S(1)} %pad_maximum_fusion.7), channel_id=1, source_target_pairs={{0,8},{1,9},{2,10},{3,11},{4,12},{5,13},{6,14},{7,15},{8,0},{9,1},... | collective-permute-start | bytes 442376 | tf_op jit(solution)/shard_map/ppermute | solution.py:661
  31.7 6.8 %collective-permute-start.5 = (bf16[1,2,1,1,48,256]{5,4,3,2,1,0:T(8,128)(2,1)S(1)}, bf16[1,2,1,1,48,256]{5,4,3,2,1,0:T(8,128)(2,1)S(1)}, u32[]{:S(2)}, u32[]{:S(2)}) collective-permute-start(bf16[1,2,1,1,48,256]{5,4,3,2,1,0:T(8,128)(2,1)S(1)} %pad_maximum_fusion.14), channel_id=1, source_target_pairs={{0,8},{1,9},{2,10},{3,11},{4,12},{5,13},{6,14},{7,15},{8,0},{9,1},... | collective-permute-start | bytes 147464 | tf_op jit(solution)/shard_map/ppermute | solution.py:661
  35.3 5.4 %collective-permute-start.3 = (bf16[2,2,1,1,24,768]{5,4,3,2,1,0:T(8,128)(2,1)S(1)}, bf16[2,2,1,1,24,768]{5,4,3,2,1,0:T(8,128)(2,1)S(1)}, u32[]{:S(2)}, u32[]{:S(2)}) collective-permute-start(bf16[2,2,1,1,24,768]{5,4,3,2,1,0:T(8,128)(2,1)S(1)} %get-tuple-element.266), channel_id=1, source_target_pairs={{0,2},{1,3},{2,0},{3,1},{4,6},{5,7},{6,4},{7,5},{8,10},{9,11},{10,... | collective-permute-start | bytes 442376 | tf_op jit(solution)/shard_map/ppermute | solution.py:661
  37.1 5.1 %collective-permute-start.4 = (bf16[2,2,1,1,24,768]{5,4,3,2,1,0:T(8,128)(2,1)S(1)}, bf16[2,2,1,1,24,768]{5,4,3,2,1,0:T(8,128)(2,1)S(1)}, u32[]{:S(2)}, u32[]{:S(2)}) collective-permute-start(bf16[2,2,1,1,24,768]{5,4,3,2,1,0:T(8,128)(2,1)S(1)} %get-tuple-element.265), channel_id=1, source_target_pairs={{0,1},{1,0},{2,3},{3,2},{4,5},{5,4},{6,7},{7,6},{8,9},{9,8},{10,11... | collective-permute-start | bytes 442376 | tf_op jit(solution)/shard_map/ppermute | solution.py:661
  42.4 5.0 %collective-permute-start.8 = (bf16[2,2,1,1,48,128]{5,4,3,2,1,0:T(8,128)(2,1)S(1)}, bf16[2,2,1,1,48,128]{5,4,3,2,1,0:T(8,128)(2,1)S(1)}, u32[]{:S(2)}, u32[]{:S(2)}) collective-permute-start(bf16[2,2,1,1,48,128]{5,4,3,2,1,0:T(8,128)(2,1)S(1)} %get-tuple-element.295), channel_id=1, source_target_pairs={{0,2},{1,3},{2,0},{3,1},{4,6},{5,7},{6,4},{7,5},{8,10},{9,11},{10,... | collective-permute-start | bytes 147464 | tf_op jit(solution)/shard_map/ppermute | solution.py:661
  42.7 5.6 %collective-permute-start.9 = (bf16[2,2,1,1,48,128]{5,4,3,2,1,0:T(8,128)(2,1)S(1)}, bf16[2,2,1,1,48,128]{5,4,3,2,1,0:T(8,128)(2,1)S(1)}, u32[]{:S(2)}, u32[]{:S(2)}) collective-permute-start(bf16[2,2,1,1,48,128]{5,4,3,2,1,0:T(8,128)(2,1)S(1)} %get-tuple-element.294), channel_id=1, source_target_pairs={{0,1},{1,0},{2,3},{3,2},{4,5},{5,4},{6,7},{7,6},{8,9},{9,8},{10,11... | collective-permute-start | bytes 147464 | tf_op jit(solution)/shard_map/ppermute | solution.py:661
  44.4 10.7 %collective-permute-start.6 = (bf16[2,2,2,1,24,768]{5,4,3,2,1,0:T(8,128)(2,1)S(1)}, bf16[2,2,2,1,24,768]{5,4,3,2,1,0:T(8,128)(2,1)S(1)}, u32[]{:S(2)}, u32[]{:S(2)}) collective-permute-start(bf16[2,2,2,1,24,768]{5,4,3,2,1,0:T(8,128)(2,1)S(1)} %pad_maximum_fusion.4), channel_id=1, source_target_pairs={{0,1},{1,0},{2,3},{3,2},{4,5},{5,4},{6,7},{7,6},{8,9},{9,8},{10,11... | collective-permute-start | bytes 884744 | tf_op jit(solution)/shard_map/ppermute | solution.py:661
  44.8 10.4 %collective-permute-start.7 = (bf16[2,2,1,2,24,768]{5,4,3,2,1,0:T(8,128)(2,1)S(1)}, bf16[2,2,1,2,24,768]{5,4,3,2,1,0:T(8,128)(2,1)S(1)}, u32[]{:S(2)}, u32[]{:S(2)}) collective-permute-start(bf16[2,2,1,2,24,768]{5,4,3,2,1,0:T(8,128)(2,1)S(1)} %pad_maximum_fusion.5), channel_id=1, source_target_pairs={{0,2},{1,3},{2,0},{3,1},{4,6},{5,7},{6,4},{7,5},{8,10},{9,11},{10,... | collective-permute-start | bytes 884744 | tf_op jit(solution)/shard_map/ppermute | solution.py:661
  55.4 6.5 %collective-permute-start.10 = (bf16[1,384,1536]{2,1,0:T(8,128)(2,1)S(1)}, bf16[1,384,1536]{2,1,0:T(8,128)(2,1)S(1)}, u32[]{:S(2)}, u32[]{:S(2)}) collective-permute-start(bf16[1,384,1536]{2,1,0:T(8,128)(2,1)S(1)} %bitcast.105), channel_id=1, source_target_pairs={{0,16},{16,0},{1,17},{17,1},{2,18},{18,2},{3,19},{19,3},{4,20},{20... | collective-permute-start | bytes 3538952 | tf_op jit(solution)/shard_map/ppermute | solution.py:661
  55.4 75.1 %collective-permute-start.14 = (bf16[768,1536]{1,0:T(8,128)(2,1)}, bf16[768,1536]{1,0:T(8,128)(2,1)}, u32[]{:S(2)}, u32[]{:S(2)}) collective-permute-start(bf16[768,1536]{1,0:T(8,128)(2,1)} %bitcast.24.refs_4_), channel_id=1, source_target_pairs={{0,16},{16,0},{1,17},{17,1},{2,18},{18,2},{3,19},{19,3},{4,20},{20... | collective-permute-start | bytes 7077896 | tf_op jit(solution)/shard_map/ppermute | solution.py:661
  55.9 74.6 %collective-permute-start.15 = (bf16[1536,768]{1,0:T(8,128)(2,1)}, bf16[1536,768]{1,0:T(8,128)(2,1)}, u32[]{:S(2)}, u32[]{:S(2)}) collective-permute-start(bf16[1536,768]{1,0:T(8,128)(2,1)} %bitcast.25.refs_6_), channel_id=1, source_target_pairs={{0,16},{16,0},{1,17},{17,1},{2,18},{18,2},{3,19},{19,3},{4,20},{20... | collective-permute-start | bytes 7077896 | tf_op jit(solution)/shard_map/ppermute | solution.py:661
  56.5 4.9 %collective-permute-start.11 = (bf16[2,2,2,1,48,128]{5,4,3,2,1,0:T(8,128)(2,1)S(1)}, bf16[2,2,2,1,48,128]{5,4,3,2,1,0:T(8,128)(2,1)S(1)}, u32[]{:S(2)}, u32[]{:S(2)}) collective-permute-start(bf16[2,2,2,1,48,128]{5,4,3,2,1,0:T(8,128)(2,1)S(1)} %pad_maximum_fusion.12), channel_id=1, source_target_pairs={{0,1},{1,0},{2,3},{3,2},{4,5},{5,4},{6,7},{7,6},{8,9},{9,8},{10,11... | collective-permute-start | bytes 294920 | tf_op jit(solution)/shard_map/ppermute | solution.py:661
  57.2 4.6 %collective-permute-start.12 = (bf16[2,2,1,2,48,128]{5,4,3,2,1,0:T(8,128)(2,1)S(1)}, bf16[2,2,1,2,48,128]{5,4,3,2,1,0:T(8,128)(2,1)S(1)}, u32[]{:S(2)}, u32[]{:S(2)}) collective-permute-start(bf16[2,2,1,2,48,128]{5,4,3,2,1,0:T(8,128)(2,1)S(1)} %pad_maximum_fusion.13), channel_id=1, source_target_pairs={{0,2},{1,3},{2,0},{3,1},{4,6},{5,7},{6,4},{7,5},{8,10},{9,11},{10,... | collective-permute-start | bytes 294920 | tf_op jit(solution)/shard_map/ppermute | solution.py:661
  63.7 8.2 %collective-permute-start.13 = (bf16[1,768,256]{2,1,0:T(8,128)(2,1)S(1)}, bf16[1,768,256]{2,1,0:T(8,128)(2,1)S(1)}, u32[]{:S(2)}, u32[]{:S(2)}) collective-permute-start(bf16[1,768,256]{2,1,0:T(8,128)(2,1)S(1)} %bitcast.114), channel_id=1, source_target_pairs={{0,16},{16,0},{1,17},{17,1},{2,18},{18,2},{3,19},{19,3},{4,20},{20... | collective-permute-start | bytes 1179656 | tf_op jit(solution)/shard_map/ppermute | solution.py:661
  65.7 36.1 %all-to-all-start = ((bf16[16,40,768]{2,1,0:T(8,128)(2,1)}), bf16[16,40,768]{2,1,0:T(8,128)(2,1)S(1)}, u32[]{:S(2)}, u32[]{:S(2)}) async-start(bf16[16,40,768]{2,1,0:T(8,128)(2,1)} %bitcast.19), calls=%async_computation | async-start | bytes 1966080 | tf_op jit(solution)/shard_map/all_to_all | solution.py:824
  118.9 33.5 %all-to-all-start.1 = ((bf16[16,40,768]{2,1,0:T(8,128)(2,1)}), bf16[16,40,768]{2,1,0:T(8,128)(2,1)S(1)}, u32[]{:S(2)}, u32[]{:S(2)}) async-start(bf16[16,40,768]{2,1,0:T(8,128)(2,1)} %bitcast.120), calls=%async_computation.1 | async-start | bytes 1966080 | tf_op jit(solution)/shard_map/all_to_all | solution.py:824
  176.1 27.6 %all-to-all-start.2 = ((bf16[16,40,768]{2,1,0:T(8,128)(2,1)}), bf16[16,40,768]{2,1,0:T(8,128)(2,1)S(1)}, u32[]{:S(2)}, u32[]{:S(2)}) async-start(bf16[16,40,768]{2,1,0:T(8,128)(2,1)} %bitcast.119), calls=%async_computation.2 | async-start | bytes 1966080 | tf_op jit(solution)/shard_map/all_to_all | solution.py:830
  181.0 159.9 %reduce-scatter.2.cloned.1.call-start = ((), (), s32[]{:S(2)}) async-start(), calls=%async_computation.6 | async-start | bytes 4866048 | tf_op jit(solution)/shard_map/reduce_scatter | solution.py:887
  181.1 23.8 %copy-start.15 = (f32[16,768]{1,0:T(8,128)S(1)}, f32[16,768]{1,0:T(8,128)}, u32[]{:S(2)}) copy-start(f32[16,768]{1,0:T(8,128)} %get-tuple-element.147) | copy-start | bytes 147460
  203.7 24.9 %collective-permute-start.16 = (bf16[768,1536]{1,0:T(8,128)(2,1)}, bf16[768,1536]{1,0:T(8,128)(2,1)}, u32[]{:S(2)}, u32[]{:S(2)}) collective-permute-start(bf16[768,1536]{1,0:T(8,128)(2,1)} %get-tuple-element.133), channel_id=1, source_target_pairs={{0,16},{16,0},{1,17},{17,1},{2,18},{18,2},{3,19},{19,3},{4,20},{20... | collective-permute-start | bytes 7077896 | tf_op jit(solution)/shard_map/ppermute | solution.py:661
  203.7 24.9 %collective-permute-start.17 = (bf16[1536,768]{1,0:T(8,128)(2,1)}, bf16[1536,768]{1,0:T(8,128)(2,1)}, u32[]{:S(2)}, u32[]{:S(2)}) collective-permute-start(bf16[1536,768]{1,0:T(8,128)(2,1)} %get-tuple-element.134), channel_id=1, source_target_pairs={{0,16},{16,0},{1,17},{17,1},{2,18},{18,2},{3,19},{19,3},{4,20},{20... | collective-permute-start | bytes 7077896 | tf_op jit(solution)/shard_map/ppermute | solution.py:661
  228.6 64.3 %all-to-all-start.3 = ((bf16[16,40,768]{2,1,0:T(8,128)(2,1)}), bf16[16,40,768]{2,1,0:T(8,128)(2,1)S(1)}, u32[]{:S(2)}, u32[]{:S(2)}) async-start(bf16[16,40,768]{2,1,0:T(8,128)(2,1)} %bitcast.28), calls=%async_computation.3 | async-start | bytes 1966080 | tf_op jit(solution)/shard_map/all_to_all | solution.py:830
  296.8 9.1 %collective-permute-start.18 = (bf16[16,32,1536]{2,1,0:T(8,128)(2,1)}, bf16[16,32,1536]{2,1,0:T(8,128)(2,1)}, u32[]{:S(2)}, u32[]{:S(2)}) collective-permute-start(bf16[16,32,1536]{2,1,0:T(8,128)(2,1)} %pad_maximum_fusion.1), channel_id=1, source_target_pairs={{0,16},{16,0},{1,17},{17,1},{2,18},{18,2},{3,19},{19,3},{4,20},{20... | collective-permute-start | bytes 4718600 | tf_op jit(solution)/shard_map/ppermute | solution.py:661
  309.1 14.3 %copy-start.14 = (f32[512,1]{1,0:T(8,128)S(1)}, f32[512,1]{1,0:T(8,128)}, u32[]{:S(2)}) copy-start(f32[512,1]{1,0:T(8,128)} %get-tuple-element.108) | copy-start | bytes 6148
  309.1 14.5 %copy-start.10 = (f32[512,768]{1,0:T(8,128)S(1)}, f32[512,768]{1,0:T(8,128)}, u32[]{:S(2)}) copy-start(f32[512,768]{1,0:T(8,128)} %get-tuple-element.107.h1_ref) | copy-start | bytes 4718596
  309.1 53.1 %all-to-all-start.4 = ((bf16[16,32,1536]{2,1,0:T(8,128)(2,1)}), bf16[16,32,1536]{2,1,0:T(8,128)(2,1)S(1)}, u32[]{:S(2)}, u32[]{:S(2)}) async-start(bf16[16,32,1536]{2,1,0:T(8,128)(2,1)} %fusion), calls=%async_computation.4 | async-start | bytes 3145728 | tf_op jit(solution)/shard_map/all_to_all | solution.py:733
  (19 other events, 97.0 us)
Sparse Core Ops, SparseCore 0:
  11.5 74.8 all-gather.2
  228.7 112.2 reduce-scatter.1
where the time goes:
time: 377 us; the launch traced here: 376 us
  Pallas kernels  143 us (38%)
  waiting for transfers between devices  81.6 us (22%)
  starting transfers between devices  66.3 us (18%)
  other arithmetic  32 us (8%)
  local copies, waits for them, and re-layouts  28.2 us (7%)
  between operations  14.9 us (4%)
  matrix products  9.52 us (3%)
    pallas_call x1, Pallas kernels, mixer_backward(): pl.pallas_call(functools.partial(backward_kernel, group=group, rank=rank,...  55.5 us
    ppermute x19, waiting for transfers between devices, swap(): return lax.ppermute(values, axis, [(i, i ^ mask) for i in range(count)])  25.1 us
    ppermute x19, starting transfers between devices, swap(): return lax.ppermute(values, axis, [(i, i ^ mask) for i in range(count)])  24.6 us
    pallas_call x1, Pallas kernels, mixer_forward(): pl.pallas_call(functools.partial(forward_kernel, group=group, rank=rank,...  23.9 us
    pallas_call x1, Pallas kernels, expert_pass(): pl.pallas_call(functools.partial(expert_kernel, parts=parts), grid=(hidde...  22.8 us
    all_to_all x2, waiting for transfers between devices, to_experts(): lax.all_to_all(values.reshape(experts, slots, -1), 'fsdp', 0, 0, tiled=True)  21.8 us
    all_to_all x1, waiting for transfers between devices, scatter_end(): lax.all_to_all(parts, 'fsdp', 0, 0, tiled=True).astype(F32)  18.9 us
    pallas_call x1, Pallas kernels, home_backward(): pl.pallas_call(home_backward_kernel, grid_spec=pltpu.PrefetchScalarGridSp...  17.6 us
  transfers between devices with their start and end apart: 26, of which 13 were waited for; matrix products, arithmetic and copies ran while one was open for 16% of the time, Pallas kernels for 32%

commit v1 on v0

--- a/solution.py
+++ b/solution.py
@@ -93,6 +93,10 @@
     for shift in range(taps):
         total = total + vec_ref[taps - 1 - shift : taps - shift, lanes] * x_ref[ROWS - shift : ROWS - shift + steps, lanes]
     return total
+
+
+def lane_halves(small):
+    return [pl.BlockSpec((small.shape[0], LANES), lambda p, lens, half=half: (0, half)) for half in range(2)]
 
 
 def forward_kernel(len_ref, u_ref, wx_ref, sela_ref, stepb_ref, vec_ref, a_ref,
@@ -169,7 +173,7 @@
     lax.fori_loop(used, steps // ROWS, clear, 0)
 
 
-def mixer_forward(sample, u, wx, sela, stepb, vec, a2, packs, rank, taps, group=12):
+def mixer_forward(sample, u, wx, small, vec, a2, packs, rank, taps, group=12):
     rows, model = u.shape
     steps = rows // packs
     states, width = a2.shape
@@ -181,7 +185,7 @@
         grid_spec=pltpu.PrefetchScalarGridSpec(
             num_scalar_prefetch=1,
             grid=(packs,),
-            in_specs=[pl.BlockSpec((steps, model), per_pack), whole(wx), whole(sela), whole(stepb), whole(vec), whole(a2)],
+            in_specs=[pl.BlockSpec((steps, model), per_pack), whole(wx), *lane_halves(small), whole(vec), whole(a2)],
             out_specs=[
                 pl.BlockSpec((steps + ROWS, width), per_pack),
                 mats,
@@ -208,13 +212,25 @@
         compiler_params=pltpu.CompilerParams(vmem_limit_bytes=56 << 20),
         cost_estimate=pl.CostEstimate(flops=0, bytes_accessed=120_000_000, transcendentals=0),
         name="mixer_forward",
-    )(sample, u, wx, sela, stepb, vec, a2)
+    )(sample, u, wx, small, small, vec, a2)
+
+
+def step_slopes(d):
+    small = d < 0.01
+    slope = 1.0 - d * (0.5 - d * (1.0 / 6.0))
+    rise = 1.0 - jnp.exp(-d)
+    return jnp.where(small, d * slope, rise), jnp.where(small, slope, rise / jnp.where(small, 1.0, d))
 
 
 def backward_kernel(len_ref, delta_ref, xs_ref, bx_ref, gm_ref, sel_ref, sela_ref, stepb_ref, vec_ref, a_ref, h_ref,
-                    wx_ref, x_ref, gain_ref, gu_ref, gh_ref,
-                    gx_ref, gsel_ref, gstep_ref, ggain_ref, gtok_ref,
-                    mu_s, bw, cw, gb, gc, gd, gxs, low, gvec_ref, ga_ref, *, group, rank, taps):
+                    wx_ref, x_ref, gain_ref, gu_ref, gh_ref, u_ref, extra_ref, second_ref, *refs,
+                    group, rank, taps, at_gain, own, groups):
+    if own:
+        outs, refs = refs[:groups], refs[groups:]
+        gtok_ref, gxw_ref, gsel_ref, gstep_ref, ggain_ref = refs[:5]
+    else:
+        gtok_ref, gxw_ref, gsel_ref, gstep_ref, ggain_ref = refs[:5]
+    mu_s, bw, cw, gb, gc, gd, gxs, low, gx_ref, gvec_ref, ga_ref, tile = refs[-12:]
     pack = pl.program_id(0)
     states, width = a_ref.shape
     steps = sel_ref.shape[0]
@@ -225,7 +241,8 @@
     def _():
         ga_ref[...] = jnp.zeros_like(ga_ref)
         gsel_ref[...] = jnp.zeros_like(gsel_ref)
-        gstep_ref[...] = jnp.zeros_like(gstep_ref)
+        gstep_ref[...] = extra_ref[...]
+        gxw_ref[...] = jnp.zeros_like(gxw_ref)
         gvec_ref[...] = jnp.zeros_like(gvec_ref)
         ggain_ref[...] = jnp.zeros_like(ggain_ref)
 
@@ -257,34 +274,38 @@
                 x = xs_ref[pl.ds(at, ROWS), lanes]
                 a = a_ref[:, lanes]
                 dx = d * x
-                h, decay = [h_ref[s, :, lanes]], []
+                tile[3 * u] = d
+                tile[3 * u + 1] = dx
+                tile[3 * u + 2] = gm_ref[pl.ds(at, ROWS), lanes]
+                h, power, decay = [h_ref[s, :, lanes]], [], []
                 for t in range(ROWS):
-                    decay.append(jnp.exp2(d[t : t + 1] * a))
-                    h.append(decay[t] * h[t] + bw[place[t], :] * dx[t : t + 1])
-                each.append(dict(lanes=lanes, d=d, x=x, gy=gm_ref[pl.ds(at, ROWS), lanes], dx=dx, a=a, mu=mu_s[:, lanes],
-                                 h=h, decay=decay, ga=ga_ref[:, lanes], sp=[None] * ROWS, gp=[None] * ROWS))
+                    power.append(tile[3 * u, t : t + 1, :] * a)
+                    decay.append(jnp.exp2(power[t]))
+                    h.append(decay[t] * h[t] + bw[place[t], :] * tile[3 * u + 1, t : t + 1, :])
+                each.append(dict(lanes=lanes, d=d, x=x, mu=mu_s[:, lanes], h=h, power=power, decay=decay,
+                                 ga=ga_ref[:, lanes], sp=[None] * ROWS, gp=[None] * ROWS))
             for t in range(ROWS - 1, -1, -1):
                 b, c = bw[place[t], :], cw[place[t], :]
                 one_b = one_c = None
-                for v in each:
-                    gyt = v["gy"][t : t + 1]
+                for u, v in enumerate(each):
+                    gyt = tile[3 * u + 2, t : t + 1, :]
                     lam = c * gyt + v["mu"]
                     v["sp"][t] = b * lam
-                    to_b = lam * v["dx"][t : t + 1]
+                    to_b = lam * tile[3 * u + 1, t : t + 1, :]
                     to_c = v["h"][t + 1] * gyt
                     one_b = to_b if one_b is None else one_b + to_b
                     one_c = to_c if one_c is None else one_c + to_c
                     v["mu"] = v["decay"][t] * lam
-                    q = v["mu"] * v["h"][t]
-                    v["gp"][t] = q * v["a"]
-                    v["ga"] = v["ga"] + q * v["d"][t : t + 1]
+                    v["gp"][t] = v["mu"] * v["h"][t] * v["power"][t]
+                    v["ga"] = v["ga"] + v["gp"][t]
                 gb[place[t], :] += one_b
                 gc[place[t], :] += one_c
             for v in each:
                 lanes = v["lanes"]
                 mu_s[:, lanes], ga_ref[:, lanes] = v["mu"], v["ga"]
                 total = sum_states(v["sp"])
-                gd[pl.ds(at, ROWS), lanes] = sum_states(v["gp"]) * LN2 + v["x"] * total
+                rise, slope = step_slopes(v["d"])
+                gd[pl.ds(at, ROWS), lanes] = sum_states(v["gp"]) * (slope * LN2) + v["x"] * total * rise
                 gxs[pl.ds(at, ROWS), lanes] = v["d"] * total
             return 0
 
@@ -298,9 +319,7 @@
 
     def sizes(k, _):
         lanes = lane_chunk(k)
-        d = delta_ref[:, lanes]
-        rise = jnp.where(d < 0.01, d * (1.0 - d * (0.5 - d * (1.0 / 6.0))), 1.0 - jnp.exp(-d))
-        grad = gd[:steps, lanes] * rise
+        grad = gd[:steps, lanes]
         add_row(bias_step, lanes, grad)
         low[:, lanes] = grad.astype(BF16)
         add_row(skip, lanes, gm_ref[:, lanes] * xs_ref[:, lanes])
@@ -336,24 +355,63 @@
     lax.fori_loop(0, chunks, values, 0, unroll=2)
     gsel_ref[...] += dot(low[...], grad_sel, ((0,), (0,)))
 
+    def product(k, _):
+        lanes = lane_chunk(k, 4)
+        gxw_ref[:, lanes] += dot(u_ref[...], gx_ref[:, lanes], ((0,), (0,)))
+        return 0
+
+    lax.fori_loop(0, chunks // 4, product, 0, unroll=True)
     hidden = x_ref[...].astype(F32)
     inv = lax.rsqrt(jnp.mean(hidden * hidden, axis=1, keepdims=True) + EPSILON)
     normed = hidden * inv
     grad_u = dot(gx_ref[...], wx_ref[...], ((1,), (1,))) + gu_ref[...]
     scaled = grad_u * gain_ref[...]
-    ggain_ref[...] += jnp.sum(grad_u * normed, axis=0, keepdims=True)
+    if own:
+        ones = jnp.ones((steps, LANES), BF16)
+        high, rest = split_low(grad_u * normed)
+        ggain_ref[...] += dot(high, ones, ((0,), (0,))) + dot(rest, ones, ((0,), (0,)))
+    else:
+        ggain_ref[...] += jnp.sum(grad_u * normed, axis=0, keepdims=True)
     gtok_ref[...] = gh_ref[...] + inv * (scaled - normed * jnp.mean(scaled * normed, axis=1, keepdims=True))
 
     @pl.when(pack == pl.num_programs(0) - 1)
     def _():
-        rows_of_vectors = jnp.concatenate([gvec_ref[...], ga_ref[...] * a_ref[...] * LN2], axis=0)
+        rows_of_vectors = jnp.concatenate([gvec_ref[...], ga_ref[...] * LN2], axis=0)
         before = jnp.zeros((rank, width), F32)
         after = jnp.zeros((LANES - rank - rows_of_vectors.shape[0], width), F32)
         gstep_ref[...] += jnp.concatenate([before, rows_of_vectors, after], axis=0).T
-
-
-def mixer_backward(sample, delta, xs, bx, gm, sel, sela, stepb, vec, a2, hall, wx, tokens, gain, grad_u, grad_h,
-                   packs, rank, taps, group=2):
+        if own:
+            lane = lax.broadcasted_iota(jnp.int32, (own, LANES), 1)
+            folds = width // (2 * LANES)
+            run = 2 * own // folds
+
+            size = own + run
+            count = width // (2 * own) // groups
+
+            def gather(slot, f):
+                i = (len_ref[pl.num_programs(0)] ^ slot) * count + f
+                mine = pl.ds(pl.multiple_of(own * i, ROWS), own)
+                for part, ref in enumerate((ggain_ref, second_ref)):
+                    here = pl.ds(pl.multiple_of(2 * own * i + own * part, ROWS), own)
+                    gstep_ref[here, :] += jnp.where(lane == at_gain, ref[mine, :], 0.0)
+                parts = []
+                for j in range(folds):
+                    here = pl.ds(pl.multiple_of(2 * own * i + run * j, ROWS), run)
+                    parts += [gsel_ref[here, :], gstep_ref[here, :]]
+                block = jnp.concatenate([gxw_ref[mine, :], jnp.concatenate(parts, axis=1)], axis=0)
+                outs[slot][pl.ds(pl.multiple_of(size * f, size), size), :] = block.astype(BF16)
+                return 0
+
+            for slot in range(groups):
+                lax.fori_loop(0, count, lambda f, _, slot=slot: gather(slot, f), 0)
+
+
+def whole_tiles(own, width):
+    return own % ROWS == 0 and 4 * own * LANES % (ROWS * width) == 0
+
+
+def mixer_backward(sample, delta, xs, bx, gm, sel, small, vec, a2, hall, wx, tokens, gain, grad_u, grad_h, u, extra, second,
+                   packs, rank, taps, at_gain, own, groups, group=3):
     rows, width = delta.shape
     steps = rows // packs
     states, model = a2.shape[0], tokens.shape[1]
@@ -362,8 +420,34 @@
     whole = lambda v: pl.BlockSpec(v.shape, fixed)
     mats = pl.BlockSpec((steps, width), per_pack)
     toks = pl.BlockSpec((steps, model), per_pack)
+    own = own if whole_tiles(own, width) else 0
+    sums = [(model, width), (width, LANES), (width, LANES), (model, LANES) if own else (1, model)]
+    size = own + 4 * own * LANES // width
+    outs = [jax.ShapeDtypeStruct((rows, model), F32)]
+    out_specs = [toks]
+    scratch = [
+        pltpu.VMEM((states, width), F32),
+        pltpu.VMEM((steps * states, LANES), F32),
+        pltpu.VMEM((steps * states, LANES), F32),
+        pltpu.VMEM((steps * states, LANES), F32),
+        pltpu.VMEM((steps * states, LANES), F32),
+        pltpu.VMEM((steps + ROWS, width), F32),
+        pltpu.VMEM((steps, width), F32),
+        pltpu.VMEM((steps, width), BF16),
+        pltpu.VMEM((steps, width), BF16),
+        pltpu.VMEM((ROWS, width), F32),
+        pltpu.VMEM((states, width), F32),
+        pltpu.VMEM((3 * group, ROWS, LANES), F32),
+    ]
+    if own:
+        outs = [jax.ShapeDtypeStruct((model // own // groups * size, width), BF16)] * groups + outs
+        out_specs = [pl.BlockSpec(outs[0].shape, fixed)] * groups + out_specs
+        scratch = [pltpu.VMEM(shape, F32) for shape in sums] + scratch
+    else:
+        outs += [jax.ShapeDtypeStruct(shape, F32) for shape in sums]
+        out_specs += [pl.BlockSpec(shape, fixed) for shape in sums]
     return pl.pallas_call(
-        functools.partial(backward_kernel, group=group, rank=rank, taps=taps),
+        functools.partial(backward_kernel, group=group, rank=rank, taps=taps, at_gain=at_gain, own=own, groups=groups),
         grid_spec=pltpu.PrefetchScalarGridSpec(
             num_scalar_prefetch=1,
             grid=(packs,),
@@ -372,41 +456,18 @@
                 pl.BlockSpec((steps + ROWS, width), per_pack),
                 mats,
                 pl.BlockSpec((steps, LANES), per_pack),
-                whole(sela), whole(stepb), whole(vec), whole(a2),
+                *lane_halves(small), whole(vec), whole(a2),
                 pl.BlockSpec((steps // ROWS, states, width), lambda p, lens: (p, 0, 0)),
-                whole(wx), toks, whole(gain), toks, toks,
+                whole(wx), toks, whole(gain), toks, toks, toks, whole(extra), whole(second),
             ],
-            out_specs=[
-                mats,
-                pl.BlockSpec((width, LANES), fixed),
-                pl.BlockSpec((width, LANES), fixed),
-                pl.BlockSpec((1, model), fixed),
-                toks,
-            ],
-            scratch_shapes=[
-                pltpu.VMEM((states, width), F32),
-                pltpu.VMEM((steps * states, LANES), F32),
-                pltpu.VMEM((steps * states, LANES), F32),
-                pltpu.VMEM((steps * states, LANES), F32),
-                pltpu.VMEM((steps * states, LANES), F32),
-                pltpu.VMEM((steps + ROWS, width), F32),
-                pltpu.VMEM((steps, width), F32),
-                pltpu.VMEM((steps, width), BF16),
-                pltpu.VMEM((ROWS, width), F32),
-                pltpu.VMEM((states, width), F32),
-            ],
+            out_specs=out_specs,
+            scratch_shapes=scratch,
         ),
-        out_shape=[
-            jax.ShapeDtypeStruct((rows, width), BF16),
-            jax.ShapeDtypeStruct((width, LANES), F32),
-            jax.ShapeDtypeStruct((width, LANES), F32),
-            jax.ShapeDtypeStruct((1, model), F32),
-            jax.ShapeDtypeStruct((rows, model), F32),
-        ],
-        compiler_params=pltpu.CompilerParams(vmem_limit_bytes=60 << 20),
-        cost_estimate=pl.CostEstimate(flops=0, bytes_accessed=190_000_000, transcendentals=0),
+        out_shape=outs,
+        compiler_params=pltpu.CompilerParams(vmem_limit_bytes=62 << 20),
+        cost_estimate=pl.CostEstimate(flops=0, bytes_accessed=100_000, transcendentals=0),
         name="mixer_backward",
-    )(sample, delta, xs, bx, gm, sel, sela, stepb, vec, a2, hall, wx, tokens, gain, grad_u, grad_h)
+    )(sample, delta, xs, bx, gm, sel, small, small, vec, a2, hall, wx, tokens, gain, grad_u, grad_h, u, extra, second)
 
 
 def expert_kernel(*refs, parts):
@@ -431,9 +492,9 @@
 
     q, gr = q_ref[...], gr_ref[...]
     root = 0.7978845608028654
-    for k in range(parts):
-        pre = dot(q, ups[k][...])
-        grad_act = dot(gr, downs[k][...], ((1,), (1,)))
+    pres = [dot(q, up[...]) for up in ups]
+    grad_acts = [dot(gr, down[...], ((1,), (1,))) for down in downs]
+    for k, (pre, grad_act) in enumerate(zip(pres, grad_acts)):
         square = pre * pre
         t = jnp.tanh(root * pre * (1.0 + 0.044715 * square))
         half = 0.5 * (1.0 + t)
@@ -481,6 +542,21 @@
         name="expert_pass",
     )(q, gy, router, mine, *ups, *downs)
     return (*outs[:4], outs[4 : 4 + parts], outs[4 + parts :])
+def rows_from(ref, here):
+    if len(ref.shape) == 2:
+        return ref[here, :]
+    run = ref.shape[1]
+    return ref[here.start // run : here.stop // run].reshape(here.stop - here.start, ref.shape[2])
+
+
+def late_out(late, own):
+    devices, count, model = late.shape
+    if own % 16 == 0:
+        return late, pl.BlockSpec((devices, own, model), lambda p, lens: (0, 1, 0))
+    out = late[:, count - own :].reshape(devices * own, model)
+    return out, pl.BlockSpec(out.shape, lambda p, lens: (0, 0))
+
+
 def live_rows(length, steps):
     return (lax.broadcasted_iota(jnp.int32, (steps, 1), 0) < length).astype(F32)
 
@@ -501,7 +577,7 @@
         z_ref[:, here] = z
         gated = (mix_ref[:, here] * (z * jax.nn.sigmoid(z))).astype(BF16)
         gated_ref[:, here] = gated
-        mixed = mixed + dot(gated, wout_ref[here, :])
+        mixed = mixed + dot(gated, rows_from(wout_ref, here))
     h1 = x_ref[...].astype(F32) + live_rows(len_ref[pack], steps) * mixed
     h1_ref[...] = h1
     routed = (norm_of(h1)[0] * gain_ref[...]).astype(BF16)
@@ -524,7 +600,8 @@
         sent_ref[...] = total[...].astype(BF16)
 
 
-def home_forward(sample, u, wz, wout, mix, tokens, gain, router, hot, chooser):
+def home_forward(sample, u, wz, late, own, mix, tokens, gain, router, hot, chooser):
+    wout, wout_spec = late_out(late, own)
     packs = sample.shape[0]
     rows, model = u.shape
     steps, inner, slots = rows // packs, mix.shape[1], chooser.shape[0]
@@ -536,7 +613,7 @@
             num_scalar_prefetch=1,
             grid=(packs,),
             in_specs=[
-                part(model), whole(wz[0]), whole(wz[1]), whole(wout), part(inner), part(model), whole(gain), whole(router),
+                part(model), whole(wz[0]), whole(wz[1]), wout_spec, part(inner), part(model), whole(gain), whole(router),
                 part(hot.shape[1]), pl.BlockSpec((slots, steps), lambda p, lens: (0, p)),
             ],
             out_specs=[
@@ -558,7 +635,8 @@
 
 def home_backward_kernel(len_ref, choose_ref, back_ref, h1_ref, gy_ref, gain_ref, wout_ref, z_ref, mix_ref, u_ref, gated_ref,
                          wl_ref, wr_ref,
-                         gh_ref, gm_ref, gu_ref, ggain_ref, gwz_ref, gwout_ref, sum_z, sum_out):
+                         gh_ref, gm_ref, gu_ref, ggain_ref, *refs, own):
+    *outs, sum_z, sum_out = refs
     pack = pl.program_id(0)
     steps, model = u_ref.shape
 
@@ -571,14 +649,19 @@
     grad = dot(choose_ref[...], back_ref[...], ((0,), (0,)))
     normed, inv = norm_of(h1_ref[...])
     scaled = grad * gain_ref[...]
-    ggain_ref[...] += jnp.sum(grad * normed, axis=0, keepdims=True)
+    if len(outs) == 1:
+        ones = jnp.ones((steps, LANES), BF16)
+        high, rest = split_low(grad * normed)
+        ggain_ref[...] += dot(high, ones, ((0,), (0,))) + dot(rest, ones, ((0,), (0,)))
+    else:
+        ggain_ref[...] += jnp.sum(grad * normed, axis=0, keepdims=True)
     gh = gy_ref[...].astype(F32) + inv * (scaled - normed * jnp.mean(scaled * normed, axis=1, keepdims=True))
     gh_ref[...] = gh
     grad_mixed = (live_rows(len_ref[pack], steps) * gh).astype(BF16)
     grad_u = jnp.zeros((steps, model), F32)
     for half, w_ref in enumerate((wl_ref, wr_ref)):
         here = slice(half * model, (half + 1) * model)
-        grad_gated = dot(grad_mixed, wout_ref[here, :], ((1,), (1,)))
+        grad_gated = dot(grad_mixed, rows_from(wout_ref, here), ((1,), (1,)))
         z = z_ref[:, here]
         sig = jax.nn.sigmoid(z)
         gm_ref[:, here] = grad_gated * (z * sig)
@@ -590,29 +673,48 @@
 
     @pl.when(pack == pl.num_programs(0) - 1)
     def _():
-        gwz_ref[...] = sum_z[...].astype(BF16)
-        gwout_ref[...] = sum_out[...].astype(BF16)
-
-
-def home_backward(sample, chooser, back, h1, gy, gain, wout, z, mix, u, gated, wz):
+        if len(outs) == 2:
+            outs[0][...] = sum_z[...].astype(BF16)
+            outs[1][...] = sum_out[...].astype(BF16)
+            return
+
+        def gather(i, _):
+            mine = pl.ds(pl.multiple_of(own * i, ROWS), own)
+            left = pl.ds(pl.multiple_of(2 * own * i, ROWS), own)
+            right = pl.ds(pl.multiple_of(2 * own * i + own, ROWS), own)
+            block = jnp.concatenate(
+                [sum_z[mine, :], jnp.concatenate([sum_out[left, :], sum_out[right, :]], axis=1)], axis=0
+            )
+            outs[0][pl.ds(pl.multiple_of(2 * own * i, 2 * own), 2 * own), :] = block.astype(BF16)
+            return 0
+
+        lax.fori_loop(0, model // own, gather, 0)
+
+
+def home_backward(sample, chooser, back, h1, gy, gain, late, own, z, mix, u, gated, wz):
+    wout, wout_spec = late_out(late, own)
     packs = sample.shape[0]
     rows, model = u.shape
     steps, inner, slots = rows // packs, mix.shape[1], chooser.shape[0]
     fixed = lambda p, lens: (0, 0)
     whole = lambda v: pl.BlockSpec(v.shape, fixed)
     part = lambda n: pl.BlockSpec((steps, n), lambda p, lens: (p, 0))
+    shard = own // 2
+    packed = whole_tiles(shard, inner)
+    sums = [(inner, inner)] if packed else [(model, inner), (inner, model)]
+    gains = (model, LANES) if packed else (1, model)
     return pl.pallas_call(
-        home_backward_kernel,
+        functools.partial(home_backward_kernel, own=shard),
         grid_spec=pltpu.PrefetchScalarGridSpec(
             num_scalar_prefetch=1,
             grid=(packs,),
             in_specs=[
                 pl.BlockSpec((slots, steps), lambda p, lens: (0, p)), whole(back), part(model), part(model), whole(gain),
-                whole(wout), part(inner), part(inner), part(model), part(inner), whole(wz[0]), whole(wz[1]),
+                wout_spec, part(inner), part(inner), part(model), part(inner), whole(wz[0]), whole(wz[1]),
             ],
             out_specs=[
-                part(model), part(inner), part(model), whole(gain),
-                pl.BlockSpec((model, inner), fixed), pl.BlockSpec((inner, model), fixed),
+                part(model), part(inner), part(model), pl.BlockSpec(gains, fixed),
+                *[pl.BlockSpec(shape, fixed) for shape in sums],
             ],
             scratch_shapes=[pltpu.VMEM((model, inner), F32), pltpu.VMEM((inner, model), F32)],
         ),
@@ -620,9 +722,8 @@
             jax.ShapeDtypeStruct((rows, model), F32),
             jax.ShapeDtypeStruct((rows, inner), F32),
             jax.ShapeDtypeStruct((rows, model), F32),
-            jax.ShapeDtypeStruct((1, model), F32),
-            jax.ShapeDtypeStruct((model, inner), BF16),
-            jax.ShapeDtypeStruct((inner, model), BF16),
+            jax.ShapeDtypeStruct(gains, F32),
+            *[jax.ShapeDtypeStruct(shape, BF16) for shape in sums],
         ],
         compiler_params=pltpu.CompilerParams(vmem_limit_bytes=60 << 20),
         cost_estimate=pl.CostEstimate(flops=0, bytes_accessed=100_000, transcendentals=0),
@@ -668,12 +769,19 @@
 
 
 def gather_stages(width):
-    bits = lax.axis_size("fsdp").bit_length() - 1
+    count = lax.axis_size("fsdp")
+    bits = count.bit_length() - 1
     place = lambda bit: bits - 1 - bit
     half = width // 2
 
-    def single(bit):
-        return lambda values: grow(values, "fsdp", 1 << bit, place(bit))
+    def upper(values):
+        shape = values.shape
+        every = jnp.stack([values] + [swap(values, "fsdp", mask) for mask in range(4, count, 4)])
+        every = every.reshape((2,) * (bits - 2) + shape)
+        for bit in range(2, bits):
+            flipped = (lax.axis_index("fsdp") & (1 << bit)) != 0
+            every = jnp.where(flipped, jnp.flip(every, place(bit)), every)
+        return every.reshape((2,) * (bits - 2) + (1, 1) + shape)
 
     def split(values):
         return grow(values[..., :half], "fsdp", 2, place(1)), grow(values[..., half:], "fsdp", 1, place(0))
@@ -686,22 +794,21 @@
         return lambda values: grow(values.reshape(1, -1, width), "dp", mask, 0)
 
     masks = [1 << i for i in range(lax.axis_size("dp").bit_length() - 1)]
-    return [single(bit) for bit in range(2, bits)] + [split, join] + [across(mask) for mask in masks]
-
-
-def gather_both(early, late, lag, beside):
-    bits = lax.axis_size("fsdp").bit_length() - 1
-    shapes = [(-1, v.shape[1]) for v in (early, late)]
-    values = [v.reshape((1,) * bits + v.shape) for v in (early, late)]
-    stages = [gather_stages(v.shape[1]) for v in (early, late)]
-    count = len(stages[0])
-    for at in range(count + lag):
-        if lag <= at:
+    return [upper, split, join] + [across(mask) for mask in masks]
+
+
+def gather_both(first, second, beside):
+    shapes = [(-1, v.shape[1]) for v in (first, second)]
+    values = [first, second]
+    steps = [gather_stages(v.shape[1]) for v in values]
+    count = len(steps[0])
+    for at in range(count + 1):
+        if at:
             *values, beside = lax.optimization_barrier((*values, beside))
         if at < count:
-            values[0] = stages[0][at](values[0])
-        if at >= lag:
-            values[1] = stages[1][at - lag](values[1])
+            values[0] = steps[0][at](values[0])
+        if at:
+            values[1] = steps[1][at - 1](values[1])
     return [v.reshape(shape) for v, shape in zip(values, shapes)] + [beside]
 
 
@@ -720,10 +827,9 @@
     return lax.dynamic_slice_in_dim(values, index * size, size, axis)
 
 
-def scatter_begin(piece):
-    me, groups = lax.axis_index("dp"), lax.axis_size("dp")
-    sent = [swap(piece(me ^ k).astype(BF16), "dp", k) for k in range(1, groups)]
-    total = piece(me).astype(F32)
+def scatter_begin(pieces):
+    sent = [swap(piece.astype(BF16), "dp", k + 1) for k, piece in enumerate(pieces[1:])]
+    total = pieces[0].astype(F32)
     for got in sent:
         total = total + got.astype(F32)
     return total.astype(BF16)
@@ -731,11 +837,6 @@
 
 def scatter_end(parts):
     return jnp.sum(lax.all_to_all(parts, "fsdp", 0, 0, tiled=True).astype(F32), axis=0)
-
-
-def rows_of(left, right, i):
-    product = dot(own_block(left, i, lax.axis_size("dp"), 1), right, ((0,), (0,)))
-    return product.reshape(lax.axis_size("fsdp"), -1, product.shape[1])
 
 
 def body(
@@ -771,6 +872,13 @@
     taps = conv_weight.shape[1]
     own_model, own_inner = norm1_gain.shape[0], conv_bias.shape[0]
 
+    packed = whole_tiles(own_model, inner)
+
+    def gains_in(first, second):
+        pair = [v.reshape(devices, 1, own_model) for v in (first, second)]
+        column = jnp.concatenate(pair, axis=1).reshape(inner, 1)
+        return jnp.where(jnp.arange(LANES) == rank + taps + 3, column, 0.0)
+
     half = experts // 2
     vectors = jnp.concatenate(
         [
@@ -796,7 +904,6 @@
     late = jnp.concatenate([input_weight[:, inner : inner + model], input_weight[:, inner + model :], out_weight], axis=0)
     late = lax.all_gather(late, ("dp", "fsdp"), axis=0, tiled=False)
     input_z = [late[:, i * own_model : (i + 1) * own_model].reshape(model, model) for i in range(2)]
-    output_full = late[:, 2 * own_model :].reshape(inner, model)
     ups = [expert_up[0]] + [swap(expert_up[0], "dp", k) for k in range(1, groups)]
     downs = [expert_down[0]] + [swap(expert_down[0], "dp", k) for k in range(1, groups)]
 
@@ -835,11 +942,10 @@
     inv_first = lax.rsqrt(jnp.mean(hidden * hidden, axis=-1, keepdims=True) + EPSILON)
     normed_first = hidden * inv_first
     input_x, small_full, upstream_rows = gather_both(
-        input_weight[:, :inner], small, 1, dot(chooser, cotangent).astype(BF16)
+        input_weight[:, :inner], small, dot(chooser, cotangent).astype(BF16)
     )
     upstream_sent = to_experts(upstream_rows)
-    select_full, step_full = small_full[:, :LANES], small_full[:, LANES:]
-    vectors_full = step_full[:, rank:].T
+    vectors_full = small_full[:, LANES + rank :].T
     vectors_first = vectors_full[:ROWS].astype(F32)
     decay_full = vectors_full[taps + 4 : taps + 4 + states].astype(F32)
     gains = vectors_full[taps + 3].reshape(devices, 2, own_model)
@@ -852,12 +958,12 @@
     decay_mat = -jnp.exp(decay_full)
     decay_two = decay_mat * LOG2E
     branch_x, scan_in, step_size, selected, mixer_out, states_kept = mixer_forward(
-        sample, normed_low, input_x, select_full, step_full, vectors_first, decay_two, micro, rank, taps
+        sample, normed_low, input_x, small_full, vectors_first, decay_two, micro, rank, taps
     )
     mixer_out, upstream_sent = lax.optimization_barrier((mixer_out, upstream_sent))
     kept_hot = route_hot.reshape(rows, experts).astype(F32) * kept[:, None]
     branch_z, gated_low, residual, weight_row, sent = home_forward(
-        sample, normed_low, input_z, output_full, mixer_out, tokens.reshape(rows, model), gain_two[None, :], router_full,
+        sample, normed_low, input_z, late, own_inner, mixer_out, tokens.reshape(rows, model), gain_two[None, :], router_full,
         kept_hot, chooser,
     )
     received = to_experts(sent)
@@ -869,49 +975,49 @@
     grad_rows, result, received, flat_grad = lax.optimization_barrier((grad_rows, result, received, flat_grad))
     grad_back = back_home(grad_rows)
     matrix_grads = expert_grads(received, flat_grad, grad_pres, acts)
-    grad_back, matrix_grads = lax.optimization_barrier((grad_back, matrix_grads))
+    at_gain, at_decay, at_router = rank + taps + 3, rank + taps + 4, rank + taps + 4 + states
+    lane = jnp.arange(LANES)
+    router_grads = router_grad.reshape(2, half, devices, own_model).transpose(2, 0, 3, 1).reshape(inner, half)
+    extra = jnp.pad(router_grads, ((0, 0), (at_router, LANES - at_router - half)))
+    gain_row = gain_one[None, :]
+    grad_back, matrix_grads, extra, gain_row, result = lax.optimization_barrier(
+        (grad_back, matrix_grads, extra, gain_row, result)
+    )
+    result = back_home(result)
     up_own, down_own, *others = matrix_grads
     others = [swap(other, "dp", k // 2 + 1) for k, other in enumerate(others)]
 
-    grad_residual, grad_mixer, grad_normed_z, gain_two_grad, input_z_grad, output_grad = home_backward(
-        sample, chooser, grad_back.reshape(experts * slots, model), residual, cotangent, gain_two[None, :], output_full,
-        branch_z, mixer_out, normed_low, gated_low, input_z,
-    )
-    late_terms = jnp.concatenate(
-        [
-            input_z_grad.reshape(devices, own_model, inner),
-            fold(output_grad.reshape(devices, own_inner, model), 2),
-        ],
-        axis=1,
-    ).reshape(-1, inner)
-    late_grads = lax.psum_scatter(late_terms, ("dp", "fsdp"), scatter_dimension=0, tiled=True)
-    grad_mixer, result, others = lax.optimization_barrier((grad_mixer, result, others))
-    result = back_home(result)
-    grad_x, select_grad, step_grad, gain_one_grad, tokens_grad = mixer_backward(
-        sample, step_size, scan_in, branch_x, grad_mixer, selected, select_full, step_full, vectors_first, decay_two,
-        states_kept, input_x, tokens.reshape(rows, model), gain_one[None, :], grad_normed_z, grad_residual,
-        micro, rank, taps,
-    )
-    grad_x, result = lax.optimization_barrier((grad_x, result))
-
-    gain_grads = jnp.concatenate(
-        [gain_one_grad.reshape(devices, 1, own_model), gain_two_grad.reshape(devices, 1, own_model)], axis=1
-    ).reshape(inner, 1)
-    router_grads = (
-        router_grad.reshape(2, half, devices, own_model).transpose(2, 0, 3, 1).reshape(inner, half)
-    )
-    at_gain, at_decay, at_router = rank + taps + 3, rank + taps + 4, rank + taps + 4 + states
-    lane = jnp.arange(LANES)
-    step_grad = jnp.where(lane == at_gain, gain_grads, step_grad) + jnp.pad(
-        router_grads, ((0, 0), (at_router, LANES - at_router - half))
-    )
-
-    def early_terms(i):
-        blocks = [own_block(v, i, groups, 0).reshape(experts, own_inner, LANES) for v in (select_grad, step_grad)]
-        return jnp.concatenate([rows_of(normed_low, grad_x, i), fold(jnp.concatenate(blocks, axis=2), folds)], axis=1)
-
-    early_parts, others, result = lax.optimization_barrier((scatter_begin(early_terms), others, result))
-    early_grads = scatter_end(early_parts)
+    grad_residual, grad_mixer, grad_normed_z, gain_two_grad, *late_terms = home_backward(
+        sample, chooser, grad_back.reshape(experts * slots, model), residual, cotangent, gain_two[None, :], late,
+        own_inner, branch_z, mixer_out, normed_low, gated_low, input_z,
+    )
+    if not packed:
+        blocks = [v.reshape(devices, -1, v.shape[1]) for v in late_terms]
+        late_terms = [jnp.concatenate([blocks[0], fold(blocks[1], 2)], axis=1).reshape(-1, inner)]
+    late_grads = lax.psum_scatter(late_terms[0], ("dp", "fsdp"), scatter_dimension=0, tiled=True)
+    if not packed:
+        extra = extra + gains_in(jnp.zeros_like(gain_two_grad), gain_two_grad)
+    grad_mixer, others = lax.optimization_barrier((grad_mixer, others))
+    mixer_grads = mixer_backward(
+        jnp.append(sample, lax.axis_index("dp")), step_size, scan_in, branch_x, grad_mixer, selected, small_full, vectors_first, decay_two,
+        states_kept, input_x, tokens.reshape(rows, model), gain_row, grad_normed_z, grad_residual, normed_low, extra,
+        gain_two_grad, micro, rank, taps, at_gain, own_model, groups,
+    )
+    if packed:
+        *early_terms, tokens_grad = mixer_grads
+        early_terms = [terms.reshape(experts, -1, inner) for terms in early_terms]
+    else:
+        tokens_grad, input_x_grad, select_grad, step_grad, gain_one_grad = mixer_grads
+        step_grad = step_grad + gains_in(gain_one_grad, jnp.zeros_like(gain_one_grad))
+        blocks = jnp.concatenate([select_grad, step_grad], axis=1).reshape(devices, own_inner, 2 * LANES)
+        blocks = jnp.concatenate([input_x_grad.reshape(devices, own_model, inner), fold(blocks, folds)], axis=1)
+        blocks = blocks.reshape(groups, experts, -1, inner)
+        me = lax.axis_index("dp")
+        early_terms = [lax.dynamic_index_in_dim(blocks, me ^ k, 0, False) for k in range(groups)]
+    early_terms, result = lax.optimization_barrier((early_terms, result))
+    early_terms = scatter_begin(early_terms)
+    early_terms, others, result = lax.optimization_barrier((early_terms, others, result))
+    early_grads = scatter_end(early_terms)
     up_grad, down_grad = up_own.astype(F32), down_own.astype(F32)
     for k in range(groups - 1):
         up_grad = up_grad + others[2 * k].astype(F32)

time: 377 us -> 355 us (0.942)
  starting transfers between devices: 66.3 us -> 53.6 us
  Pallas kernels: 143 us -> 152 us
  other arithmetic: 32 us -> 25.5 us
  local copies, waits for them, and re-layouts: 28.2 us -> 21.8 us
    reduce_scatter x1, waiting for transfers between devices: 5.13 us -> 24.7 us  [body(): lax.psum_scatter(late_terms[0], ('dp', 'fsdp'), scatter_dimension=0, tile...]
    all_to_all x1, waiting for transfers between devices: 18.9 us -> 0.67 us  [scatter_end(): lax.all_to_all(parts, 'fsdp', 0, 0, tiled=True).astype(F32)]
    pallas_call x1, Pallas kernels: 55.5 us -> 64 us  [mixer_backward(): pl.pallas_call(functools.partial(backward_kernel, group=group, rank=rank,...]
    ppermute x19 -> x21, waiting for transfers between devices: 25.1 us -> 17.7 us  [swap(): return lax.ppermute(values, axis, [(i, i ^ mask) for i in range(count)])]
    ppermute x19 -> x21, starting transfers between devices: 24.6 us -> 18 us  [swap(): return lax.ppermute(values, axis, [(i, i ^ mask) for i in range(count)])]
    slice x4 -> x1, local copies, waits for them, and re-layouts: 6.67 us -> 0.17 us  [body(): vectors_full = small_full[:, LANES + rank:].T]
    all_to_all x2, waiting for transfers between devices: 21.8 us -> 26.8 us  [to_experts(): lax.all_to_all(values.reshape(experts, slots, -1), 'fsdp', 0, 0, tiled=True)]
    dot_general x4 -> x2, matrix products: 9.32 us -> 5.95 us  [dot(): lax.dot_general(left, right, (dims, ((), ())), preferred_element_type=F32)]
  transfers between devices with their start and end apart: 26 -> 28, of which waited for: 13 -> 14; matrix products, arithmetic and copies ran while one was open for 16% -> 13% of each run, Pallas kernels for 32% -> 37%
where the time goes in v1:
time: 355 us; the launch traced here: 352 us
  Pallas kernels  152 us (43%)
  waiting for transfers between devices  78.3 us (22%)
  starting transfers between devices  53.6 us (15%)
  other arithmetic  25.5 us (7%)
  local copies, waits for them, and re-layouts  21.8 us (6%)
  between operations  14.7 us (4%)
  matrix products  6.15 us (2%)
    pallas_call x1, Pallas kernels, mixer_backward(): pl.pallas_call(functools.partial(backward_kernel, group=group, rank=rank,...  64 us
    all_to_all x2, waiting for transfers between devices, to_experts(): lax.all_to_all(values.reshape(experts, slots, -1), 'fsdp', 0, 0, tiled=True)  26.8 us
    pallas_call x1, Pallas kernels, mixer_forward(): pl.pallas_call(functools.partial(forward_kernel, group=group, rank=rank,...  26.5 us
    reduce_scatter x1, waiting for transfers between devices, body(): lax.psum_scatter(late_terms[0], ('dp', 'fsdp'), scatter_dimension=0, tile...  24.7 us
    pallas_call x1, Pallas kernels, expert_pass(): pl.pallas_call(functools.partial(expert_kernel, parts=parts), grid=(hidde...  21 us
    ppermute x21, starting transfers between devices, swap(): return lax.ppermute(values, axis, [(i, i ^ mask) for i in range(count)])  18 us
    ppermute x21, waiting for transfers between devices, swap(): return lax.ppermute(values, axis, [(i, i ^ mask) for i in range(count)])  17.7 us
    pallas_call x1, Pallas kernels, home_backward(): pl.pallas_call(functools.partial(home_backward_kernel, own=shard), grid_s...  17.2 us
  transfers between devices with their start and end apart: 28, of which 14 were waited for; matrix products, arithmetic and copies ran while one was open for 13% of the time, Pallas kernels for 37%

profile of v1, /device:TPU:8, one launch (start us, length us, event | category | flops | bytes accessed | tf_op | source)
XLA Modules:
  0.0 351.6 jit_solution(5047333447279787011)
XLA Ops:
  8.2 2.7 collective-permute-start.1
  12.6 1.6 pad_maximum_fusion.6
  18.4 2.8 convolution_convert_fusion
  21.9 1.6 collective-permute-start.7
  23.5 2.0 collective-permute-start.6
  26.9 1.6 collective-permute-start.4
  30.1 2.0 collective-permute-done.4
  34.4 1.5 collective-permute-start.10
  39.1 3.5 collective-permute-done.8
  47.1 3.2 collective-permute-done.13
  51.8 1.6 pad_maximum_fusion
  54.5 7.8 %all-to-all-start = ((bf16[16,40,768]{2,1,0:T(8,128)(2,1)}), bf16[16,40,768]{2,1,0:T(8,128)(2,1)S(1)}, u32[]{:S(2)}, u32[]{:S(2)}) async-start(bf16[16,40,768]{2,1,0:T(8,128)(2,1)} %bitcast.104), calls=%async_computation | async-start | bytes 1966080 | tf_op jit(solution)/shard_map/all_to_all | solution.py:931
  67.3 26.5 %mixer_forward.1 = (f32[528,1536]{1,0:T(8,128)}, f32[512,1536]{1,0:T(8,128)}, f32[512,1536]{1,0:T(8,128)}, f32[512,128]{1,0:T(8,128)}, f32[512,1536]{1,0:T(8,128)}, /*index=5*/f32[64,16,1536]{2,1,0:T(8,128)}) custom-call(s32[2]{0:T(128)} %copy-done.14, bf16[512,768]{1,0:T(8,128)(2,1)} %multiply_convert_fusion.u_ref, bf16[768,1536]{1,0:T(8,128)(2,1)} %bitcast.84, ...), custom_call_target="tpu_custom_call" | custom-call | bytes 120000000 | tf_op jit(solution)/shard_map/mixer_forward/pallas_call | solution.py:183
  93.8 3.2 all-to-all-done
  96.9 3.5 %fusion.25 = (bf16[32,24,768]{2,1,0:T(8,128)(2,1)}, bf16[32,24,768]{2,1,0:T(8,128)(2,1)}) fusion(bf16[32,96,768]{2,1,0:T(8,128)(2,1)} %bitcast.76), kind=kLoop, calls=%fused_computation.108 | loop fusion | bytes 4718592 | tf_op jit(solution)/shard_map/slice | solution.py:906
  100.5 11.0 %home_forward.1 = (f32[512,1536]{1,0:T(8,128)}, bf16[512,1536]{1,0:T(8,128)(2,1)}, f32[512,768]{1,0:T(8,128)}, f32[512,1]{1,0:T(8,128)}, bf16[640,768]{1,0:T(8,128)(2,1)}) custom-call(s32[2]{0:T(128)} %copy-done.14, bf16[512,768]{1,0:T(8,128)(2,1)} %multiply_convert_fusion.u_ref, bf16[768,768]{1,0:T(8,128)(2,1)} %bitcast.90, bf16[768,768]{1,0:T(8,128)(2,1)} %bitcast.88, ...), custom_call_target="tpu_custom_call" | custom-call | tf_op jit(solution)/shard_map/home_forward/pallas_call | solution.py:610
  111.5 6.1 %all-to-all-start.1 = ((bf16[16,40,768]{2,1,0:T(8,128)(2,1)}), bf16[16,40,768]{2,1,0:T(8,128)(2,1)S(1)}, u32[]{:S(2)}, u32[]{:S(2)}) async-start(bf16[16,40,768]{2,1,0:T(8,128)(2,1)} %bitcast.107), calls=%async_computation.1 | async-start | bytes 1966080 | tf_op jit(solution)/shard_map/all_to_all | solution.py:931
  118.1 23.7 %all-to-all-done.1 = bf16[16,40,768]{2,1,0:T(8,128)(2,1)S(1)} async-done(((bf16[16,40,768]{2,1,0:T(8,128)(2,1)}), bf16[16,40,768]{2,1,0:T(8,128)(2,1)S(1)}, u32[]{:S(2)}, u32[]{:S(2)}) %all-to-all-start.1) | async-done | bytes 983072 | tf_op jit(solution)/shard_map/all_to_all | solution.py:931
  142.7 21.0 %expert_pass.1 = (bf16[640,768]{1,0:T(8,128)(2,1)}, bf16[640,768]{1,0:T(8,128)(2,1)}, bf16[640,768]{1,0:T(8,128)(2,1)}, f32[16,768]{1,0:T(8,128)}, bf16[640,1536...) custom-call(bf16[640,768]{1,0:T(8,128)(2,1)} %bitcast.92, ...), custom_call_target="tpu_custom_call" | custom-call | bytes 70000000 | tf_op jit(solution)/shard_map/expert_pass/pallas_call | solution.py:529
  163.8 5.0 %all-to-all-start.2 = ((bf16[16,40,768]{2,1,0:T(8,128)(2,1)}), bf16[16,40,768]{2,1,0:T(8,128)(2,1)S(1)}, u32[]{:S(2)}, u32[]{:S(2)}) async-start(bf16[16,40,768]{2,1,0:T(8,128)(2,1)} %bitcast.106), calls=%async_computation.2 | async-start | bytes 1966080 | tf_op jit(solution)/shard_map/all_to_all | solution.py:937
  171.1 11.9 %expert_grads.1 = (bf16[768,1536]{1,0:T(8,128)(2,1)}, bf16[1536,768]{1,0:T(8,128)(2,1)}, bf16[768,1536]{1,0:T(8,128)(2,1)}, bf16[1536,768]{1,0:T(8,128)(2,1)}) custom-call(bf16[640,768]{1,0:T(8,128)(2,1)} %bitcast.93, bf16[640,768]{1,0:T(8,128)(2,1)} %get-tuple-element.113.gr_ref, bf16[640,1536]{1,0:T(8,128)(2,1)} %get-tuple-element.114.refs_0_, ...), custom_call_target="tpu_custom_call" | custom-call | bytes 100000 | tf_op jit(solution)/shard_map/expert_grads/pallas_call | solution.py:748
  183.0 8.4 %all-to-all-done.2 = bf16[16,40,768]{2,1,0:T(8,128)(2,1)S(1)} async-done(((bf16[16,40,768]{2,1,0:T(8,128)(2,1)}), bf16[16,40,768]{2,1,0:T(8,128)(2,1)S(1)}, u32[]{:S(2)}, u32[]{:S(2)}) %all-to-all-start.2) | async-done | bytes 983072 | tf_op jit(solution)/shard_map/all_to_all | solution.py:937
  191.9 4.9 %all-to-all-start.3 = ((bf16[16,40,768]{2,1,0:T(8,128)(2,1)}), bf16[16,40,768]{2,1,0:T(8,128)(2,1)S(1)}, u32[]{:S(2)}, u32[]{:S(2)}) async-start(bf16[16,40,768]{2,1,0:T(8,128)(2,1)} %bitcast.42), calls=%async_computation.3 | async-start | bytes 1966080 | tf_op jit(solution)/shard_map/all_to_all | solution.py:937
  196.9 17.2 %home_backward.1 = (f32[512,768]{1,0:T(8,128)}, f32[512,1536]{1,0:T(8,128)}, f32[512,768]{1,0:T(8,128)}, f32[768,128]{1,0:T(8,128)}, bf16[1536,1536]{1,0:T(8,128)(2,1)}) custom-call(s32[2]{0:T(128)} %copy-done.14, bf16[640,512]{1,0:T(8,128)(2,1)} %fusion.2.choose_ref, bf16[640,768]{1,0:T(8,128)(2,1)} %bitcast.97, f32[512,768]{1,0:T(8,128)} %get-tuple-element.101.h1_ref, ...), custom_call_target="tpu_custom_call" | custom-call | bytes 100000 | tf_op jit(solution)/shard_map/home_backward/pallas_call | solution.py:706
  215.4 64.0 %mixer_backward.1 = (bf16[512,1536]{1,0:T(8,128)(2,1)}, bf16[512,1536]{1,0:T(8,128)(2,1)}, f32[512,768]{1,0:T(8,128)}) custom-call(s32[3]{0:T(128)} %pad_add_fusion.len_ref, f32[512,1536]{1,0:T(8,128)} %get-tuple-element.103.delta_ref, f32[512,1536]{1,0:T(8,128)} %get-tuple-element.104.xs_ref, f32[528,1536]{1,0:T(8,128)} %get-tuple-element.105.bx_ref, ...), custom_call_target="tpu_custom_call" | custom-call | bytes 100000 | tf_op jit(solution)/shard_map/mixer_backward/pallas_call | solution.py:449
  279.5 3.6 %collective-permute-done.20 = bf16[16,32,1536]{2,1,0:T(8,128)(2,1)S(1)} collective-permute-done((bf16[16,32,1536]{2,1,0:T(8,128)(2,1)}, bf16[16,32,1536]{2,1,0:T(8,128)(2,1)S(1)}, u32[]{:S(2)}, u32[]{:S(2)}) %collective-permute-start.20) | collective-permute-done | bytes 1572896 | tf_op jit(solution)/shard_map/ppermute | solution.py:762
  283.1 3.0 add_convert_fusion
  286.1 11.7 %all-to-all-start.4 = ((bf16[16,32,1536]{2,1,0:T(8,128)(2,1)}), bf16[16,32,1536]{2,1,0:T(8,128)(2,1)S(1)}, u32[]{:S(2)}, u32[]{:S(2)}) async-start(bf16[16,32,1536]{2,1,0:T(8,128)(2,1)} %add_convert_fusion), calls=%async_computation.4 | async-start | bytes 3145728 | tf_op jit(solution)/shard_map/all_to_all | solution.py:839
  298.0 3.1 add_convert_fusion.1
  301.2 4.7 %add_bitcast_fusion.1 = f32[1,768,1536]{2,1,0:T(8,128)} fusion(bf16[768,1536]{1,0:T(8,128)(2,1)} %collective-permute-done.18, bf16[768,1536]{1,0:T(8,128)(2,1)S(1)} %copy-done.6), kind=kLoop, calls=%fused_computation.1 | loop fusion | flops 3538944 | bytes 9437184 | tf_op jit(solution)/shard_map/broadcast_in_dim | solution.py:1045
  305.9 4.4 %add_bitcast_fusion = f32[1,1536,768]{2,1,0:T(8,128)} fusion(bf16[1536,768]{1,0:T(8,128)(2,1)} %collective-permute-done.19, bf16[1536,768]{1,0:T(8,128)(2,1)S(1)} %copy-done.5), kind=kLoop, calls=%fused_computation | loop fusion | flops 3538944 | bytes 9437184 | tf_op jit(solution)/shard_map/broadcast_in_dim | solution.py:1046
  310.2 24.7 %reduce-scatter.2.cloned.1.call-done = bf16[48,1536]{1,0:T(8,128)(2,1)} async-done(((bf16[1536,1536]{1,0:T(8,128)(2,1)}), bf16[48,1536]{1,0:T(8,128)(2,1)}) %reduce-scatter.2.cloned.1.call-update) | async-done | bytes 147472 | tf_op jit(solution)/shard_map/reduce_scatter | solution.py:997
  (183 shorter events, 43.4 us)
Async XLA Ops:
  7.2 89.8 %all-gather.3.cloned.1.call-start = ((), (), s32[]{:S(2)}) async-start(), calls=%async_computation.7 | async-start | bytes 4866048 | tf_op jit(solution)/shard_map/all_gather | solution.py:905
  8.2 13.1 %copy-start.17 = (bf16[48,4]{0,1:T(4,128)(2,1)S(1)}, bf16[48,4]{0,1:T(4,128)(2,1)}, u32[]{:S(2)}) copy-start(bf16[48,4]{0,1:T(4,128)(2,1)} %param.24) | copy-start | bytes 1156
  8.2 13.2 %copy-start.16 = (bf16[48,16]{0,1:T(8,128)(2,1)S(1)}, bf16[48,16]{0,1:T(8,128)(2,1)}, u32[]{:S(2)}) copy-start(bf16[48,16]{0,1:T(8,128)(2,1)} %param.29) | copy-start | bytes 4612
  8.2 13.3 %copy-start.12 = (bf16[48,80]{1,0:T(8,128)(2,1)S(1)}, bf16[48,80]{1,0:T(8,128)(2,1)}, u32[]{:S(2)}) copy-start(bf16[48,80]{1,0:T(8,128)(2,1)} %param.26) | copy-start | bytes 23044
  8.2 13.3 %copy-start.13 = (bf16[48,48]{1,0:T(8,128)(2,1)S(1)}, bf16[48,48]{1,0:T(8,128)(2,1)}, u32[]{:S(2)}) copy-start(bf16[48,48]{1,0:T(8,128)(2,1)} %param.27) | copy-start | bytes 13828
  8.2 13.4 %collective-permute-start.1 = (bf16[24,1536]{1,0:T(8,128)(2,1)S(1)}, bf16[24,1536]{1,0:T(8,128)(2,1)S(1)}, u32[]{:S(2)}, u32[]{:S(2)}) collective-permute-start(bf16[24,1536]{1,0:T(8,128)(2,1)S(1)} %get-tuple-element.247), channel_id=1, source_target_pairs={{0,8},{1,9},{2,10},{3,11},{4,12},{5,13},{6,14},{7,15},{8,0},{9,1},... | collective-permute-start | bytes 221192 | tf_op jit(solution)/shard_map/ppermute | solution.py:762
  10.9 10.8 %collective-permute-start = (bf16[24,1536]{1,0:T(8,128)(2,1)S(1)}, bf16[24,1536]{1,0:T(8,128)(2,1)S(1)}, u32[]{:S(2)}, u32[]{:S(2)}) collective-permute-start(bf16[24,1536]{1,0:T(8,128)(2,1)S(1)} %get-tuple-element.247), channel_id=1, source_target_pairs={{0,4},{1,5},{2,6},{3,7},{4,0},{5,1},{6,2},{7,3},{8,12},{9,13},{10,... | collective-permute-start | bytes 221192 | tf_op jit(solution)/shard_map/ppermute | solution.py:762
  11.3 10.4 %collective-permute-start.2 = (bf16[24,1536]{1,0:T(8,128)(2,1)S(1)}, bf16[24,1536]{1,0:T(8,128)(2,1)S(1)}, u32[]{:S(2)}, u32[]{:S(2)}) collective-permute-start(bf16[24,1536]{1,0:T(8,128)(2,1)S(1)} %get-tuple-element.247), channel_id=1, source_target_pairs={{0,12},{1,13},{2,14},{3,15},{4,8},{5,9},{6,10},{7,11},{8,4},{9,5},... | collective-permute-start | bytes 221192 | tf_op jit(solution)/shard_map/ppermute | solution.py:762
  21.9 8.1 %collective-permute-start.7 = (bf16[48,256]{1,0:T(8,128)(2,1)S(1)}, bf16[48,256]{1,0:T(8,128)(2,1)S(1)}, u32[]{:S(2)}, u32[]{:S(2)}) collective-permute-start(bf16[48,256]{1,0:T(8,128)(2,1)S(1)} %concatenate.74), channel_id=1, source_target_pairs={{0,12},{1,13},{2,14},{3,15},{4,8},{5,9},{6,10},{7,11},{8,4},{9,5},... | collective-permute-start | bytes 73736 | tf_op jit(solution)/shard_map/ppermute | solution.py:762
  23.5 6.5 %collective-permute-start.6 = (bf16[48,256]{1,0:T(8,128)(2,1)S(1)}, bf16[48,256]{1,0:T(8,128)(2,1)S(1)}, u32[]{:S(2)}, u32[]{:S(2)}) collective-permute-start(bf16[48,256]{1,0:T(8,128)(2,1)S(1)} %concatenate.74), channel_id=1, source_target_pairs={{0,8},{1,9},{2,10},{3,11},{4,12},{5,13},{6,14},{7,15},{8,0},{9,1},... | collective-permute-start | bytes 73736 | tf_op jit(solution)/shard_map/ppermute | solution.py:762
  25.5 4.5 %collective-permute-start.5 = (bf16[48,256]{1,0:T(8,128)(2,1)S(1)}, bf16[48,256]{1,0:T(8,128)(2,1)S(1)}, u32[]{:S(2)}, u32[]{:S(2)}) collective-permute-start(bf16[48,256]{1,0:T(8,128)(2,1)S(1)} %concatenate.74), channel_id=1, source_target_pairs={{0,4},{1,5},{2,6},{3,7},{4,0},{5,1},{6,2},{7,3},{8,12},{9,13},{10,... | collective-permute-start | bytes 73736 | tf_op jit(solution)/shard_map/ppermute | solution.py:762
  26.9 5.2 %collective-permute-start.4 = (bf16[2,2,1,1,24,768]{5,4,1,0,3,2:T(8,128)(2,1)S(1)}, bf16[2,2,1,1,24,768]{5,4,1,0,3,2:T(8,128)(2,1)S(1)}, u32[]{:S(2)}, u32[]{:S(2)}) collective-permute-start(bf16[2,2,1,1,24,768]{5,4,1,0,3,2:T(8,128)(2,1)S(1)} %get-tuple-element.223), channel_id=1, source_target_pairs={{0,1},{1,0},{2,3},{3,2},{4,5},{5,4},{6,7},{7,6},{8,9},{9,8},{10,11... | collective-permute-start | bytes 442376 | tf_op jit(solution)/shard_map/ppermute | solution.py:762
  28.5 5.1 %collective-permute-start.3 = (bf16[2,2,1,1,24,768]{5,4,1,0,3,2:T(8,128)(2,1)S(1)}, bf16[2,2,1,1,24,768]{5,4,1,0,3,2:T(8,128)(2,1)S(1)}, u32[]{:S(2)}, u32[]{:S(2)}) collective-permute-start(bf16[2,2,1,1,24,768]{5,4,1,0,3,2:T(8,128)(2,1)S(1)} %get-tuple-element.224), channel_id=1, source_target_pairs={{0,2},{1,3},{2,0},{3,1},{4,6},{5,7},{6,4},{7,5},{8,10},{9,11},{10,... | collective-permute-start | bytes 442376 | tf_op jit(solution)/shard_map/ppermute | solution.py:762
  33.8 4.7 %collective-permute-start.11 = (bf16[2,2,1,1,48,128]{5,4,3,2,1,0:T(8,128)(2,1)S(1)}, bf16[2,2,1,1,48,128]{5,4,3,2,1,0:T(8,128)(2,1)S(1)}, u32[]{:S(2)}, u32[]{:S(2)}) collective-permute-start(bf16[2,2,1,1,48,128]{5,4,3,2,1,0:T(8,128)(2,1)S(1)} %get-tuple-element.250), channel_id=1, source_target_pairs={{0,1},{1,0},{2,3},{3,2},{4,5},{5,4},{6,7},{7,6},{8,9},{9,8},{10,11... | collective-permute-start | bytes 147464 | tf_op jit(solution)/shard_map/ppermute | solution.py:762
  34.4 4.7 %collective-permute-start.10 = (bf16[2,2,1,1,48,128]{5,4,3,2,1,0:T(8,128)(2,1)S(1)}, bf16[2,2,1,1,48,128]{5,4,3,2,1,0:T(8,128)(2,1)S(1)}, u32[]{:S(2)}, u32[]{:S(2)}) collective-permute-start(bf16[2,2,1,1,48,128]{5,4,3,2,1,0:T(8,128)(2,1)S(1)} %get-tuple-element.251), channel_id=1, source_target_pairs={{0,2},{1,3},{2,0},{3,1},{4,6},{5,7},{6,4},{7,5},{8,10},{9,11},{10,... | collective-permute-start | bytes 147464 | tf_op jit(solution)/shard_map/ppermute | solution.py:762
  35.9 6.7 %collective-permute-start.8 = (bf16[2,2,2,1,24,768]{5,4,1,0,3,2:T(8,128)(2,1)S(1)}, bf16[2,2,2,1,24,768]{5,4,1,0,3,2:T(8,128)(2,1)S(1)}, u32[]{:S(2)}, u32[]{:S(2)}) collective-permute-start(bf16[2,2,2,1,24,768]{5,4,1,0,3,2:T(8,128)(2,1)S(1)} %pad_maximum_fusion.3), channel_id=1, source_target_pairs={{0,1},{1,0},{2,3},{3,2},{4,5},{5,4},{6,7},{7,6},{8,9},{9,8},{10,11... | collective-permute-start | bytes 884744 | tf_op jit(solution)/shard_map/ppermute | solution.py:762
  37.4 6.8 %collective-permute-start.9 = (bf16[2,2,1,2,24,768]{5,4,1,0,3,2:T(8,128)(2,1)S(1)}, bf16[2,2,1,2,24,768]{5,4,1,0,3,2:T(8,128)(2,1)S(1)}, u32[]{:S(2)}, u32[]{:S(2)}) collective-permute-start(bf16[2,2,1,2,24,768]{5,4,1,0,3,2:T(8,128)(2,1)S(1)} %pad_maximum_fusion.4), channel_id=1, source_target_pairs={{0,2},{1,3},{2,0},{3,1},{4,6},{5,7},{6,4},{7,5},{8,10},{9,11},{10,... | collective-permute-start | bytes 884744 | tf_op jit(solution)/shard_map/ppermute | solution.py:762
  44.4 7.2 %collective-permute-start.12 = (bf16[1,384,1536]{2,1,0:T(8,128)(2,1)S(1)}, bf16[1,384,1536]{2,1,0:T(8,128)(2,1)S(1)}, u32[]{:S(2)}, u32[]{:S(2)}) collective-permute-start(bf16[1,384,1536]{2,1,0:T(8,128)(2,1)S(1)} %bitcast.94), channel_id=1, source_target_pairs={{0,16},{16,0},{1,17},{17,1},{2,18},{18,2},{3,19},{19,3},{4,20},{20... | collective-permute-start | bytes 3538952 | tf_op jit(solution)/shard_map/ppermute | solution.py:762
  44.5 73.6 %collective-permute-start.16 = (bf16[768,1536]{1,0:T(8,128)(2,1)}, bf16[768,1536]{1,0:T(8,128)(2,1)}, u32[]{:S(2)}, u32[]{:S(2)}) collective-permute-start(bf16[768,1536]{1,0:T(8,128)(2,1)} %bitcast.34.refs_4_), channel_id=1, source_target_pairs={{0,16},{16,0},{1,17},{17,1},{2,18},{18,2},{3,19},{19,3},{4,20},{20... | collective-permute-start | bytes 7077896 | tf_op jit(solution)/shard_map/ppermute | solution.py:762
  45.0 73.1 %collective-permute-start.17 = (bf16[1536,768]{1,0:T(8,128)(2,1)}, bf16[1536,768]{1,0:T(8,128)(2,1)}, u32[]{:S(2)}, u32[]{:S(2)}) collective-permute-start(bf16[1536,768]{1,0:T(8,128)(2,1)} %bitcast.35.refs_6_), channel_id=1, source_target_pairs={{0,16},{16,0},{1,17},{17,1},{2,18},{18,2},{3,19},{19,3},{4,20},{20... | collective-permute-start | bytes 7077896 | tf_op jit(solution)/shard_map/ppermute | solution.py:762
  45.1 5.3 %collective-permute-start.13 = (bf16[2,2,2,1,48,128]{5,4,3,2,1,0:T(8,128)(2,1)S(1)}, bf16[2,2,2,1,48,128]{5,4,3,2,1,0:T(8,128)(2,1)S(1)}, u32[]{:S(2)}, u32[]{:S(2)}) collective-permute-start(bf16[2,2,2,1,48,128]{5,4,3,2,1,0:T(8,128)(2,1)S(1)} %pad_maximum_fusion.9), channel_id=1, source_target_pairs={{0,1},{1,0},{2,3},{3,2},{4,5},{5,4},{6,7},{7,6},{8,9},{9,8},{10,11... | collective-permute-start | bytes 294920 | tf_op jit(solution)/shard_map/ppermute | solution.py:762
  46.6 4.9 %collective-permute-start.14 = (bf16[2,2,1,2,48,128]{5,4,3,2,1,0:T(8,128)(2,1)S(1)}, bf16[2,2,1,2,48,128]{5,4,3,2,1,0:T(8,128)(2,1)S(1)}, u32[]{:S(2)}, u32[]{:S(2)}) collective-permute-start(bf16[2,2,1,2,48,128]{5,4,3,2,1,0:T(8,128)(2,1)S(1)} %pad_maximum_fusion.10), channel_id=1, source_target_pairs={{0,2},{1,3},{2,0},{3,1},{4,6},{5,7},{6,4},{7,5},{8,10},{9,11},{10,... | collective-permute-start | bytes 294920 | tf_op jit(solution)/shard_map/ppermute | solution.py:762
  53.4 8.9 %collective-permute-start.15 = (bf16[1,768,256]{2,1,0:T(8,128)(2,1)S(1)}, bf16[1,768,256]{2,1,0:T(8,128)(2,1)S(1)}, u32[]{:S(2)}, u32[]{:S(2)}) collective-permute-start(bf16[1,768,256]{2,1,0:T(8,128)(2,1)S(1)} %bitcast.99), channel_id=1, source_target_pairs={{0,16},{16,0},{1,17},{17,1},{2,18},{18,2},{3,19},{19,3},{4,20},{20... | collective-permute-start | bytes 1179656 | tf_op jit(solution)/shard_map/ppermute | solution.py:762
  54.5 42.4 %all-to-all-start = ((bf16[16,40,768]{2,1,0:T(8,128)(2,1)}), bf16[16,40,768]{2,1,0:T(8,128)(2,1)S(1)}, u32[]{:S(2)}, u32[]{:S(2)}) async-start(bf16[16,40,768]{2,1,0:T(8,128)(2,1)} %bitcast.104), calls=%async_computation | async-start | bytes 1966080 | tf_op jit(solution)/shard_map/all_to_all | solution.py:931
  111.5 30.3 %all-to-all-start.1 = ((bf16[16,40,768]{2,1,0:T(8,128)(2,1)}), bf16[16,40,768]{2,1,0:T(8,128)(2,1)S(1)}, u32[]{:S(2)}, u32[]{:S(2)}) async-start(bf16[16,40,768]{2,1,0:T(8,128)(2,1)} %bitcast.107), calls=%async_computation.1 | async-start | bytes 1966080 | tf_op jit(solution)/shard_map/all_to_all | solution.py:931
  163.8 27.7 %all-to-all-start.2 = ((bf16[16,40,768]{2,1,0:T(8,128)(2,1)}), bf16[16,40,768]{2,1,0:T(8,128)(2,1)S(1)}, u32[]{:S(2)}, u32[]{:S(2)}) async-start(bf16[16,40,768]{2,1,0:T(8,128)(2,1)} %bitcast.106), calls=%async_computation.2 | async-start | bytes 1966080 | tf_op jit(solution)/shard_map/all_to_all | solution.py:937
  191.4 23.9 %collective-permute-start.18 = (bf16[768,1536]{1,0:T(8,128)(2,1)}, bf16[768,1536]{1,0:T(8,128)(2,1)}, u32[]{:S(2)}, u32[]{:S(2)}) collective-permute-start(bf16[768,1536]{1,0:T(8,128)(2,1)} %get-tuple-element.128), channel_id=1, source_target_pairs={{0,16},{16,0},{1,17},{17,1},{2,18},{18,2},{3,19},{19,3},{4,20},{20... | collective-permute-start | bytes 7077896 | tf_op jit(solution)/shard_map/ppermute | solution.py:762
  191.4 23.9 %collective-permute-start.19 = (bf16[1536,768]{1,0:T(8,128)(2,1)}, bf16[1536,768]{1,0:T(8,128)(2,1)}, u32[]{:S(2)}, u32[]{:S(2)}) collective-permute-start(bf16[1536,768]{1,0:T(8,128)(2,1)} %get-tuple-element.129), channel_id=1, source_target_pairs={{0,16},{16,0},{1,17},{17,1},{2,18},{18,2},{3,19},{19,3},{4,20},{20... | collective-permute-start | bytes 7077896 | tf_op jit(solution)/shard_map/ppermute | solution.py:762
  191.9 87.5 %all-to-all-start.3 = ((bf16[16,40,768]{2,1,0:T(8,128)(2,1)}), bf16[16,40,768]{2,1,0:T(8,128)(2,1)S(1)}, u32[]{:S(2)}, u32[]{:S(2)}) async-start(bf16[16,40,768]{2,1,0:T(8,128)(2,1)} %bitcast.42), calls=%async_computation.3 | async-start | bytes 1966080 | tf_op jit(solution)/shard_map/all_to_all | solution.py:937
  196.9 138.1 %reduce-scatter.2.cloned.1.call-start = ((), (), s32[]{:S(2)}) async-start(), calls=%async_computation.6 | async-start | bytes 4866048 | tf_op jit(solution)/shard_map/reduce_scatter | solution.py:997
  279.4 3.7 %collective-permute-start.20 = (bf16[16,32,1536]{2,1,0:T(8,128)(2,1)}, bf16[16,32,1536]{2,1,0:T(8,128)(2,1)S(1)}, u32[]{:S(2)}, u32[]{:S(2)}) collective-permute-start(bf16[16,32,1536]{2,1,0:T(8,128)(2,1)} %bitcast.136), channel_id=1, source_target_pairs={{0,16},{16,0},{1,17},{17,1},{2,18},{18,2},{3,19},{19,3},{4,20},{20... | collective-permute-start | bytes 4718600 | tf_op jit(solution)/shard_map/ppermute | solution.py:762
  286.1 51.9 %all-to-all-start.4 = ((bf16[16,32,1536]{2,1,0:T(8,128)(2,1)}), bf16[16,32,1536]{2,1,0:T(8,128)(2,1)S(1)}, u32[]{:S(2)}, u32[]{:S(2)}) async-start(bf16[16,32,1536]{2,1,0:T(8,128)(2,1)} %add_convert_fusion), calls=%async_computation.4 | async-start | bytes 3145728 | tf_op jit(solution)/shard_map/all_to_all | solution.py:839
  (17 other events, 106.4 us)
Sparse Core Ops, SparseCore 0:
  14.3 76.6 all-gather.2
  214.3 120.6 reduce-scatter.1

commit v2 on v1

--- a/solution.py
+++ b/solution.py
@@ -99,9 +99,35 @@
     return [pl.BlockSpec((small.shape[0], LANES), lambda p, lens, half=half: (0, half)) for half in range(2)]
 
 
-def forward_kernel(len_ref, u_ref, wx_ref, sela_ref, stepb_ref, vec_ref, a_ref,
-                   bx_ref, xs_ref, delta_ref, sel_ref, mix_ref, h_ref,
-                   state, bw, cw, low, *, group, rank, taps):
+def unpack_small(small_ref, taps, rank, states, own, half, vec_ref, a_ref, gain_ref, router_ref):
+    width = small_ref.shape[0]
+    columns = small_ref[...].astype(F32)
+    rows = columns.T
+    first = rank + taps + 4
+    vec_ref[...] = rows[rank : rank + ROWS]
+    a_ref[...] = -jnp.exp(rows[first : first + states]) * LOG2E
+    devices = columns.reshape(width // (2 * own), 2 * own, LANES)
+    for part in range(2):
+        rows = devices[:, part * own : (part + 1) * own].reshape(width // 2, LANES).T
+        gain_ref[part : part + 1, :] = rows[first - 1 : first]
+        router_ref[part * half : (part + 1) * half, :] = rows[first + states : first + states + half].astype(BF16)
+
+
+def forward_kernel(len_ref, x_ref, wx_ref, sela_ref, stepb_ref, *refs, group, rank, taps, own, half):
+    if own:
+        *refs, vec_ref, a_ref, gain_ref, router_ref, u_ref = refs
+
+        @pl.when(pl.program_id(0) == 0)
+        def _():
+            unpack_small(stepb_ref, taps, rank, a_ref.shape[0], own, half, vec_ref, a_ref, gain_ref, router_ref)
+
+        hidden = x_ref[...].astype(F32)
+        inv = lax.rsqrt(jnp.mean(hidden * hidden, axis=1, keepdims=True) + EPSILON)
+        u_ref[...] = (hidden * inv * gain_ref[:1, :]).astype(BF16)
+    else:
+        vec_ref, a_ref, *refs = refs
+        u_ref = x_ref
+    bx_ref, xs_ref, delta_ref, sel_ref, mix_ref, h_ref, state, bw, cw, low = refs
     states, width = a_ref.shape
     steps = u_ref.shape[0]
     chunks = width // LANES
@@ -173,46 +199,64 @@
     lax.fori_loop(used, steps // ROWS, clear, 0)
 
 
-def mixer_forward(sample, u, wx, small, vec, a2, packs, rank, taps, group=12):
-    rows, model = u.shape
-    steps = rows // packs
-    states, width = a2.shape
+def mixer_forward(sample, x, wx, small, vec, a2, packs, rank, taps, states, own, half, group=12):
+    rows, model = x.shape
+    steps, width = rows // packs, wx.shape[1]
     per_pack = lambda p, lens: (p, 0)
-    whole = lambda v: pl.BlockSpec(v.shape, lambda p, lens: (0, 0))
+    fixed = lambda p, lens: (0, 0)
+    whole = lambda v: pl.BlockSpec(v.shape, fixed)
     mats = pl.BlockSpec((steps, width), per_pack)
+    toks = pl.BlockSpec((steps, model), per_pack)
+    given = [] if own else [vec, a2]
+    outs = [
+        jax.ShapeDtypeStruct((rows + packs * ROWS, width), F32),
+        jax.ShapeDtypeStruct((rows, width), F32),
+        jax.ShapeDtypeStruct((rows, width), F32),
+        jax.ShapeDtypeStruct((rows, LANES), F32),
+        jax.ShapeDtypeStruct((rows, width), F32),
+        jax.ShapeDtypeStruct((rows // ROWS, states, width), F32),
+    ]
+    out_specs = [
+        pl.BlockSpec((steps + ROWS, width), per_pack),
+        mats,
+        mats,
+        pl.BlockSpec((steps, LANES), per_pack),
+        mats,
+        pl.BlockSpec((steps // ROWS, states, width), lambda p, lens: (p, 0, 0)),
+    ]
+    scratch = [
+        pltpu.VMEM((states, width), F32),
+        pltpu.VMEM((steps * states, LANES), F32),
+        pltpu.VMEM((steps * states, LANES), F32),
+        pltpu.VMEM((steps, width), BF16),
+    ]
+    count = len(outs)
+    if own:
+        more = [((ROWS, width), F32), ((states, width), F32), ((2, model), F32), ((2 * half, model), BF16)]
+        outs += [jax.ShapeDtypeStruct(*one) for one in more] + [jax.ShapeDtypeStruct((rows, model), BF16)]
+        out_specs += [pl.BlockSpec(shape, fixed) for shape, _ in more] + [toks]
+
+    def kernel(len_ref, x_ref, wx_ref, sela_ref, stepb_ref, *refs):
+        at = len(given) + count
+        refs = refs[:at] + refs[len(given) + len(outs) :] + refs[at : len(given) + len(outs)]
+        forward_kernel(
+            len_ref, x_ref, wx_ref, sela_ref, stepb_ref, *refs, group=group, rank=rank, taps=taps, own=own, half=half
+        )
+
     return pl.pallas_call(
-        functools.partial(forward_kernel, group=group, rank=rank, taps=taps),
+        kernel,
         grid_spec=pltpu.PrefetchScalarGridSpec(
             num_scalar_prefetch=1,
             grid=(packs,),
-            in_specs=[pl.BlockSpec((steps, model), per_pack), whole(wx), *lane_halves(small), whole(vec), whole(a2)],
-            out_specs=[
-                pl.BlockSpec((steps + ROWS, width), per_pack),
-                mats,
-                mats,
-                pl.BlockSpec((steps, LANES), per_pack),
-                mats,
-                pl.BlockSpec((steps // ROWS, states, width), lambda p, lens: (p, 0, 0)),
-            ],
-            scratch_shapes=[
-                pltpu.VMEM((states, width), F32),
-                pltpu.VMEM((steps * states, LANES), F32),
-                pltpu.VMEM((steps * states, LANES), F32),
-                pltpu.VMEM((steps, width), BF16),
-            ],
+            in_specs=[toks, whole(wx), *lane_halves(small), *[whole(v) for v in given]],
+            out_specs=out_specs,
+            scratch_shapes=scratch,
         ),
-        out_shape=[
-            jax.ShapeDtypeStruct((rows + packs * ROWS, width), F32),
-            jax.ShapeDtypeStruct((rows, width), F32),
-            jax.ShapeDtypeStruct((rows, width), F32),
-            jax.ShapeDtypeStruct((rows, LANES), F32),
-            jax.ShapeDtypeStruct((rows, width), F32),
-            jax.ShapeDtypeStruct((rows // ROWS, states, width), F32),
-        ],
+        out_shape=outs,
         compiler_params=pltpu.CompilerParams(vmem_limit_bytes=56 << 20),
         cost_estimate=pl.CostEstimate(flops=0, bytes_accessed=120_000_000, transcendentals=0),
         name="mixer_forward",
-    )(sample, u, wx, small, small, vec, a2)
+    )(sample, x, wx, small, small, *given)
 
 
 def step_slopes(d):
@@ -549,12 +593,34 @@
     return ref[here.start // run : here.stop // run].reshape(here.stop - here.start, ref.shape[2])
 
 
-def late_out(late, own):
+def late_specs(late, own):
     devices, count, model = late.shape
     if own % 16 == 0:
-        return late, pl.BlockSpec((devices, own, model), lambda p, lens: (0, 1, 0))
-    out = late[:, count - own :].reshape(devices * own, model)
-    return out, pl.BlockSpec(out.shape, lambda p, lens: (0, 0))
+        block = (devices, own, model)
+        return [late, late], [pl.BlockSpec(block, lambda p, lens, at=at: (0, at, 0)) for at in range(2)]
+    rows = [late[:, at : at + size].reshape(-1, model) for at, size in ((0, own // 2), (own // 2, own // 2), (own, own))]
+    return rows, [pl.BlockSpec(v.shape, lambda p, lens: (0, 0)) for v in rows]
+
+
+def gate_halves(refs, scratch):
+    if len(refs) == 3:
+        return refs[:2], refs[2]
+
+    @pl.when(pl.program_id(0) == 0)
+    def _():
+        devices, run, model = refs[0].shape
+        step = 4
+        for at in range(0, devices, step):
+            both = refs[0][at : at + step].astype(F32)
+            for half, ref in enumerate(scratch):
+                one = both[:, half * (run // 2) : (half + 1) * (run // 2)]
+                ref[at * (run // 2) : (at + step) * (run // 2), :] = one.reshape(step * (run // 2), model).astype(BF16)
+
+    return scratch, refs[1]
+
+
+def gate_scratch(operands, model):
+    return [pltpu.VMEM((model, model), BF16)] * 2 if len(operands) == 2 else []
 
 
 def live_rows(length, steps):
@@ -566,12 +632,14 @@
     return values * inv, inv
 
 
-def home_forward_kernel(len_ref, u_ref, wl_ref, wr_ref, wout_ref, mix_ref, x_ref, gain_ref, router_ref, hot_ref, choose_ref,
-                        z_ref, gated_ref, h1_ref, weight_ref, sent_ref, total):
+def home_forward_kernel(len_ref, u_ref, mix_ref, x_ref, gain_ref, router_ref, hot_ref, choose_ref, *refs, count):
+    late, refs = refs[:count], refs[count:]
+    z_ref, gated_ref, h1_ref, weight_ref, sent_ref, total, *scratch = refs
+    gates, wout_ref = gate_halves(late, scratch)
     pack = pl.program_id(0)
     steps, model = u_ref.shape
     mixed = jnp.zeros((steps, model), F32)
-    for half, w_ref in enumerate((wl_ref, wr_ref)):
+    for half, w_ref in enumerate(gates):
         here = slice(half * model, (half + 1) * model)
         z = dot(u_ref[...], w_ref[...])
         z_ref[:, here] = z
@@ -580,7 +648,7 @@
         mixed = mixed + dot(gated, rows_from(wout_ref, here))
     h1 = x_ref[...].astype(F32) + live_rows(len_ref[pack], steps) * mixed
     h1_ref[...] = h1
-    routed = (norm_of(h1)[0] * gain_ref[...]).astype(BF16)
+    routed = (norm_of(h1)[0] * gain_ref[1:2, :]).astype(BF16)
     logits = dot(routed, router_ref[...], ((1,), (1,)))
     odds = jnp.exp(logits - jnp.max(logits, axis=1, keepdims=True))
     probs = odds / jnp.sum(odds, axis=1, keepdims=True)
@@ -600,26 +668,26 @@
         sent_ref[...] = total[...].astype(BF16)
 
 
-def home_forward(sample, u, wz, late, own, mix, tokens, gain, router, hot, chooser):
-    wout, wout_spec = late_out(late, own)
+def home_forward(sample, u, late, own, mix, tokens, gain, router, hot, chooser):
+    operands, specs = late_specs(late, own)
     packs = sample.shape[0]
     rows, model = u.shape
     steps, inner, slots = rows // packs, mix.shape[1], chooser.shape[0]
     whole = lambda v: pl.BlockSpec(v.shape, lambda p, lens: (0, 0))
     part = lambda n: pl.BlockSpec((steps, n), lambda p, lens: (p, 0))
     return pl.pallas_call(
-        home_forward_kernel,
+        functools.partial(home_forward_kernel, count=len(operands)),
         grid_spec=pltpu.PrefetchScalarGridSpec(
             num_scalar_prefetch=1,
             grid=(packs,),
             in_specs=[
-                part(model), whole(wz[0]), whole(wz[1]), wout_spec, part(inner), part(model), whole(gain), whole(router),
-                part(hot.shape[1]), pl.BlockSpec((slots, steps), lambda p, lens: (0, p)),
+                part(model), part(inner), part(model), whole(gain), whole(router),
+                part(hot.shape[1]), pl.BlockSpec((slots, steps), lambda p, lens: (0, p)), *specs,
             ],
             out_specs=[
                 part(inner), part(inner), part(model), part(1), pl.BlockSpec((slots, model), lambda p, lens: (0, 0)),
             ],
-            scratch_shapes=[pltpu.VMEM((slots, model), F32)],
+            scratch_shapes=[pltpu.VMEM((slots, model), F32), *gate_scratch(operands, model)],
         ),
         out_shape=[
             jax.ShapeDtypeStruct((rows, inner), F32),
@@ -630,13 +698,15 @@
         ],
         compiler_params=pltpu.CompilerParams(vmem_limit_bytes=56 << 20),
         name="home_forward",
-    )(sample, u, wz[0], wz[1], wout, mix, tokens, gain, router, hot, chooser)
-
-
-def home_backward_kernel(len_ref, choose_ref, back_ref, h1_ref, gy_ref, gain_ref, wout_ref, z_ref, mix_ref, u_ref, gated_ref,
-                         wl_ref, wr_ref,
-                         gh_ref, gm_ref, gu_ref, ggain_ref, *refs, own):
-    *outs, sum_z, sum_out = refs
+    )(sample, u, mix, tokens, gain, router, hot, chooser, *operands)
+
+
+def home_backward_kernel(len_ref, choose_ref, back_ref, h1_ref, gy_ref, gain_ref, z_ref, mix_ref, u_ref, gated_ref, *refs,
+                         own, count, sums):
+    late, refs = refs[:count], refs[count:]
+    gh_ref, gm_ref, gu_ref, ggain_ref, *refs = refs
+    outs, (sum_z, sum_out, *scratch) = refs[:sums], refs[sums:]
+    gates, wout_ref = gate_halves(late, scratch)
     pack = pl.program_id(0)
     steps, model = u_ref.shape
 
@@ -648,7 +718,7 @@
 
     grad = dot(choose_ref[...], back_ref[...], ((0,), (0,)))
     normed, inv = norm_of(h1_ref[...])
-    scaled = grad * gain_ref[...]
+    scaled = grad * gain_ref[1:2, :]
     if len(outs) == 1:
         ones = jnp.ones((steps, LANES), BF16)
         high, rest = split_low(grad * normed)
@@ -659,7 +729,7 @@
     gh_ref[...] = gh
     grad_mixed = (live_rows(len_ref[pack], steps) * gh).astype(BF16)
     grad_u = jnp.zeros((steps, model), F32)
-    for half, w_ref in enumerate((wl_ref, wr_ref)):
+    for half, w_ref in enumerate(gates):
         here = slice(half * model, (half + 1) * model)
         grad_gated = dot(grad_mixed, rows_from(wout_ref, here), ((1,), (1,)))
         z = z_ref[:, here]
@@ -691,8 +761,8 @@
         lax.fori_loop(0, model // own, gather, 0)
 
 
-def home_backward(sample, chooser, back, h1, gy, gain, late, own, z, mix, u, gated, wz):
-    wout, wout_spec = late_out(late, own)
+def home_backward(sample, chooser, back, h1, gy, gain, late, own, z, mix, u, gated):
+    operands, specs = late_specs(late, own)
     packs = sample.shape[0]
     rows, model = u.shape
     steps, inner, slots = rows // packs, mix.shape[1], chooser.shape[0]
@@ -704,19 +774,21 @@
     sums = [(inner, inner)] if packed else [(model, inner), (inner, model)]
     gains = (model, LANES) if packed else (1, model)
     return pl.pallas_call(
-        functools.partial(home_backward_kernel, own=shard),
+        functools.partial(home_backward_kernel, own=shard, count=len(operands), sums=len(sums)),
         grid_spec=pltpu.PrefetchScalarGridSpec(
             num_scalar_prefetch=1,
             grid=(packs,),
             in_specs=[
                 pl.BlockSpec((slots, steps), lambda p, lens: (0, p)), whole(back), part(model), part(model), whole(gain),
-                wout_spec, part(inner), part(inner), part(model), part(inner), whole(wz[0]), whole(wz[1]),
+                part(inner), part(inner), part(model), part(inner), *specs,
             ],
             out_specs=[
                 part(model), part(inner), part(model), pl.BlockSpec(gains, fixed),
                 *[pl.BlockSpec(shape, fixed) for shape in sums],
             ],
-            scratch_shapes=[pltpu.VMEM((model, inner), F32), pltpu.VMEM((inner, model), F32)],
+            scratch_shapes=[
+                pltpu.VMEM((model, inner), F32), pltpu.VMEM((inner, model), F32), *gate_scratch(operands, model),
+            ],
         ),
         out_shape=[
             jax.ShapeDtypeStruct((rows, model), F32),
@@ -728,7 +800,7 @@
         compiler_params=pltpu.CompilerParams(vmem_limit_bytes=60 << 20),
         cost_estimate=pl.CostEstimate(flops=0, bytes_accessed=100_000, transcendentals=0),
         name="home_backward",
-    )(sample, chooser, back, h1, gy, gain, wout, z, mix, u, gated, wz[0], wz[1])
+    )(sample, chooser, back, h1, gy, gain, z, mix, u, gated, *operands)
 
 
 def expert_grads_kernel(q_ref, gr_ref, *refs, parts):
@@ -757,6 +829,50 @@
     )(q, gr, *gps, *acts)
 
 
+def finish_kernel(parts_ref, late_ref, in_ref, out_ref, scan_ref, step_ref, conv_ref, decay_ref, router_ref, *vector_refs,
+                  own, rank, taps, states, half):
+    total = parts_ref[0].astype(F32)
+    for i in range(1, parts_ref.shape[0]):
+        total = total + parts_ref[i].astype(F32)
+    late = late_ref[...].astype(F32)
+    width = total.shape[1]
+    model = out_ref.shape[1]
+    in_ref[:, :width] = total[:own]
+    in_ref[:, width:] = late[:own]
+    out_ref[:own, :] = late[own:, :model]
+    out_ref[own:, :] = late[own:, model:]
+    small = [total[own:, at : at + 2 * LANES] for at in range(0, width, 2 * LANES)]
+    first = jnp.concatenate([v[:, :LANES] for v in small], axis=0)
+    second = jnp.concatenate([v[:, LANES:] for v in small], axis=0)
+    scan_ref[...] = first[:, : rank + 2 * states]
+    step_ref[...] = second[:, :rank]
+    rows = jnp.concatenate([second, jnp.zeros((LANES - 2 * own, LANES), F32)], axis=0).T
+    at = rank + taps + 4
+    conv_ref[...] = rows[rank : rank + taps, : 2 * own]
+    decay_ref[...] = rows[at : at + states, : 2 * own]
+    routers = rows[at + states : at + states + half]
+    router_ref[:half, :] = routers[:, :own]
+    router_ref[half:, :] = pltpu.roll(routers, LANES - own, 1)[:, :own]
+    for i, ref in enumerate(vector_refs[:3]):
+        ref[...] = rows[rank + taps + i, : 2 * own]
+    gains = rows[at - 1 : at]
+    vector_refs[3][...] = gains[0, :own]
+    vector_refs[4][...] = pltpu.roll(gains, LANES - own, 1)[0, :own]
+
+
+def finish(parts, late, own, rank, taps, states, half):
+    width = late.shape[1]
+    shapes = [
+        (own, 2 * width), (2 * own, width // 2), (2 * own, rank + 2 * states), (2 * own, rank), (taps, 2 * own),
+        (states, 2 * own), (2 * half, own), (2 * own,), (2 * own,), (2 * own,), (own,), (own,),
+    ]
+    return pl.pallas_call(
+        functools.partial(finish_kernel, own=own, rank=rank, taps=taps, states=states, half=half),
+        out_shape=[jax.ShapeDtypeStruct(shape, F32) for shape in shapes],
+        name="finish",
+    )(parts, late)
+
+
 def swap(values, axis, mask):
     count = lax.axis_size(axis)
     return lax.ppermute(values, axis, [(i, i ^ mask) for i in range(count)])
@@ -833,10 +949,6 @@
     for got in sent:
         total = total + got.astype(F32)
     return total.astype(BF16)
-
-
-def scatter_end(parts):
-    return jnp.sum(lax.all_to_all(parts, "fsdp", 0, 0, tiled=True).astype(F32), axis=0)
 
 
 def body(
@@ -903,7 +1015,6 @@
     folds = inner // (2 * LANES)
     late = jnp.concatenate([input_weight[:, inner : inner + model], input_weight[:, inner + model :], out_weight], axis=0)
     late = lax.all_gather(late, ("dp", "fsdp"), axis=0, tiled=False)
-    input_z = [late[:, i * own_model : (i + 1) * own_model].reshape(model, model) for i in range(2)]
     ups = [expert_up[0]] + [swap(expert_up[0], "dp", k) for k in range(1, groups)]
     downs = [expert_down[0]] + [swap(expert_down[0], "dp", k) for k in range(1, groups)]
 
@@ -938,33 +1049,31 @@
 
     cotangent = cotangent.reshape(rows, model)
 
-    hidden = tokens.reshape(rows, model).astype(F32)
-    inv_first = lax.rsqrt(jnp.mean(hidden * hidden, axis=-1, keepdims=True) + EPSILON)
-    normed_first = hidden * inv_first
     input_x, small_full, upstream_rows = gather_both(
         input_weight[:, :inner], small, dot(chooser, cotangent).astype(BF16)
     )
     upstream_sent = to_experts(upstream_rows)
-    vectors_full = small_full[:, LANES + rank :].T
-    vectors_first = vectors_full[:ROWS].astype(F32)
-    decay_full = vectors_full[taps + 4 : taps + 4 + states].astype(F32)
-    gains = vectors_full[taps + 3].reshape(devices, 2, own_model)
-    gain_one = gains[:, 0].reshape(model).astype(F32)
-    gain_two = gains[:, 1].reshape(model).astype(F32)
-    router_full = vectors_full[taps + 4 + states : taps + 4 + states + half].reshape(half, devices, 2, own_model)
-    router_full = router_full.transpose(2, 0, 1, 3).reshape(experts, model)
-
-    normed_low = (normed_first * gain_one).astype(BF16)
-    decay_mat = -jnp.exp(decay_full)
-    decay_two = decay_mat * LOG2E
-    branch_x, scan_in, step_size, selected, mixer_out, states_kept = mixer_forward(
-        sample, normed_low, input_x, small_full, vectors_first, decay_two, micro, rank, taps
-    )
+    tokens = tokens.reshape(rows, model)
+    mixer_in = [sample, tokens, input_x, small_full, None, None]
+    if not packed:
+        vectors_full = small_full[:, LANES + rank :].T
+        vectors_first = vectors_full[:ROWS].astype(F32)
+        decay_two = -jnp.exp(vectors_full[taps + 4 : taps + 4 + states].astype(F32)) * LOG2E
+        gains = vectors_full[taps + 3].reshape(devices, 2, own_model).transpose(1, 0, 2).reshape(2, model).astype(F32)
+        router_full = vectors_full[taps + 4 + states : taps + 4 + states + half].reshape(half, devices, 2, own_model)
+        router_full = router_full.transpose(2, 0, 1, 3).reshape(experts, model)
+        hidden = tokens.astype(F32)
+        inv_first = lax.rsqrt(jnp.mean(hidden * hidden, axis=-1, keepdims=True) + EPSILON)
+        normed_low = (hidden * inv_first * gains[:1]).astype(BF16)
+        mixer_in = [sample, normed_low, input_x, small_full, vectors_first, decay_two]
+    mixer_outs = mixer_forward(*mixer_in, micro, rank, taps, states, own_model if packed else 0, half)
+    branch_x, scan_in, step_size, selected, mixer_out, states_kept = mixer_outs[:6]
+    if packed:
+        vectors_first, decay_two, gains, router_full, normed_low = mixer_outs[6:]
     mixer_out, upstream_sent = lax.optimization_barrier((mixer_out, upstream_sent))
     kept_hot = route_hot.reshape(rows, experts).astype(F32) * kept[:, None]
     branch_z, gated_low, residual, weight_row, sent = home_forward(
-        sample, normed_low, input_z, late, own_inner, mixer_out, tokens.reshape(rows, model), gain_two[None, :], router_full,
-        kept_hot, chooser,
+        sample, normed_low, late, own_inner, mixer_out, tokens, gains, router_full, kept_hot, chooser,
     )
     received = to_experts(sent)
 
@@ -979,7 +1088,7 @@
     lane = jnp.arange(LANES)
     router_grads = router_grad.reshape(2, half, devices, own_model).transpose(2, 0, 3, 1).reshape(inner, half)
     extra = jnp.pad(router_grads, ((0, 0), (at_router, LANES - at_router - half)))
-    gain_row = gain_one[None, :]
+    gain_row = gains[:1]
     grad_back, matrix_grads, extra, gain_row, result = lax.optimization_barrier(
         (grad_back, matrix_grads, extra, gain_row, result)
     )
@@ -988,8 +1097,8 @@
     others = [swap(other, "dp", k // 2 + 1) for k, other in enumerate(others)]
 
     grad_residual, grad_mixer, grad_normed_z, gain_two_grad, *late_terms = home_backward(
-        sample, chooser, grad_back.reshape(experts * slots, model), residual, cotangent, gain_two[None, :], late,
-        own_inner, branch_z, mixer_out, normed_low, gated_low, input_z,
+        sample, chooser, grad_back.reshape(experts * slots, model), residual, cotangent, gains, late,
+        own_inner, branch_z, mixer_out, normed_low, gated_low,
     )
     if not packed:
         blocks = [v.reshape(devices, -1, v.shape[1]) for v in late_terms]
@@ -1000,7 +1109,7 @@
     grad_mixer, others = lax.optimization_barrier((grad_mixer, others))
     mixer_grads = mixer_backward(
         jnp.append(sample, lax.axis_index("dp")), step_size, scan_in, branch_x, grad_mixer, selected, small_full, vectors_first, decay_two,
-        states_kept, input_x, tokens.reshape(rows, model), gain_row, grad_normed_z, grad_residual, normed_low, extra,
+        states_kept, input_x, tokens, gain_row, grad_normed_z, grad_residual, normed_low, extra,
         gain_two_grad, micro, rank, taps, at_gain, own_model, groups,
     )
     if packed:
@@ -1017,31 +1126,47 @@
     early_terms, result = lax.optimization_barrier((early_terms, result))
     early_terms = scatter_begin(early_terms)
     early_terms, others, result = lax.optimization_barrier((early_terms, others, result))
-    early_grads = scatter_end(early_terms)
+    early_parts = lax.all_to_all(early_terms, "fsdp", 0, 0, tiled=True)
     up_grad, down_grad = up_own.astype(F32), down_own.astype(F32)
     for k in range(groups - 1):
         up_grad = up_grad + others[2 * k].astype(F32)
         down_grad = down_grad + others[2 * k + 1].astype(F32)
-    late_grads = late_grads.astype(F32)
     block_output = (residual + weight_row * from_experts(result)).astype(BF16)
-    small_grads = unfold(early_grads[own_model:], folds)
-    vector_grads = small_grads[:, LANES:]
-    routers = vector_grads[:, at_router : at_router + half]
+    if packed:
+        in_grad, out_grad, scan_grad, step_grad, conv_grad, decay_grad, router_grad, *vector_grads = finish(
+            early_parts, late_grads, own_model, rank, taps, states, half
+        )
+        conv_grad, decay_grad, router_grad = conv_grad.T, decay_grad.T, router_grad.T
+    else:
+        early_grads = jnp.sum(early_parts.astype(F32), axis=0)
+        late_grads = late_grads.astype(F32)
+        in_grad = jnp.concatenate([early_grads[:own_model], late_grads[:own_model]], axis=1)
+        out_grad = unfold(late_grads[own_model:], 2)
+        small_grads = unfold(early_grads[own_model:], folds)
+        scan_grad, step_grad = small_grads[:, : rank + 2 * states], small_grads[:, LANES : LANES + rank]
+        small_grads = small_grads[:, LANES:]
+        conv_grad = small_grads[:, rank : rank + taps]
+        decay_grad = small_grads[:, at_decay : at_decay + states]
+        routers = small_grads[:, at_router : at_router + half]
+        router_grad = jnp.concatenate([routers[:own_model], routers[own_model:]], axis=1)
+        *vector_grads, gain_grads = [small_grads[:, rank + taps + i] for i in range(4)]
+        vector_grads += [gain_grads[:own_model], gain_grads[own_model:]]
+    conv_bias_grad, step_bias_grad, skip_grad, gain_one_grad, gain_two_grad = vector_grads
     return (
         block_output.reshape(micro, steps, model),
         tokens_grad.reshape(micro, steps, model),
-        vector_grads[:own_model, at_gain],
-        jnp.concatenate([early_grads[:own_model], late_grads[:own_model]], axis=1),
-        vector_grads[:, rank : rank + taps],
-        vector_grads[:, rank + taps],
-        small_grads[:, : rank + 2 * states],
-        vector_grads[:, :rank],
-        vector_grads[:, rank + taps + 1],
-        vector_grads[:, at_decay : at_decay + states],
-        vector_grads[:, rank + taps + 2],
-        unfold(late_grads[own_model:], 2),
-        vector_grads[own_model:, at_gain],
-        jnp.concatenate([routers[:own_model], routers[own_model:]], axis=1),
+        gain_one_grad,
+        in_grad,
+        conv_grad,
+        conv_bias_grad,
+        scan_grad,
+        step_grad,
+        step_bias_grad,
+        decay_grad,
+        skip_grad,
+        out_grad,
+        gain_two_grad,
+        router_grad,
         up_grad[None],
         down_grad[None],
     )

time: 355 us -> 345 us (0.972)
  local copies, waits for them, and re-layouts: 21.8 us -> 11.5 us
  starting transfers between devices: 53.6 us -> 45.9 us
  Pallas kernels: 152 us -> 159 us
  waiting for transfers between devices: 78.3 us -> 82.8 us
    slice x16 -> x1, local copies, waits for them, and re-layouts: 9.09 us -> 0.58 us  [body(): gain_row = gains[:1]]
    all_to_all x1, starting transfers between devices: 11.7 us -> 5.24 us  [body(): early_parts = lax.all_to_all(early_terms, 'fsdp', 0, 0, tiled=True)]
    pallas_call x3 -> x4, Pallas kernels: 54.7 us -> 59.1 us  [the longest x1 28 us: mixer_forward(): pl.pallas_call(kernel, grid_spec=pltpu.PrefetchScalarGridSpec(num_scalar_...]
  transfers between devices with their start and end apart: 28 -> 28, of which waited for: 14 -> 14; matrix products, arithmetic and copies ran while one was open for 13% -> 11% of each run, Pallas kernels for 37% -> 40%
where the time goes in v2:
time: 345 us; the launch traced here: 342 us
  Pallas kernels  159 us (46%)
  waiting for transfers between devices  82.8 us (24%)
  starting transfers between devices  45.9 us (13%)
  other arithmetic  22.7 us (7%)
  between operations  14.6 us (4%)
  local copies, waits for them, and re-layouts  11.5 us (3%)
  matrix products  6.15 us (2%)
    pallas_call x1, Pallas kernels, mixer_backward(): pl.pallas_call(functools.partial(backward_kernel, group=group, rank=rank,...  66.7 us
    reduce_scatter x1, waiting for transfers between devices, body(): lax.psum_scatter(late_terms[0], ('dp', 'fsdp'), scatter_dimension=0, tile...  28.2 us
    pallas_call x1, Pallas kernels, mixer_forward(): pl.pallas_call(kernel, grid_spec=pltpu.PrefetchScalarGridSpec(num_scalar_...  28 us
    all_to_all x2, waiting for transfers between devices, to_experts(): lax.all_to_all(values.reshape(experts, slots, -1), 'fsdp', 0, 0, tiled=True)  25.9 us
    pallas_call x1, Pallas kernels, expert_pass(): pl.pallas_call(functools.partial(expert_kernel, parts=parts), grid=(hidde...  21 us
    ppermute x21, waiting for transfers between devices, swap(): return lax.ppermute(values, axis, [(i, i ^ mask) for i in range(count)])  19 us
    ppermute x21, starting transfers between devices, swap(): return lax.ppermute(values, axis, [(i, i ^ mask) for i in range(count)])  18.2 us
    pallas_call x1, Pallas kernels, home_backward(): pl.pallas_call(functools.partial(home_backward_kernel, own=shard, count=l...  17.4 us
  transfers between devices with their start and end apart: 28, of which 14 were waited for; matrix products, arithmetic and copies ran while one was open for 11% of the time, Pallas kernels for 40%

profile of v2, /device:TPU:8, one launch (start us, length us, event | category | flops | bytes accessed | tf_op | source)
XLA Modules:
  0.0 342.4 jit_solution(14241823201489489897)
XLA Ops:
  8.2 2.7 collective-permute-start.1
  12.5 1.6 pad_maximum_fusion.5
  18.4 2.8 convolution_convert_fusion
  21.9 1.6 collective-permute-start.7
  23.5 2.0 collective-permute-start.6
  26.9 1.6 collective-permute-start.4
  30.1 2.0 collective-permute-done.4
  39.1 3.5 %collective-permute-done.8 = bf16[2,2,2,1,24,768]{5,4,1,0,3,2:T(8,128)(2,1)S(1)} collective-permute-done((bf16[2,2,2,1,24,768]{5,4,1,0,3,2:T(8,128)(2,1)S(1)}, bf16[2,2,2,1,24,768]{5,4,1,0,3,2:T(8,128)(2,1)S(1)}, u32[]{:S(2)}, u32[]{:S(2)}) %collective-permute-start.8) | collective-permute-done | bytes 294944 | tf_op jit(solution)/shard_map/ppermute | solution.py:878
  45.5 4.8 %collective-permute-done.13 = bf16[2,2,2,1,48,128]{5,4,1,0,3,2:T(8,128)(2,1)S(1)} collective-permute-done((bf16[2,2,2,1,48,128]{5,4,1,0,3,2:T(8,128)(2,1)S(1)}, bf16[2,2,2,1,48,128]{5,4,1,0,3,2:T(8,128)(2,1)S(1)}, u32[]{:S(2)}, u32[]{:S(2)}) %collective-permute-start.13) | collective-permute-done | bytes 98336 | tf_op jit(solution)/shard_map/ppermute | solution.py:878
  51.4 1.6 pad_maximum_fusion
  53.0 7.4 %all-to-all-start = ((bf16[16,40,768]{2,1,0:T(8,128)(2,1)}), bf16[16,40,768]{2,1,0:T(8,128)(2,1)S(1)}, u32[]{:S(2)}, u32[]{:S(2)}) async-start(bf16[16,40,768]{2,1,0:T(8,128)(2,1)} %bitcast.97), calls=%async_computation | async-start | bytes 1966080 | tf_op jit(solution)/shard_map/all_to_all | solution.py:1042
  66.0 28.0 %mixer_forward.1 = (f32[528,1536]{1,0:T(8,128)}, f32[512,1536]{1,0:T(8,128)}, f32[512,1536]{1,0:T(8,128)}, f32[512,128]{1,0:T(8,128)}, f32[512,1536]{1,0:T(8,128...) custom-call(s32[2]{0:T(128)} %copy-done.14, ...), custom_call_target="tpu_custom_call" | custom-call | bytes 120000000 | tf_op jit(solution)/shard_map/mixer_forward/pallas_call | solution.py:246
  94.0 2.7 all-to-all-done
  96.7 11.2 %home_forward.1 = (f32[512,1536]{1,0:T(8,128)}, bf16[512,1536]{1,0:T(8,128)(2,1)}, f32[512,768]{1,0:T(8,128)}, f32[512,1]{1,0:T(8,128)}, bf16[640,768]{1,0:T(8,128)(2,1)}) custom-call(s32[2]{0:T(128)} %copy-done.14, bf16[512,768]{1,0:T(8,128)(2,1)} %get-tuple-element.115.u_ref, f32[512,1536]{1,0:T(8,128)} %get-tuple-element.118.mix_ref, ...), custom_call_target="tpu_custom_call" | custom-call | tf_op jit(solution)/shard_map/home_forward/pallas_call | solution.py:678
  107.9 5.0 %all-to-all-start.1 = ((bf16[16,40,768]{2,1,0:T(8,128)(2,1)}), bf16[16,40,768]{2,1,0:T(8,128)(2,1)S(1)}, u32[]{:S(2)}, u32[]{:S(2)}) async-start(bf16[16,40,768]{2,1,0:T(8,128)(2,1)} %bitcast.100), calls=%async_computation.1 | async-start | bytes 1966080 | tf_op jit(solution)/shard_map/all_to_all | solution.py:1042
  113.4 23.2 %all-to-all-done.1 = bf16[16,40,768]{2,1,0:T(8,128)(2,1)S(1)} async-done(((bf16[16,40,768]{2,1,0:T(8,128)(2,1)}), bf16[16,40,768]{2,1,0:T(8,128)(2,1)S(1)}, u32[]{:S(2)}, u32[]{:S(2)}) %all-to-all-start.1) | async-done | bytes 983072 | tf_op jit(solution)/shard_map/all_to_all | solution.py:1042
  137.5 21.0 %expert_pass.1 = (bf16[640,768]{1,0:T(8,128)(2,1)}, bf16[640,768]{1,0:T(8,128)(2,1)}, bf16[640,768]{1,0:T(8,128)(2,1)}, f32[16,768]{1,0:T(8,128)}, bf16[640,1536...) custom-call(bf16[640,768]{1,0:T(8,128)(2,1)} %bitcast.78, ...), custom_call_target="tpu_custom_call" | custom-call | bytes 70000000 | tf_op jit(solution)/shard_map/expert_pass/pallas_call | solution.py:573
  158.6 4.8 %all-to-all-start.2 = ((bf16[16,40,768]{2,1,0:T(8,128)(2,1)}), bf16[16,40,768]{2,1,0:T(8,128)(2,1)S(1)}, u32[]{:S(2)}, u32[]{:S(2)}) async-start(bf16[16,40,768]{2,1,0:T(8,128)(2,1)} %bitcast.99), calls=%async_computation.2 | async-start | bytes 1966080 | tf_op jit(solution)/shard_map/all_to_all | solution.py:1048
  166.4 12.0 %expert_grads.1 = (bf16[768,1536]{1,0:T(8,128)(2,1)}, bf16[1536,768]{1,0:T(8,128)(2,1)}, bf16[768,1536]{1,0:T(8,128)(2,1)}, bf16[1536,768]{1,0:T(8,128)(2,1)}) custom-call(bf16[640,768]{1,0:T(8,128)(2,1)} %bitcast.79, bf16[640,768]{1,0:T(8,128)(2,1)} %get-tuple-element.133.gr_ref, bf16[640,1536]{1,0:T(8,128)(2,1)} %get-tuple-element.134.refs_0_, ...), custom_call_target="tpu_custom_call" | custom-call | bytes 100000 | tf_op jit(solution)/shard_map/expert_grads/pallas_call | solution.py:820
  178.4 7.6 %all-to-all-done.2 = bf16[16,40,768]{2,1,0:T(8,128)(2,1)S(1)} async-done(((bf16[16,40,768]{2,1,0:T(8,128)(2,1)}), bf16[16,40,768]{2,1,0:T(8,128)(2,1)S(1)}, u32[]{:S(2)}, u32[]{:S(2)}) %all-to-all-start.2) | async-done | bytes 983072 | tf_op jit(solution)/shard_map/all_to_all | solution.py:1048
  186.6 4.9 %all-to-all-start.3 = ((bf16[16,40,768]{2,1,0:T(8,128)(2,1)}), bf16[16,40,768]{2,1,0:T(8,128)(2,1)S(1)}, u32[]{:S(2)}, u32[]{:S(2)}) async-start(bf16[16,40,768]{2,1,0:T(8,128)(2,1)} %bitcast.38), calls=%async_computation.3 | async-start | bytes 1966080 | tf_op jit(solution)/shard_map/all_to_all | solution.py:1048
  191.8 17.4 %home_backward.1 = (f32[512,768]{1,0:T(8,128)}, f32[512,1536]{1,0:T(8,128)}, f32[512,768]{1,0:T(8,128)}, f32[768,128]{1,0:T(8,128)}, bf16[1536,1536]{1,0:T(8,128)(2,1)}) custom-call(s32[2]{0:T(128)} %copy-done.14, bf16[640,512]{1,0:T(8,128)(2,1)} %fusion.2.choose_ref, bf16[640,768]{1,0:T(8,128)(2,1)} %bitcast.86, f32[512,768]{1,0:T(8,128)} %get-tuple-element.121.h1_ref, ...), custom_call_target="tpu_custom_call" | custom-call | bytes 100000 | tf_op jit(solution)/shard_map/home_backward/pallas_call | solution.py:776
  210.5 66.7 %mixer_backward.1 = (bf16[512,1536]{1,0:T(8,128)(2,1)}, bf16[512,1536]{1,0:T(8,128)(2,1)}, f32[512,768]{1,0:T(8,128)}) custom-call(s32[3]{0:T(128)} %pad_add_fusion.len_ref, f32[512,1536]{1,0:T(8,128)} %get-tuple-element.123.delta_ref, f32[512,1536]{1,0:T(8,128)} %get-tuple-element.124.xs_ref, f32[528,1536]{1,0:T(8,128)} %get-tuple-element.125.bx_ref, ...), custom_call_target="tpu_custom_call" | custom-call | bytes 100000 | tf_op jit(solution)/shard_map/mixer_backward/pallas_call | solution.py:493
  277.3 3.6 %collective-permute-done.20 = bf16[16,32,1536]{2,1,0:T(8,128)(2,1)S(1)} collective-permute-done((bf16[16,32,1536]{2,1,0:T(8,128)(2,1)}, bf16[16,32,1536]{2,1,0:T(8,128)(2,1)S(1)}, u32[]{:S(2)}, u32[]{:S(2)}) %collective-permute-start.20) | collective-permute-done | bytes 1572896 | tf_op jit(solution)/shard_map/ppermute | solution.py:878
  280.9 3.0 add_convert_fusion
  284.0 5.2 %all-to-all-start.4 = ((bf16[16,32,1536]{2,1,0:T(8,128)(2,1)}), bf16[16,32,1536]{2,1,0:T(8,128)(2,1)S(1)}, u32[]{:S(2)}, u32[]{:S(2)}) async-start(bf16[16,32,1536]{2,1,0:T(8,128)(2,1)} %add_convert_fusion), calls=%async_computation.4 | async-start | bytes 3145728 | tf_op jit(solution)/shard_map/all_to_all | solution.py:1129
  289.4 3.1 add_convert_fusion.1
  292.5 4.7 %add_bitcast_fusion.1 = f32[1,768,1536]{2,1,0:T(8,128)} fusion(bf16[768,1536]{1,0:T(8,128)(2,1)} %collective-permute-done.18, bf16[768,1536]{1,0:T(8,128)(2,1)S(1)} %copy-done.6), kind=kLoop, calls=%fused_computation.1 | loop fusion | flops 3538944 | bytes 9437184 | tf_op jit(solution)/shard_map/broadcast_in_dim | solution.py:1170
  297.2 4.4 %add_bitcast_fusion = f32[1,1536,768]{2,1,0:T(8,128)} fusion(bf16[1536,768]{1,0:T(8,128)(2,1)} %collective-permute-done.19, bf16[1536,768]{1,0:T(8,128)(2,1)S(1)} %copy-done.5), kind=kLoop, calls=%fused_computation | loop fusion | flops 3538944 | bytes 9437184 | tf_op jit(solution)/shard_map/broadcast_in_dim | solution.py:1171
  301.6 28.2 %reduce-scatter.2.cloned.1.call-done.late_ref = bf16[48,1536]{1,0:T(8,128)(2,1)} async-done(((bf16[1536,1536]{1,0:T(8,128)(2,1)}), bf16[48,1536]{1,0:T(8,128)(2,1)}) %reduce-scatter.2.cloned.1.call-update) | async-done | bytes 147472 | tf_op jit(solution)/shard_map/reduce_scatter | solution.py:1106
  329.8 2.1 all-to-all-done.4.parts_ref
  333.1 2.5 finish.1
  (141 shorter events, 34.8 us)
Async XLA Ops:
  7.2 14.2 %copy-start.16 = (bf16[48,16]{0,1:T(8,128)(2,1)S(1)}, bf16[48,16]{0,1:T(8,128)(2,1)}, u32[]{:S(2)}) copy-start(bf16[48,16]{0,1:T(8,128)(2,1)} %param.29) | copy-start | bytes 4612
  7.2 14.3 %copy-start.13 = (bf16[48,48]{1,0:T(8,128)(2,1)S(1)}, bf16[48,48]{1,0:T(8,128)(2,1)}, u32[]{:S(2)}) copy-start(bf16[48,48]{1,0:T(8,128)(2,1)} %param.27) | copy-start | bytes 13828
  7.2 14.3 %copy-start.12 = (bf16[48,80]{1,0:T(8,128)(2,1)S(1)}, bf16[48,80]{1,0:T(8,128)(2,1)}, u32[]{:S(2)}) copy-start(bf16[48,80]{1,0:T(8,128)(2,1)} %param.26) | copy-start | bytes 23044
  7.3 89.4 %all-gather.3.cloned.1.call-start = ((), (), s32[]{:S(2)}) async-start(), calls=%async_computation.7 | async-start | bytes 4866048 | tf_op jit(solution)/shard_map/all_gather | solution.py:1017
  8.2 13.5 %collective-permute-start.1 = (bf16[24,1536]{1,0:T(8,128)(2,1)S(1)}, bf16[24,1536]{1,0:T(8,128)(2,1)S(1)}, u32[]{:S(2)}, u32[]{:S(2)}) collective-permute-start(bf16[24,1536]{1,0:T(8,128)(2,1)S(1)} %get-tuple-element.215), channel_id=1, source_target_pairs={{0,8},{1,9},{2,10},{3,11},{4,12},{5,13},{6,14},{7,15},{8,0},{9,1},... | collective-permute-start | bytes 221192 | tf_op jit(solution)/shard_map/ppermute | solution.py:878
  10.9 10.8 %collective-permute-start = (bf16[24,1536]{1,0:T(8,128)(2,1)S(1)}, bf16[24,1536]{1,0:T(8,128)(2,1)S(1)}, u32[]{:S(2)}, u32[]{:S(2)}) collective-permute-start(bf16[24,1536]{1,0:T(8,128)(2,1)S(1)} %get-tuple-element.215), channel_id=1, source_target_pairs={{0,4},{1,5},{2,6},{3,7},{4,0},{5,1},{6,2},{7,3},{8,12},{9,13},{10,... | collective-permute-start | bytes 221192 | tf_op jit(solution)/shard_map/ppermute | solution.py:878
  11.3 10.4 %collective-permute-start.2 = (bf16[24,1536]{1,0:T(8,128)(2,1)S(1)}, bf16[24,1536]{1,0:T(8,128)(2,1)S(1)}, u32[]{:S(2)}, u32[]{:S(2)}) collective-permute-start(bf16[24,1536]{1,0:T(8,128)(2,1)S(1)} %get-tuple-element.215), channel_id=1, source_target_pairs={{0,12},{1,13},{2,14},{3,15},{4,8},{5,9},{6,10},{7,11},{8,4},{9,5},... | collective-permute-start | bytes 221192 | tf_op jit(solution)/shard_map/ppermute | solution.py:878
  21.9 8.1 %collective-permute-start.7 = (bf16[48,256]{1,0:T(8,128)(2,1)S(1)}, bf16[48,256]{1,0:T(8,128)(2,1)S(1)}, u32[]{:S(2)}, u32[]{:S(2)}) collective-permute-start(bf16[48,256]{1,0:T(8,128)(2,1)S(1)} %concatenate.54), channel_id=1, source_target_pairs={{0,12},{1,13},{2,14},{3,15},{4,8},{5,9},{6,10},{7,11},{8,4},{9,5},... | collective-permute-start | bytes 73736 | tf_op jit(solution)/shard_map/ppermute | solution.py:878
  23.5 6.5 %collective-permute-start.6 = (bf16[48,256]{1,0:T(8,128)(2,1)S(1)}, bf16[48,256]{1,0:T(8,128)(2,1)S(1)}, u32[]{:S(2)}, u32[]{:S(2)}) collective-permute-start(bf16[48,256]{1,0:T(8,128)(2,1)S(1)} %concatenate.54), channel_id=1, source_target_pairs={{0,8},{1,9},{2,10},{3,11},{4,12},{5,13},{6,14},{7,15},{8,0},{9,1},... | collective-permute-start | bytes 73736 | tf_op jit(solution)/shard_map/ppermute | solution.py:878
  25.5 4.5 %collective-permute-start.5 = (bf16[48,256]{1,0:T(8,128)(2,1)S(1)}, bf16[48,256]{1,0:T(8,128)(2,1)S(1)}, u32[]{:S(2)}, u32[]{:S(2)}) collective-permute-start(bf16[48,256]{1,0:T(8,128)(2,1)S(1)} %concatenate.54), channel_id=1, source_target_pairs={{0,4},{1,5},{2,6},{3,7},{4,0},{5,1},{6,2},{7,3},{8,12},{9,13},{10,... | collective-permute-start | bytes 73736 | tf_op jit(solution)/shard_map/ppermute | solution.py:878
  26.9 5.2 %collective-permute-start.4 = (bf16[2,2,1,1,24,768]{5,4,1,0,3,2:T(8,128)(2,1)S(1)}, bf16[2,2,1,1,24,768]{5,4,1,0,3,2:T(8,128)(2,1)S(1)}, u32[]{:S(2)}, u32[]{:S(2)}) collective-permute-start(bf16[2,2,1,1,24,768]{5,4,1,0,3,2:T(8,128)(2,1)S(1)} %get-tuple-element.202), channel_id=1, source_target_pairs={{0,1},{1,0},{2,3},{3,2},{4,5},{5,4},{6,7},{7,6},{8,9},{9,8},{10,11... | collective-permute-start | bytes 442376 | tf_op jit(solution)/shard_map/ppermute | solution.py:878
  28.5 5.1 %collective-permute-start.3 = (bf16[2,2,1,1,24,768]{5,4,1,0,3,2:T(8,128)(2,1)S(1)}, bf16[2,2,1,1,24,768]{5,4,1,0,3,2:T(8,128)(2,1)S(1)}, u32[]{:S(2)}, u32[]{:S(2)}) collective-permute-start(bf16[2,2,1,1,24,768]{5,4,1,0,3,2:T(8,128)(2,1)S(1)} %get-tuple-element.203), channel_id=1, source_target_pairs={{0,2},{1,3},{2,0},{3,1},{4,6},{5,7},{6,4},{7,5},{8,10},{9,11},{10,... | collective-permute-start | bytes 442376 | tf_op jit(solution)/shard_map/ppermute | solution.py:878
  33.8 4.7 %collective-permute-start.11 = (bf16[2,2,1,1,48,128]{5,4,1,0,3,2:T(8,128)(2,1)S(1)}, bf16[2,2,1,1,48,128]{5,4,1,0,3,2:T(8,128)(2,1)S(1)}, u32[]{:S(2)}, u32[]{:S(2)}) collective-permute-start(bf16[2,2,1,1,48,128]{5,4,1,0,3,2:T(8,128)(2,1)S(1)} %get-tuple-element.218), channel_id=1, source_target_pairs={{0,1},{1,0},{2,3},{3,2},{4,5},{5,4},{6,7},{7,6},{8,9},{9,8},{10,11... | collective-permute-start | bytes 147464 | tf_op jit(solution)/shard_map/ppermute | solution.py:878
  34.4 4.7 %collective-permute-start.10 = (bf16[2,2,1,1,48,128]{5,4,1,0,3,2:T(8,128)(2,1)S(1)}, bf16[2,2,1,1,48,128]{5,4,1,0,3,2:T(8,128)(2,1)S(1)}, u32[]{:S(2)}, u32[]{:S(2)}) collective-permute-start(bf16[2,2,1,1,48,128]{5,4,1,0,3,2:T(8,128)(2,1)S(1)} %get-tuple-element.219), channel_id=1, source_target_pairs={{0,2},{1,3},{2,0},{3,1},{4,6},{5,7},{6,4},{7,5},{8,10},{9,11},{10,... | collective-permute-start | bytes 147464 | tf_op jit(solution)/shard_map/ppermute | solution.py:878
  35.9 6.7 %collective-permute-start.8 = (bf16[2,2,2,1,24,768]{5,4,1,0,3,2:T(8,128)(2,1)S(1)}, bf16[2,2,2,1,24,768]{5,4,1,0,3,2:T(8,128)(2,1)S(1)}, u32[]{:S(2)}, u32[]{:S(2)}) collective-permute-start(bf16[2,2,2,1,24,768]{5,4,1,0,3,2:T(8,128)(2,1)S(1)} %pad_maximum_fusion.3), channel_id=1, source_target_pairs={{0,1},{1,0},{2,3},{3,2},{4,5},{5,4},{6,7},{7,6},{8,9},{9,8},{10,11... | collective-permute-start | bytes 884744 | tf_op jit(solution)/shard_map/ppermute | solution.py:878
  37.4 6.8 %collective-permute-start.9 = (bf16[2,2,1,2,24,768]{5,4,1,0,3,2:T(8,128)(2,1)S(1)}, bf16[2,2,1,2,24,768]{5,4,1,0,3,2:T(8,128)(2,1)S(1)}, u32[]{:S(2)}, u32[]{:S(2)}) collective-permute-start(bf16[2,2,1,2,24,768]{5,4,1,0,3,2:T(8,128)(2,1)S(1)} %pad_maximum_fusion.4), channel_id=1, source_target_pairs={{0,2},{1,3},{2,0},{3,1},{4,6},{5,7},{6,4},{7,5},{8,10},{9,11},{10,... | collective-permute-start | bytes 884744 | tf_op jit(solution)/shard_map/ppermute | solution.py:878
  44.4 6.8 %collective-permute-start.12 = (bf16[1,384,1536]{2,1,0:T(8,128)(2,1)S(1)}, bf16[1,384,1536]{2,1,0:T(8,128)(2,1)S(1)}, u32[]{:S(2)}, u32[]{:S(2)}) collective-permute-start(bf16[1,384,1536]{2,1,0:T(8,128)(2,1)S(1)} %bitcast.83), channel_id=1, source_target_pairs={{0,16},{16,0},{1,17},{17,1},{2,18},{18,2},{3,19},{19,3},{4,20},{20... | collective-permute-start | bytes 3538952 | tf_op jit(solution)/shard_map/ppermute | solution.py:878
  44.5 5.9 %collective-permute-start.13 = (bf16[2,2,2,1,48,128]{5,4,1,0,3,2:T(8,128)(2,1)S(1)}, bf16[2,2,2,1,48,128]{5,4,1,0,3,2:T(8,128)(2,1)S(1)}, u32[]{:S(2)}, u32[]{:S(2)}) collective-permute-start(bf16[2,2,2,1,48,128]{5,4,1,0,3,2:T(8,128)(2,1)S(1)} %pad_maximum_fusion.7), channel_id=1, source_target_pairs={{0,1},{1,0},{2,3},{3,2},{4,5},{5,4},{6,7},{7,6},{8,9},{9,8},{10,11... | collective-permute-start | bytes 294920 | tf_op jit(solution)/shard_map/ppermute | solution.py:878
  45.0 5.3 %collective-permute-start.14 = (bf16[2,2,1,2,48,128]{5,4,1,0,3,2:T(8,128)(2,1)S(1)}, bf16[2,2,1,2,48,128]{5,4,1,0,3,2:T(8,128)(2,1)S(1)}, u32[]{:S(2)}, u32[]{:S(2)}) collective-permute-start(bf16[2,2,1,2,48,128]{5,4,1,0,3,2:T(8,128)(2,1)S(1)} %pad_maximum_fusion.8), channel_id=1, source_target_pairs={{0,2},{1,3},{2,0},{3,1},{4,6},{5,7},{6,4},{7,5},{8,10},{9,11},{10,... | collective-permute-start | bytes 294920 | tf_op jit(solution)/shard_map/ppermute | solution.py:878
  53.0 43.7 %all-to-all-start = ((bf16[16,40,768]{2,1,0:T(8,128)(2,1)}), bf16[16,40,768]{2,1,0:T(8,128)(2,1)S(1)}, u32[]{:S(2)}, u32[]{:S(2)}) async-start(bf16[16,40,768]{2,1,0:T(8,128)(2,1)} %bitcast.97), calls=%async_computation | async-start | bytes 1966080 | tf_op jit(solution)/shard_map/all_to_all | solution.py:1042
  60.4 53.0 %collective-permute-start.16 = (bf16[768,1536]{1,0:T(8,128)(2,1)S(1)}, bf16[768,1536]{1,0:T(8,128)(2,1)}, u32[]{:S(2)}, u32[]{:S(2)}) collective-permute-start(bf16[768,1536]{1,0:T(8,128)(2,1)S(1)} %bitcast.89), channel_id=1, source_target_pairs={{0,16},{16,0},{1,17},{17,1},{2,18},{18,2},{3,19},{19,3},{4,20},{20... | collective-permute-start | bytes 7077896 | tf_op jit(solution)/shard_map/ppermute | solution.py:878
  60.5 52.9 %collective-permute-start.17 = (bf16[1536,768]{1,0:T(8,128)(2,1)}, bf16[1536,768]{1,0:T(8,128)(2,1)}, u32[]{:S(2)}, u32[]{:S(2)}) collective-permute-start(bf16[1536,768]{1,0:T(8,128)(2,1)} %bitcast.90), channel_id=1, source_target_pairs={{0,16},{16,0},{1,17},{17,1},{2,18},{18,2},{3,19},{19,3},{4,20},{20... | collective-permute-start | bytes 7077896 | tf_op jit(solution)/shard_map/ppermute | solution.py:878
  62.0 3.0 collective-permute-start.15
  107.9 28.7 %all-to-all-start.1 = ((bf16[16,40,768]{2,1,0:T(8,128)(2,1)}), bf16[16,40,768]{2,1,0:T(8,128)(2,1)S(1)}, u32[]{:S(2)}, u32[]{:S(2)}) async-start(bf16[16,40,768]{2,1,0:T(8,128)(2,1)} %bitcast.100), calls=%async_computation.1 | async-start | bytes 1966080 | tf_op jit(solution)/shard_map/all_to_all | solution.py:1042
  137.5 25.9 %copy-start.10 = (f32[2,768]{1,0:T(2,128)S(1)}, f32[2,768]{1,0:T(2,128)}, u32[]{:S(2)}) copy-start(f32[2,768]{1,0:T(2,128)} %get-tuple-element.119.gain_ref) | copy-start | bytes 18436
  158.6 27.5 %all-to-all-start.2 = ((bf16[16,40,768]{2,1,0:T(8,128)(2,1)}), bf16[16,40,768]{2,1,0:T(8,128)(2,1)S(1)}, u32[]{:S(2)}, u32[]{:S(2)}) async-start(bf16[16,40,768]{2,1,0:T(8,128)(2,1)} %bitcast.99), calls=%async_computation.2 | async-start | bytes 1966080 | tf_op jit(solution)/shard_map/all_to_all | solution.py:1048
  186.1 24.4 %collective-permute-start.18 = (bf16[768,1536]{1,0:T(8,128)(2,1)}, bf16[768,1536]{1,0:T(8,128)(2,1)}, u32[]{:S(2)}, u32[]{:S(2)}) collective-permute-start(bf16[768,1536]{1,0:T(8,128)(2,1)} %get-tuple-element.148), channel_id=1, source_target_pairs={{0,16},{16,0},{1,17},{17,1},{2,18},{18,2},{3,19},{19,3},{4,20},{20... | collective-permute-start | bytes 7077896 | tf_op jit(solution)/shard_map/ppermute | solution.py:878
  186.1 24.4 %collective-permute-start.19 = (bf16[1536,768]{1,0:T(8,128)(2,1)}, bf16[1536,768]{1,0:T(8,128)(2,1)}, u32[]{:S(2)}, u32[]{:S(2)}) collective-permute-start(bf16[1536,768]{1,0:T(8,128)(2,1)} %get-tuple-element.149), channel_id=1, source_target_pairs={{0,16},{16,0},{1,17},{17,1},{2,18},{18,2},{3,19},{19,3},{4,20},{20... | collective-permute-start | bytes 7077896 | tf_op jit(solution)/shard_map/ppermute | solution.py:878
  186.6 90.6 %all-to-all-start.3 = ((bf16[16,40,768]{2,1,0:T(8,128)(2,1)}), bf16[16,40,768]{2,1,0:T(8,128)(2,1)S(1)}, u32[]{:S(2)}, u32[]{:S(2)}) async-start(bf16[16,40,768]{2,1,0:T(8,128)(2,1)} %bitcast.38), calls=%async_computation.3 | async-start | bytes 1966080 | tf_op jit(solution)/shard_map/all_to_all | solution.py:1048
  191.5 138.3 %reduce-scatter.2.cloned.1.call-start = ((), (), s32[]{:S(2)}) async-start(), calls=%async_computation.6 | async-start | bytes 4866048 | tf_op jit(solution)/shard_map/reduce_scatter | solution.py:1106
  277.2 3.7 %collective-permute-start.20 = (bf16[16,32,1536]{2,1,0:T(8,128)(2,1)}, bf16[16,32,1536]{2,1,0:T(8,128)(2,1)S(1)}, u32[]{:S(2)}, u32[]{:S(2)}) collective-permute-start(bf16[16,32,1536]{2,1,0:T(8,128)(2,1)} %bitcast.123), channel_id=1, source_target_pairs={{0,16},{16,0},{1,17},{17,1},{2,18},{18,2},{3,19},{19,3},{4,20},{20... | collective-permute-start | bytes 4718600 | tf_op jit(solution)/shard_map/ppermute | solution.py:878
  284.0 47.9 %all-to-all-start.4 = ((bf16[16,32,1536]{2,1,0:T(8,128)(2,1)}), bf16[16,32,1536]{2,1,0:T(8,128)(2,1)S(1)}, u32[]{:S(2)}, u32[]{:S(2)}) async-start(bf16[16,32,1536]{2,1,0:T(8,128)(2,1)} %add_convert_fusion), calls=%async_computation.4 | async-start | bytes 3145728 | tf_op jit(solution)/shard_map/all_to_all | solution.py:1129
  (17 other events, 124.2 us)
Sparse Core Ops, SparseCore 0:
  14.2 77.7 all-gather.2
  209.4 120.3 reduce-scatter.1
